TPU v7x, 32 devices: a whole 2x2x4 slice. The times are simulated.
32 devices in a mesh: ctx: 8 (over z, x), head: 4 (over y, core).
Axes of the slice: x: 2, y: 2, z: 4, core: 2. Of those that a mesh axis runs over, the one named last changes fastest.
Arguments:
- queries: bfloat16 [2048, 4096], P(('ctx', 'head')), may hold values from -200 to 200
- keys: bfloat16 [2048, 512], P(('ctx', 'head')), may hold values from -6 to 6
- values: bfloat16 [2048, 512], P(('ctx', 'head')), may hold values from -6 to 6
Outputs:
- attended: bfloat16 [2048, 4096], P(('ctx', 'head'))
All inputs are finite; a program needn't handle non-finite values.
Results may differ from a plain program's by a relative error of at most 0.0065.
Values may be sent and summed in bfloat16 or wider, within the bound.
No kernel may reach another device: no remote copies, remote signals or barrier semaphores. Data moves between devices by JAX's collectives and lax.ppermute only.
A program may use at most 64 MiB of HBM per device.

v0:
```python
import math

import jax
import jax.numpy as jnp
from jax import lax
from jax.sharding import PartitionSpec as P

QH = 32
KVH = 4
HD = 128


def attend_block(state, query_block, key_rows, value_rows, query_first, key_first):
    maxima, totals, summed = state
    scale = 1.0 / math.sqrt(HD)
    scores = (
        jnp.einsum("tsgd,ksd->sgtk", query_block, key_rows, preferred_element_type=jnp.float32)
        * scale
    )
    query_pos = query_first + jnp.arange(query_block.shape[0], dtype=jnp.int32)
    key_pos = key_first + jnp.arange(key_rows.shape[0], dtype=jnp.int32)
    allowed = query_pos[:, None] >= key_pos[None, :]
    scores = jnp.where(allowed, scores, -1e30)
    new_max = jnp.maximum(maxima, jnp.max(scores, axis=-1))
    factor = jnp.exp(maxima - new_max)
    weights = jnp.exp(scores - new_max[..., None])
    totals = totals * factor + jnp.sum(weights, axis=-1)
    product = jnp.einsum(
        "sgtk,ksd->sgtd",
        weights.astype(jnp.bfloat16),
        value_rows,
        preferred_element_type=jnp.float32,
    )
    summed = summed * factor[..., None] + product
    return (new_max, totals, summed)


def make_work(query_block, query_first, taken, key_first):

    def work(current):
        return attend_block(current, query_block, taken[0], taken[1], query_first, key_first)

    return work


def keep_state(current):
    return current


def make_folder(query_parts, step_size):

    def folder(states, piece, start):
        step_len = min(step_size, piece.shape[1])
        count = piece.shape[1] // step_len

        def one_step(index, inner):
            key_first = index * step_len
            taken = lax.dynamic_slice_in_dim(piece, index * step_len, step_len, 1)
            updated = []
            for (query_block, query_first), current in zip(query_parts, inner):
                last_row = query_first + query_block.shape[0] - 1
                work = make_work(query_block, query_first, taken, key_first)
                updated.append(lax.cond(key_first <= last_row, work, keep_state, current))
            return tuple(updated)

        return lax.fori_loop(0, count, one_step, states)

    return folder


def empty_state(slots, group, rows):
    return (
        jnp.full((slots, group, rows), -1e30, jnp.float32),
        jnp.zeros((slots, group, rows), jnp.float32),
        jnp.zeros((slots, group, rows, HD), jnp.float32),
    )


def finish(state, head_local):
    maxima, totals, summed = state
    result = summed / totals[..., None]
    rows = result.shape[2]
    return result.transpose(2, 0, 1, 3).reshape(rows, head_local, HD).astype(jnp.bfloat16)


def shards(queries, keys, values):
    head_count = lax.axis_size("head")
    tok_rows = queries.shape[0]
    repeat = max(1, head_count // KVH)
    query_local = queries.reshape(tok_rows, QH, HD)
    paired = jnp.stack([keys.reshape(tok_rows, KVH, HD), values.reshape(tok_rows, KVH, HD)], 0)
    query_span = lax.all_to_all(query_local, "head", split_axis=1, concat_axis=0, tiled=True)
    span_len = query_span.shape[0]
    head_local = query_span.shape[1]
    slots = KVH * repeat // head_count
    group = head_local // slots
    query_block = query_span.reshape(span_len, slots, group, HD)
    ctx_index = lax.axis_index("ctx")
    query_first = ctx_index * span_len
    spread = jnp.repeat(paired, repeat, axis=2)
    paired_span = lax.all_to_all(spread, "head", split_axis=2, concat_axis=1, tiled=True)
    query_parts = [(query_block, query_first)]
    start_states = (empty_state(slots, group, span_len),)
    folder = make_folder(query_parts, span_len)
    states = folder(
        start_states, lax.all_gather(paired_span, "ctx", axis=1, tiled=True), jnp.int32(0)
    )
    result = finish(states[0], head_local)
    returned = lax.all_to_all(result, "head", split_axis=0, concat_axis=1, tiled=True)
    return returned.reshape(tok_rows, QH * HD)


def solution(mesh):
    return jax.shard_map(
        shards,
        mesh=mesh,
        in_specs=(P(("ctx", "head"), None), P(("ctx", "head"), None), P(("ctx", "head"), None)),
        out_specs=P(("ctx", "head"), None),
        check_vma=False,
    )
```

profile of v0, /device:TPU:26, one launch (start us, length us, event | category | flops | bytes accessed | tf_op | source)
XLA Modules:
  0.0 104.4 jit_solution(4848093940330254821)
XLA Ops:
  6.5 0.0 copy-start
  6.5 0.0 all-gather.2.cloned.1.call-start
  6.5 0.9 stack_reshape.6
  7.5 0.9 stack_reshape.7
  8.3 0.1 pad_maximum_fusion
  8.4 7.2 %all_to_all.48 = bf16[2,64,4,128]{3,1,0,2:T(8,128)(2,1)S(1)} all-to-all(bf16[2,64,4,128]{3,1,0,2:T(8,128)(2,1)S(1)} %copy.26), channel_id=1, replica_groups=mesh['ctx'=8,'head'=4] {'head'}, dimensions={2} | all-to-all | bytes 262144 | tf_op jit(solution)/shard_map/all_to_all | solution.py:101
  15.7 0.7 copy.27
  16.3 0.0 all-gather.2.cloned.1.call-update
  16.4 0.0 copy-done
  16.4 0.9 copy_bitcast_fusion.1
  17.3 3.5 %all-to-all-start.1 = ((bf16[64,32,128]{2,0,1:T(8,128)(2,1)}), bf16[64,32,128]{2,0,1:T(8,128)(2,1)S(1)}, u32[]{:S(2)}, u32[]{:S(2)}) async-start(bf16[64,32,128]{2,0,1:T(8,128)(2,1)} %copy_bitcast_fusion.1), calls=%async_computation.1 | async-start | bytes 1048576 | tf_op jit(solution)/shard_map/all_to_all | solution.py:92
  20.8 8.8 %all-to-all-done.1 = bf16[64,32,128]{2,0,1:T(8,128)(2,1)S(1)} async-done(((bf16[64,32,128]{2,0,1:T(8,128)(2,1)}), bf16[64,32,128]{2,0,1:T(8,128)(2,1)S(1)}, u32[]{:S(2)}, u32[]{:S(2)}) %all-to-all-start.1) | async-done | bytes 524320 | tf_op jit(solution)/shard_map/all_to_all | solution.py:92
  29.6 0.3 copy.30
  29.9 0.1 copy.32
  30.0 24.5 %all-gather.2.cloned.1.call-done = bf16[2,2048,1,128]{3,1,0,2:T(8,128)(2,1)} async-done(((bf16[2,256,1,128]{3,1,0,2:T(8,128)(2,1)}), bf16[2,2048,1,128]{3,1,0,2:T(8,128)(2,1)}) %all-gather.2.cloned.1.call-update) | async-done | bytes 1048592 | tf_op jit(solution)/shard_map/all_gather | solution.py:106
  54.5 0.1 broadcast_in_dim.28
  54.6 29.6 %while.19 = (s32[]{:T(128)}, f32[1,8,256]{2,1,0:T(8,128)S(1)}, f32[1,8,256]{2,1,0:T(8,128)S(1)}, f32[1,8,256,128]{3,2,1,0:T(8,128)S(1)}, s32[]{:T(128)}, /*index...) while((s32[]{:T(128)}, f32[1,8,256]{2,1,0:T(8,128)S(1)}, ...), condition=%wide.region_5.6_spmd, body=%wide.region_0.5_spmd.sunk | while | flops 272701952 | bytes 9310513 | solution.py:66
  54.6 3.7 %conditional.2 = ((f32[1,8,256]{2,1,0:T(8,128)S(1)}, f32[1,8,256]{2,1,0:T(8,128)S(1)}, f32[1,8,256,128]{3,2,1,0:T(8,128)S(1)})) conditional(s32[]{:T(128)} %convert_element_type.34, (f32[1,8,256]{2,1,0:T(8,128)S(1)}, f32[1,8,256]{2,1,0:T(8,128)S(1)}, f32[1,8,256,128]{3,2,1,0:T(8,128)S(1)}) %tuple.57, (s32[]{:T(128)}, s32[]{:T(128)}, ...), branch_computations={%region_1.0_spmd, %region_2.4_spmd} | conditional | flops 272701952 | bytes 9310306 | solution.py:63
  54.7 0.1 broadcast_compare_fusion
  54.8 1.3 %fusion.12 = (f32[8,256]{1,0:T(8,128)S(1)}, f32[1,8,256,256]{2,3,1,0:T(8,128)S(1)}) fusion(bf16[256,1,8,128]{3,0,2,1:T(8,128)(2,1)S(1)} %get-tuple-element.257, bf16[2,2048,1,128]{3,1,2,0:T(8,128)(2,1)} %get-tuple-element.256, s32[]{:T(128)S(6)} %select_n.15, pred[256,256]{0,1:T(8,128)(4,1)S(1)} %broadcast_compare_fusion), kind=kOutput, calls=%fused_computation.26 | convolution fusion | flops 135788544 | bytes 2760708 | tf_op jit(solution)/shard_map/while/body/eval_jaxpr/cond/branch_1_fun/tsgd,ksd->sgtk/dot_general | solution.py:17
  56.1 1.9 %fusion.2 = f32[1,8,256,128]{3,2,1,0:T(8,128)S(1)} fusion(f32[1,8,256,256]{2,3,1,0:T(8,128)S(1)} %get-tuple-element.319, f32[1,8,256,128]{3,2,1,0:T(8,128)S(1)} %get-tuple-element.259, f32[8,256]{1,0:T(8,128)S(1)} %bitcast.64, f32[8,256]{1,0:T(8,128)S(1)} %get-tuple-element.316, bf16[2,2048,1,128]{3,1,2,0:T(8,128)(2,1)} %get-tuple-element.256, s32[]{:T(128)S(6)} %add.78, ...), kind=kOutput, calls=%fused_computation.5 | convolution fusion | flops 135790592 | bytes 4276232 | tf_op jit(solution)/shard_map/while/body/eval_jaxpr/cond/branch_1_fun/sgtk,ksd->sgtd/dot_general | solution.py:28
  58.0 0.3 fusion.1
  58.3 3.7 %conditional.2 = ((f32[1,8,256]{2,1,0:T(8,128)S(1)}, f32[1,8,256]{2,1,0:T(8,128)S(1)}, f32[1,8,256,128]{3,2,1,0:T(8,128)S(1)})) conditional(s32[]{:T(128)} %convert_element_type.34, (f32[1,8,256]{2,1,0:T(8,128)S(1)}, f32[1,8,256]{2,1,0:T(8,128)S(1)}, f32[1,8,256,128]{3,2,1,0:T(8,128)S(1)}) %tuple.57, (s32[]{:T(128)}, s32[]{:T(128)}, ...), branch_computations={%region_1.0_spmd, %region_2.4_spmd} | conditional | flops 272701952 | bytes 9310306 | solution.py:63
  58.4 0.1 broadcast_compare_fusion
  58.5 1.3 %fusion.12 = (f32[8,256]{1,0:T(8,128)S(1)}, f32[1,8,256,256]{2,3,1,0:T(8,128)S(1)}) fusion(bf16[256,1,8,128]{3,0,2,1:T(8,128)(2,1)S(1)} %get-tuple-element.257, bf16[2,2048,1,128]{3,1,2,0:T(8,128)(2,1)} %get-tuple-element.256, s32[]{:T(128)S(6)} %select_n.15, pred[256,256]{0,1:T(8,128)(4,1)S(1)} %broadcast_compare_fusion), kind=kOutput, calls=%fused_computation.26 | convolution fusion | flops 135788544 | bytes 2760708 | tf_op jit(solution)/shard_map/while/body/eval_jaxpr/cond/branch_1_fun/tsgd,ksd->sgtk/dot_general | solution.py:17
  59.8 1.9 %fusion.2 = f32[1,8,256,128]{3,2,1,0:T(8,128)S(1)} fusion(f32[1,8,256,256]{2,3,1,0:T(8,128)S(1)} %get-tuple-element.319, f32[1,8,256,128]{3,2,1,0:T(8,128)S(1)} %get-tuple-element.259, f32[8,256]{1,0:T(8,128)S(1)} %bitcast.64, f32[8,256]{1,0:T(8,128)S(1)} %get-tuple-element.316, bf16[2,2048,1,128]{3,1,2,0:T(8,128)(2,1)} %get-tuple-element.256, s32[]{:T(128)S(6)} %add.78, ...), kind=kOutput, calls=%fused_computation.5 | convolution fusion | flops 135790592 | bytes 4276232 | tf_op jit(solution)/shard_map/while/body/eval_jaxpr/cond/branch_1_fun/sgtk,ksd->sgtd/dot_general | solution.py:28
  61.7 0.3 fusion.1
  62.0 3.7 %conditional.2 = ((f32[1,8,256]{2,1,0:T(8,128)S(1)}, f32[1,8,256]{2,1,0:T(8,128)S(1)}, f32[1,8,256,128]{3,2,1,0:T(8,128)S(1)})) conditional(s32[]{:T(128)} %convert_element_type.34, (f32[1,8,256]{2,1,0:T(8,128)S(1)}, f32[1,8,256]{2,1,0:T(8,128)S(1)}, f32[1,8,256,128]{3,2,1,0:T(8,128)S(1)}) %tuple.57, (s32[]{:T(128)}, s32[]{:T(128)}, ...), branch_computations={%region_1.0_spmd, %region_2.4_spmd} | conditional | flops 272701952 | bytes 9310306 | solution.py:63
  62.0 0.1 broadcast_compare_fusion
  62.2 1.3 %fusion.12 = (f32[8,256]{1,0:T(8,128)S(1)}, f32[1,8,256,256]{2,3,1,0:T(8,128)S(1)}) fusion(bf16[256,1,8,128]{3,0,2,1:T(8,128)(2,1)S(1)} %get-tuple-element.257, bf16[2,2048,1,128]{3,1,2,0:T(8,128)(2,1)} %get-tuple-element.256, s32[]{:T(128)S(6)} %select_n.15, pred[256,256]{0,1:T(8,128)(4,1)S(1)} %broadcast_compare_fusion), kind=kOutput, calls=%fused_computation.26 | convolution fusion | flops 135788544 | bytes 2760708 | tf_op jit(solution)/shard_map/while/body/eval_jaxpr/cond/branch_1_fun/tsgd,ksd->sgtk/dot_general | solution.py:17
  63.5 1.9 %fusion.2 = f32[1,8,256,128]{3,2,1,0:T(8,128)S(1)} fusion(f32[1,8,256,256]{2,3,1,0:T(8,128)S(1)} %get-tuple-element.319, f32[1,8,256,128]{3,2,1,0:T(8,128)S(1)} %get-tuple-element.259, f32[8,256]{1,0:T(8,128)S(1)} %bitcast.64, f32[8,256]{1,0:T(8,128)S(1)} %get-tuple-element.316, bf16[2,2048,1,128]{3,1,2,0:T(8,128)(2,1)} %get-tuple-element.256, s32[]{:T(128)S(6)} %add.78, ...), kind=kOutput, calls=%fused_computation.5 | convolution fusion | flops 135790592 | bytes 4276232 | tf_op jit(solution)/shard_map/while/body/eval_jaxpr/cond/branch_1_fun/sgtk,ksd->sgtd/dot_general | solution.py:28
  65.4 0.3 fusion.1
  65.7 3.7 %conditional.2 = ((f32[1,8,256]{2,1,0:T(8,128)S(1)}, f32[1,8,256]{2,1,0:T(8,128)S(1)}, f32[1,8,256,128]{3,2,1,0:T(8,128)S(1)})) conditional(s32[]{:T(128)} %convert_element_type.34, (f32[1,8,256]{2,1,0:T(8,128)S(1)}, f32[1,8,256]{2,1,0:T(8,128)S(1)}, f32[1,8,256,128]{3,2,1,0:T(8,128)S(1)}) %tuple.57, (s32[]{:T(128)}, s32[]{:T(128)}, ...), branch_computations={%region_1.0_spmd, %region_2.4_spmd} | conditional | flops 272701952 | bytes 9310306 | solution.py:63
  65.7 0.1 broadcast_compare_fusion
  65.9 1.3 %fusion.12 = (f32[8,256]{1,0:T(8,128)S(1)}, f32[1,8,256,256]{2,3,1,0:T(8,128)S(1)}) fusion(bf16[256,1,8,128]{3,0,2,1:T(8,128)(2,1)S(1)} %get-tuple-element.257, bf16[2,2048,1,128]{3,1,2,0:T(8,128)(2,1)} %get-tuple-element.256, s32[]{:T(128)S(6)} %select_n.15, pred[256,256]{0,1:T(8,128)(4,1)S(1)} %broadcast_compare_fusion), kind=kOutput, calls=%fused_computation.26 | convolution fusion | flops 135788544 | bytes 2760708 | tf_op jit(solution)/shard_map/while/body/eval_jaxpr/cond/branch_1_fun/tsgd,ksd->sgtk/dot_general | solution.py:17
  67.2 1.9 %fusion.2 = f32[1,8,256,128]{3,2,1,0:T(8,128)S(1)} fusion(f32[1,8,256,256]{2,3,1,0:T(8,128)S(1)} %get-tuple-element.319, f32[1,8,256,128]{3,2,1,0:T(8,128)S(1)} %get-tuple-element.259, f32[8,256]{1,0:T(8,128)S(1)} %bitcast.64, f32[8,256]{1,0:T(8,128)S(1)} %get-tuple-element.316, bf16[2,2048,1,128]{3,1,2,0:T(8,128)(2,1)} %get-tuple-element.256, s32[]{:T(128)S(6)} %add.78, ...), kind=kOutput, calls=%fused_computation.5 | convolution fusion | flops 135790592 | bytes 4276232 | tf_op jit(solution)/shard_map/while/body/eval_jaxpr/cond/branch_1_fun/sgtk,ksd->sgtd/dot_general | solution.py:28
  69.1 0.3 fusion.1
  69.4 3.7 %conditional.2 = ((f32[1,8,256]{2,1,0:T(8,128)S(1)}, f32[1,8,256]{2,1,0:T(8,128)S(1)}, f32[1,8,256,128]{3,2,1,0:T(8,128)S(1)})) conditional(s32[]{:T(128)} %convert_element_type.34, (f32[1,8,256]{2,1,0:T(8,128)S(1)}, f32[1,8,256]{2,1,0:T(8,128)S(1)}, f32[1,8,256,128]{3,2,1,0:T(8,128)S(1)}) %tuple.57, (s32[]{:T(128)}, s32[]{:T(128)}, ...), branch_computations={%region_1.0_spmd, %region_2.4_spmd} | conditional | flops 272701952 | bytes 9310306 | solution.py:63
  69.4 0.1 broadcast_compare_fusion
  69.6 1.3 %fusion.12 = (f32[8,256]{1,0:T(8,128)S(1)}, f32[1,8,256,256]{2,3,1,0:T(8,128)S(1)}) fusion(bf16[256,1,8,128]{3,0,2,1:T(8,128)(2,1)S(1)} %get-tuple-element.257, bf16[2,2048,1,128]{3,1,2,0:T(8,128)(2,1)} %get-tuple-element.256, s32[]{:T(128)S(6)} %select_n.15, pred[256,256]{0,1:T(8,128)(4,1)S(1)} %broadcast_compare_fusion), kind=kOutput, calls=%fused_computation.26 | convolution fusion | flops 135788544 | bytes 2760708 | tf_op jit(solution)/shard_map/while/body/eval_jaxpr/cond/branch_1_fun/tsgd,ksd->sgtk/dot_general | solution.py:17
  70.9 1.9 %fusion.2 = f32[1,8,256,128]{3,2,1,0:T(8,128)S(1)} fusion(f32[1,8,256,256]{2,3,1,0:T(8,128)S(1)} %get-tuple-element.319, f32[1,8,256,128]{3,2,1,0:T(8,128)S(1)} %get-tuple-element.259, f32[8,256]{1,0:T(8,128)S(1)} %bitcast.64, f32[8,256]{1,0:T(8,128)S(1)} %get-tuple-element.316, bf16[2,2048,1,128]{3,1,2,0:T(8,128)(2,1)} %get-tuple-element.256, s32[]{:T(128)S(6)} %add.78, ...), kind=kOutput, calls=%fused_computation.5 | convolution fusion | flops 135790592 | bytes 4276232 | tf_op jit(solution)/shard_map/while/body/eval_jaxpr/cond/branch_1_fun/sgtk,ksd->sgtd/dot_general | solution.py:28
  72.8 0.3 fusion.1
  73.1 3.7 %conditional.2 = ((f32[1,8,256]{2,1,0:T(8,128)S(1)}, f32[1,8,256]{2,1,0:T(8,128)S(1)}, f32[1,8,256,128]{3,2,1,0:T(8,128)S(1)})) conditional(s32[]{:T(128)} %convert_element_type.34, (f32[1,8,256]{2,1,0:T(8,128)S(1)}, f32[1,8,256]{2,1,0:T(8,128)S(1)}, f32[1,8,256,128]{3,2,1,0:T(8,128)S(1)}) %tuple.57, (s32[]{:T(128)}, s32[]{:T(128)}, ...), branch_computations={%region_1.0_spmd, %region_2.4_spmd} | conditional | flops 272701952 | bytes 9310306 | solution.py:63
  73.1 0.1 broadcast_compare_fusion
  73.3 1.3 %fusion.12 = (f32[8,256]{1,0:T(8,128)S(1)}, f32[1,8,256,256]{2,3,1,0:T(8,128)S(1)}) fusion(bf16[256,1,8,128]{3,0,2,1:T(8,128)(2,1)S(1)} %get-tuple-element.257, bf16[2,2048,1,128]{3,1,2,0:T(8,128)(2,1)} %get-tuple-element.256, s32[]{:T(128)S(6)} %select_n.15, pred[256,256]{0,1:T(8,128)(4,1)S(1)} %broadcast_compare_fusion), kind=kOutput, calls=%fused_computation.26 | convolution fusion | flops 135788544 | bytes 2760708 | tf_op jit(solution)/shard_map/while/body/eval_jaxpr/cond/branch_1_fun/tsgd,ksd->sgtk/dot_general | solution.py:17
  74.6 1.9 %fusion.2 = f32[1,8,256,128]{3,2,1,0:T(8,128)S(1)} fusion(f32[1,8,256,256]{2,3,1,0:T(8,128)S(1)} %get-tuple-element.319, f32[1,8,256,128]{3,2,1,0:T(8,128)S(1)} %get-tuple-element.259, f32[8,256]{1,0:T(8,128)S(1)} %bitcast.64, f32[8,256]{1,0:T(8,128)S(1)} %get-tuple-element.316, bf16[2,2048,1,128]{3,1,2,0:T(8,128)(2,1)} %get-tuple-element.256, s32[]{:T(128)S(6)} %add.78, ...), kind=kOutput, calls=%fused_computation.5 | convolution fusion | flops 135790592 | bytes 4276232 | tf_op jit(solution)/shard_map/while/body/eval_jaxpr/cond/branch_1_fun/sgtk,ksd->sgtd/dot_general | solution.py:28
  76.4 0.3 fusion.1
  76.8 3.7 %conditional.2 = ((f32[1,8,256]{2,1,0:T(8,128)S(1)}, f32[1,8,256]{2,1,0:T(8,128)S(1)}, f32[1,8,256,128]{3,2,1,0:T(8,128)S(1)})) conditional(s32[]{:T(128)} %convert_element_type.34, (f32[1,8,256]{2,1,0:T(8,128)S(1)}, f32[1,8,256]{2,1,0:T(8,128)S(1)}, f32[1,8,256,128]{3,2,1,0:T(8,128)S(1)}) %tuple.57, (s32[]{:T(128)}, s32[]{:T(128)}, ...), branch_computations={%region_1.0_spmd, %region_2.4_spmd} | conditional | flops 272701952 | bytes 9310306 | solution.py:63
  76.8 0.1 broadcast_compare_fusion
  76.9 1.3 %fusion.12 = (f32[8,256]{1,0:T(8,128)S(1)}, f32[1,8,256,256]{2,3,1,0:T(8,128)S(1)}) fusion(bf16[256,1,8,128]{3,0,2,1:T(8,128)(2,1)S(1)} %get-tuple-element.257, bf16[2,2048,1,128]{3,1,2,0:T(8,128)(2,1)} %get-tuple-element.256, s32[]{:T(128)S(6)} %select_n.15, pred[256,256]{0,1:T(8,128)(4,1)S(1)} %broadcast_compare_fusion), kind=kOutput, calls=%fused_computation.26 | convolution fusion | flops 135788544 | bytes 2760708 | tf_op jit(solution)/shard_map/while/body/eval_jaxpr/cond/branch_1_fun/tsgd,ksd->sgtk/dot_general | solution.py:17
  78.3 1.9 %fusion.2 = f32[1,8,256,128]{3,2,1,0:T(8,128)S(1)} fusion(f32[1,8,256,256]{2,3,1,0:T(8,128)S(1)} %get-tuple-element.319, f32[1,8,256,128]{3,2,1,0:T(8,128)S(1)} %get-tuple-element.259, f32[8,256]{1,0:T(8,128)S(1)} %bitcast.64, f32[8,256]{1,0:T(8,128)S(1)} %get-tuple-element.316, bf16[2,2048,1,128]{3,1,2,0:T(8,128)(2,1)} %get-tuple-element.256, s32[]{:T(128)S(6)} %add.78, ...), kind=kOutput, calls=%fused_computation.5 | convolution fusion | flops 135790592 | bytes 4276232 | tf_op jit(solution)/shard_map/while/body/eval_jaxpr/cond/branch_1_fun/sgtk,ksd->sgtd/dot_general | solution.py:28
  80.1 0.3 fusion.1
  80.5 3.7 %conditional.2 = ((f32[1,8,256]{2,1,0:T(8,128)S(1)}, f32[1,8,256]{2,1,0:T(8,128)S(1)}, f32[1,8,256,128]{3,2,1,0:T(8,128)S(1)})) conditional(s32[]{:T(128)} %convert_element_type.34, (f32[1,8,256]{2,1,0:T(8,128)S(1)}, f32[1,8,256]{2,1,0:T(8,128)S(1)}, f32[1,8,256,128]{3,2,1,0:T(8,128)S(1)}) %tuple.57, (s32[]{:T(128)}, s32[]{:T(128)}, ...), branch_computations={%region_1.0_spmd, %region_2.4_spmd} | conditional | flops 272701952 | bytes 9310306 | solution.py:63
  80.5 0.1 broadcast_compare_fusion
  80.6 1.3 %fusion.12 = (f32[8,256]{1,0:T(8,128)S(1)}, f32[1,8,256,256]{2,3,1,0:T(8,128)S(1)}) fusion(bf16[256,1,8,128]{3,0,2,1:T(8,128)(2,1)S(1)} %get-tuple-element.257, bf16[2,2048,1,128]{3,1,2,0:T(8,128)(2,1)} %get-tuple-element.256, s32[]{:T(128)S(6)} %select_n.15, pred[256,256]{0,1:T(8,128)(4,1)S(1)} %broadcast_compare_fusion), kind=kOutput, calls=%fused_computation.26 | convolution fusion | flops 135788544 | bytes 2760708 | tf_op jit(solution)/shard_map/while/body/eval_jaxpr/cond/branch_1_fun/tsgd,ksd->sgtk/dot_general | solution.py:17
  82.0 1.9 %fusion.2 = f32[1,8,256,128]{3,2,1,0:T(8,128)S(1)} fusion(f32[1,8,256,256]{2,3,1,0:T(8,128)S(1)} %get-tuple-element.319, f32[1,8,256,128]{3,2,1,0:T(8,128)S(1)} %get-tuple-element.259, f32[8,256]{1,0:T(8,128)S(1)} %bitcast.64, f32[8,256]{1,0:T(8,128)S(1)} %get-tuple-element.316, bf16[2,2048,1,128]{3,1,2,0:T(8,128)(2,1)} %get-tuple-element.256, s32[]{:T(128)S(6)} %add.78, ...), kind=kOutput, calls=%fused_computation.5 | convolution fusion | flops 135790592 | bytes 4276232 | tf_op jit(solution)/shard_map/while/body/eval_jaxpr/cond/branch_1_fun/sgtk,ksd->sgtd/dot_general | solution.py:28
  83.8 0.3 fusion.1
  84.2 0.1 copy.33
  84.3 0.7 fusion.11
  85.0 11.4 %all_to_all.49 = bf16[256,8,128]{2,1,0:T(8,128)(2,1)S(1)} all-to-all(bf16[256,8,128]{2,1,0:T(8,128)(2,1)S(1)} %fusion.11), channel_id=1, replica_groups=mesh['ctx'=8,'head'=4] {'head'}, dimensions={0} | all-to-all | bytes 1048576 | tf_op jit(solution)/shard_map/all_to_all | solution.py:109
  96.4 0.1 copy.35
  96.5 1.0 copy.47
  (35 shorter events, 0.2 us)
Async XLA Ops:
  6.5 9.8 %copy-start = (bf16[64,4096]{1,0:T(8,128)(2,1)S(1)}, bf16[64,4096]{1,0:T(8,128)(2,1)}, u32[]{:S(2)}) copy-start(bf16[64,4096]{1,0:T(8,128)(2,1)} %param.7) | copy-start | bytes 1572868
  6.5 48.0 %all-gather.2.cloned.1.call-start = ((), (), s32[]{:S(2)}) async-start(), calls=%async_computation.3 | async-start | bytes 1179648 | tf_op jit(solution)/shard_map/all_gather | solution.py:106
  17.3 12.3 %all-to-all-start.1 = ((bf16[64,32,128]{2,0,1:T(8,128)(2,1)}), bf16[64,32,128]{2,0,1:T(8,128)(2,1)S(1)}, u32[]{:S(2)}, u32[]{:S(2)}) async-start(bf16[64,32,128]{2,0,1:T(8,128)(2,1)} %copy_bitcast_fusion.1), calls=%async_computation.1 | async-start | bytes 1048576 | tf_op jit(solution)/shard_map/all_to_all | solution.py:92
Sparse Core Ops, SparseCore 0:
  16.5 38.0 all-gather.1
where the time goes:
time: 105 us; the launch traced here: 104 us
  waiting for transfers between devices  33.3 us (32%)
  matrix products  25.3 us (24%)
  blocking collectives  18.6 us (18%)
  between operations  13.5 us (13%)
  local copies, waits for them, and re-layouts  5.12 us (5%)
  other arithmetic  4.18 us (4%)
  starting transfers between devices  3.47 us (3%)
    all_gather x1, waiting for transfers between devices, shards(): lax.all_gather(paired_span, 'ctx', axis=1, tiled=True)  24.5 us
    dot_general x8, matrix products, attend_block(): jnp.einsum('sgtk,ksd->sgtd', weights.astype(jnp.bfloat16), value_rows, pr...  14.8 us
    all_to_all x1, blocking collectives, shards(): lax.all_to_all(result, 'head', split_axis=0, concat_axis=1, tiled=True)  11.4 us
    dot_general x8, matrix products, attend_block(): jnp.einsum('tsgd,ksd->sgtk', query_block, key_rows, preferred_element_typ...  10.5 us
    all_to_all x1, waiting for transfers between devices, shards(): lax.all_to_all(query_local, 'head', split_axis=1, concat_axis=0, tiled=True)  8.81 us
    all_to_all x1, blocking collectives, shards(): lax.all_to_all(spread, 'head', split_axis=2, concat_axis=1, tiled=True)  7.22 us
    all_to_all x1, starting transfers between devices, shards(): lax.all_to_all(query_local, 'head', split_axis=1, concat_axis=0, tiled=True)  3.47 us
    reduce_sum x8, other arithmetic, attend_block(): totals = totals * factor + jnp.sum(weights, axis=-1)  2.35 us
  transfers between devices with their start and end apart: 2, of which 2 were waited for; matrix products, arithmetic and copies ran while one was open for 1% of the time, Pallas kernels for 0%

commit v1 on v0

v1 whole, which is shorter than its diff:
```python
import functools
import math

import jax
import jax.numpy as jnp
from jax import lax
from jax.experimental import pallas as pl
from jax.experimental.pallas import tpu as pltpu
from jax.sharding import PartitionSpec as P

QH = 32
KVH = 4
HD = 128
GROUP = QH // KVH
AXES = ("ctx", "head")
PLANE = 8
FAR = -1e30
FAR_PLACE = 2**30
FACTOR = math.log2(math.e) / math.sqrt(HD)
VMEM = pl.BlockSpec(memory_space=pltpu.VMEM)
FREE = pl.CostEstimate(flops=0, bytes_accessed=0, transcendentals=0)


def pack_kernel(keys_ref, values_ref, out_ref, sems):
    width = keys_ref.shape[1]
    copies = [
        pltpu.make_async_copy(keys_ref, out_ref.at[:, :width], sems.at[0]),
        pltpu.make_async_copy(values_ref, out_ref.at[:, width:], sems.at[1]),
    ]
    for copy in copies:
        copy.start()
    for copy in copies:
        copy.wait()


def pack(keys, values):
    rows, width = keys.shape
    return pl.pallas_call(
        pack_kernel,
        out_shape=jax.ShapeDtypeStruct((rows, 2 * width), keys.dtype),
        in_specs=[pl.BlockSpec(memory_space=pltpu.HBM)] * 2,
        out_specs=VMEM,
        scratch_shapes=[pltpu.SemaphoreType.DMA((2,))],
        compiler_params=pltpu.CompilerParams(vmem_limit_bytes=2 * 2**20),
        name="pack",
    )(keys, values)


def join_kernel(a_ref, b_ref, *refs):
    rows, out_ref = a_ref.shape[0], refs[-1]
    out_ref[:rows] = a_ref[...]
    out_ref[rows:] = b_ref[...]


def join(a, b, after=()):
    return pl.pallas_call(
        join_kernel,
        out_shape=jax.ShapeDtypeStruct((2 * a.shape[0], a.shape[1]), a.dtype),
        in_specs=[VMEM] * 2 + [pl.BlockSpec(memory_space=pl.ANY)] * len(after),
        out_specs=VMEM,
        compiler_params=pltpu.CompilerParams(vmem_limit_bytes=2 * 2**20),
        cost_estimate=FREE,
        name="join",
    )(a, b, *after)


def hold_kernel(block_ref, *refs):
    refs[-1][...] = block_ref[...]


def hold(block, after=()):
    return pl.pallas_call(
        hold_kernel,
        out_shape=jax.ShapeDtypeStruct(block.shape, block.dtype),
        in_specs=[VMEM] + [pl.BlockSpec(memory_space=pl.ANY)] * len(after),
        out_specs=VMEM,
        compiler_params=pltpu.CompilerParams(vmem_limit_bytes=2 * 2**20),
        cost_estimate=FREE,
        name="hold",
    )(block, *after)


def columns(blocks, at):
    return jnp.concatenate([b[:, at : at + HD] for b in blocks], axis=0)


def lane_groups(scores):
    return [scores[:, at : at + HD] for at in range(0, scores.shape[1], HD)]


def fold_head(h, q_ref, blocks, allowed, state):
    queries = jnp.concatenate(
        [q_ref[:, (h * GROUP + g) * HD : (h * GROUP + g + 1) * HD] for g in range(GROUP)], axis=0
    )
    keys = columns(blocks, h * HD)
    values = columns(blocks, (KVH + h) * HD)
    values = jnp.concatenate([values, jnp.ones_like(values)], axis=1)
    scores = lax.dot_general(
        queries, keys, (((1,), (1,)), ((), ())), preferred_element_type=jnp.float32
    )
    if allowed is not None:
        rows, cols = allowed.shape
        scores = jnp.where(allowed[None], scores.reshape(GROUP, rows, cols), FAR)
        scores = scores.reshape(GROUP * rows, cols)
    parts = lane_groups(scores)
    peak = jnp.max(functools.reduce(jnp.maximum, parts), axis=1, keepdims=True)
    peak = jnp.broadcast_to(peak, parts[0].shape)
    if state is not None:
        peak = jnp.maximum(peak, state[0])
    weights = [jnp.exp2((part - peak) * FACTOR).astype(jnp.bfloat16) for part in parts]
    summed = lax.dot_general(
        jnp.concatenate(weights, axis=1), values, (((1,), (0,)), ((), ())),
        preferred_element_type=jnp.float32,
    )
    if state is not None:
        fade = jnp.exp2((state[0] - peak) * FACTOR)
        summed = summed + state[1] * jnp.concatenate([fade, fade], axis=1)
    return peak, summed


def store_head(h, peak, summed, peak_ref, sum_ref):
    peak_ref[h] = peak
    sum_ref[h] = summed


def finish_head(h, summed, out_ref):
    result = (summed[:, :HD] / summed[:, HD:]).astype(out_ref.dtype)
    rows = out_ref.shape[0]
    for g in range(GROUP):
        at = (h * GROUP + g) * HD
        out_ref[:, at : at + HD] = result[g * rows : (g + 1) * rows]


def own_places(shape, swapped):
    place = lax.rem(lax.axis_index(AXES), PLANE)
    even = lax.rem(place, 2) == 0
    one, two = jnp.where(even, 4, 2), jnp.where(even, 2, 4)
    order = [1, 1 ^ two, 1 ^ one, 7] if swapped else [0, one, two, 6]
    key = lax.broadcasted_iota(jnp.int32, shape, 1)
    return [(place ^ o) * shape[0] + key for o in order]


def may_read(shape, key_places):
    place = lax.rem(lax.axis_index(AXES), PLANE)
    query = place * shape[0] + lax.broadcasted_iota(jnp.int32, shape, 0)
    return jnp.concatenate(key_places, axis=1) <= jnp.concatenate([query] * len(key_places), axis=1)


def own_kernel(q_ref, mine, second, peak_ref, sum_ref):
    shape = (q_ref.shape[0], q_ref.shape[0])
    allowed = may_read(shape, own_places(shape, False))
    for h in range(KVH):
        store_head(h, *fold_head(h, q_ref, (mine, second), allowed, None), peak_ref, sum_ref)


def other_core_kernel(step, q_ref, peak_in, sum_in, *refs):
    blocks, (peak_ref, sum_ref) = refs[:-2], refs[-2:]
    shape = (q_ref.shape[0], q_ref.shape[0])
    group = jnp.full(shape, jnp.where(is_earlier(step), -1, FAR_PLACE), jnp.int32)
    allowed = may_read(shape, own_places(shape, True) + [group] * PLANE)
    for h in range(KVH):
        state = (peak_in[h], sum_in[h])
        store_head(h, *fold_head(h, q_ref, blocks, allowed, state), peak_ref, sum_ref)


def is_earlier(step):
    plane = lax.div(lax.axis_index(AXES), PLANE)
    return (plane ^ step) < plane


def next_kernel(step, q_ref, peak_in, sum_in, *refs):
    blocks, (peak_ref, sum_ref) = refs[:-2], refs[-2:]

    @pl.when(is_earlier(step))
    def _():
        for h in range(KVH):
            state = (peak_in[h], sum_in[h])
            store_head(h, *fold_head(h, q_ref, blocks, None, state), peak_ref, sum_ref)


def last_kernel(step, q_ref, peak_in, sum_in, *refs):
    blocks, out_ref = refs[:-1], refs[-1]
    earlier = is_earlier(step)

    @pl.when(earlier)
    def _():
        for h in range(KVH):
            state = (peak_in[h], sum_in[h])
            finish_head(h, fold_head(h, q_ref, blocks, None, state)[1], out_ref)

    @pl.when(jnp.logical_not(earlier))
    def _():
        for h in range(KVH):
            finish_head(h, sum_in[h], out_ref)


def state_shapes(rows):
    return (
        jax.ShapeDtypeStruct((KVH, GROUP * rows, HD), jnp.float32),
        jax.ShapeDtypeStruct((KVH, GROUP * rows, 2 * HD), jnp.float32),
    )


def call_fold(kernel, name, queries, state, blocks, out_shape, alias):
    operands = [queries, *state, *blocks]
    multi = isinstance(out_shape, tuple)
    return pl.pallas_call(
        kernel,
        out_shape=out_shape,
        in_specs=[VMEM] * len(operands),
        out_specs=(VMEM,) * len(out_shape) if multi else VMEM,
        input_output_aliases={1: 0, 2: 1} if alias else {},
        compiler_params=pltpu.CompilerParams(vmem_limit_bytes=32 * 2**20),
        cost_estimate=FREE,
        name=name,
    )(*operands)


def planes_path(queries, keys, values, count):
    rows = queries.shape[0]
    own = pack(keys, values)

    def exchange(block, even_bits, odd_bits):
        pairs = [(i, i ^ (odd_bits if i % 2 else even_bits)) for i in range(count)]
        return lax.ppermute(block, AXES, pairs)

    def spread(block, join_after=(), swap_after=()):
        mine = join(block, exchange(block, 4, 2), join_after)
        second = exchange(mine, 2, 4)
        return mine, second, exchange(mine, 1, 1), exchange(hold(second, swap_after) if swap_after else second, 1, 1)

    arrived = {1: exchange(own, PLANE, PLANE)}
    arrived[3] = hold(hold(hold(exchange(own, 3 * PLANE, 3 * PLANE))))
    arrived[2] = exchange(arrived[3], PLANE, PLANE)
    mine, second, *swapped = spread(own)
    shapes = state_shapes(rows)
    state = call_fold(own_kernel, "own", queries, (), (mine, second), shapes, False)
    early = (state[0],)
    blocks = (*swapped, *spread(arrived[1]))
    kernel = functools.partial(other_core_kernel, 1)
    state = call_fold(kernel, "other", queries, state, blocks, shapes, True)
    blocks = spread(arrived[3], early)
    kernel = functools.partial(next_kernel, 3)
    state = call_fold(kernel, "next", queries, state, blocks, shapes, True)
    blocks = spread(arrived[2], (), (state[0],))
    out = jax.ShapeDtypeStruct(queries.shape, queries.dtype)
    kernel = functools.partial(last_kernel, 2)
    return call_fold(kernel, "last", queries, state, blocks, out, False)


def span_kernel(pos_ref, q_ref, peak_in, sum_in, kv_ref, peak_ref, sum_ref):
    span, rows = kv_ref.shape[0], q_ref.shape[0]
    first, key_first = pos_ref[0], pos_ref[1] + pl.program_id(0) * span

    @pl.when(pl.program_id(0) == 0)
    def _():
        peak_ref[...] = peak_in[...]
        sum_ref[...] = sum_in[...]

    @pl.when((key_first >= 0) & (key_first < first + rows))
    def _():
        shape = (rows, span)
        key_pos = key_first + lax.broadcasted_iota(jnp.int32, shape, 1)
        allowed = key_pos <= first + lax.broadcasted_iota(jnp.int32, shape, 0)
        for h in range(KVH):
            state = (peak_ref[h], sum_ref[h])
            store_head(h, *fold_head(h, q_ref, (kv_ref,), allowed, state), peak_ref, sum_ref)


def finish_kernel(sum_ref, out_ref):
    for h in range(KVH):
        finish_head(h, sum_ref[h], out_ref)


def ring_path(queries, keys, values, spans):
    rows = queries.shape[0]
    own = pack(keys, values)
    held = lax.all_gather(own, "head", axis=0, tiled=True)
    span_len = held.shape[0]
    span = math.gcd(span_len, 512)
    shapes = state_shapes(rows)
    ctx = lax.axis_index("ctx")
    first = lax.axis_index(AXES) * rows
    whole = [pl.BlockSpec(s.shape, lambda i, d=len(s.shape): (0,) * d) for s in (queries, *shapes)]
    fold = pl.pallas_call(
        span_kernel,
        out_shape=shapes,
        grid=(span_len // span,),
        in_specs=[
            pl.BlockSpec(memory_space=pltpu.SMEM),
            *whole,
            pl.BlockSpec((span, held.shape[1]), lambda i: (i, 0)),
        ],
        out_specs=tuple(whole[1:]),
        compiler_params=pltpu.CompilerParams(vmem_limit_bytes=48 * 2**20),
        name="span",
    )

    def one_step(step, carry):
        held, state = carry
        following = lax.ppermute(held, "ctx", [(i, (i + 1) % spans) for i in range(spans)])
        place = jnp.where(ctx >= step, (ctx - step) * span_len, -span_len)
        state = fold(jnp.stack([first, place]), queries, *state, held)
        return following, tuple(state)

    state = (jnp.full(shapes[0].shape, FAR, jnp.float32), jnp.zeros(shapes[1].shape, jnp.float32))
    sums = lax.fori_loop(0, spans, one_step, (held, state))[1][1]
    return pl.pallas_call(
        finish_kernel,
        out_shape=jax.ShapeDtypeStruct(queries.shape, queries.dtype),
        in_specs=[pl.BlockSpec(memory_space=pltpu.VMEM)],
        out_specs=pl.BlockSpec(memory_space=pltpu.VMEM),
        name="finish",
    )(sums)


def solution(mesh):
    count = mesh.shape["ctx"] * mesh.shape["head"]
    by_planes = mesh.shape["head"] == 4 and mesh.shape["ctx"] == 8

    def shards(queries, keys, values):
        if by_planes:
            return planes_path(queries, keys, values, count)
        return ring_path(queries, keys, values, mesh.shape["ctx"])

    spec = P(AXES, None)
    return jax.shard_map(
        shards, mesh=mesh, in_specs=(spec, spec, spec), out_specs=spec, check_vma=False
    )
```

time: 105 us -> 38.7 us (0.37)
  the two profiles are of different devices: /device:TPU:26 before, /device:TPU:25 now
where the time goes in v1:
time: 38.7 us; the launch traced here: 38.5 us
  starting transfers between devices  20.8 us (54%)
  Pallas kernels  9.06 us (23%)
  waiting for transfers between devices  6.89 us (18%)
  local copies, waits for them, and re-layouts  1.68 us (4%)
    ppermute x19, starting transfers between devices, exchange(): return lax.ppermute(block, AXES, pairs)  20.8 us
    pallas_call x4, Pallas kernels, call_fold(): pl.pallas_call(kernel, out_shape=out_shape, in_specs=[VMEM] * len(operand...  8.9 us
    ppermute x19, waiting for transfers between devices, exchange(): return lax.ppermute(block, AXES, pairs)  6.89 us
    unnamed x6, local copies, waits for them, and re-layouts  1.68 us
  transfers between devices with their start and end apart: 19, of which 4 were waited for; matrix products, arithmetic and copies ran while one was open for 0% of the time, Pallas kernels for 17%

profile of v1, /device:TPU:25, one launch (start us, length us, event | category | flops | bytes accessed | tf_op | source)
XLA Modules:
  0.0 38.5 jit_solution(4760137765229796221)
XLA Ops:
  0.0 0.0 copy-start.1
  0.0 0.8 %copy-done.1 = bf16[64,512]{1,0:T(8,128)(2,1)S(1)} copy-done((bf16[64,512]{1,0:T(8,128)(2,1)S(1)}, bf16[64,512]{1,0:T(8,128)(2,1)}, u32[]{:S(2)}) %copy-start.1) | copy-done | bytes 65560
  0.8 0.0 copy-start.2
  0.8 0.8 %copy-done.2 = bf16[64,512]{1,0:T(8,128)(2,1)S(1)} copy-done((bf16[64,512]{1,0:T(8,128)(2,1)S(1)}, bf16[64,512]{1,0:T(8,128)(2,1)}, u32[]{:S(2)}) %copy-start.2) | copy-done | bytes 65560
  1.7 0.0 copy-start
  1.7 1.3 %collective-permute-start = (bf16[64,1024]{1,0:T(8,128)(2,1)S(1)}, bf16[64,1024]{1,0:T(8,128)(2,1)S(1)}, u32[]{:S(2)}, u32[]{:S(2)}) collective-permute-start(bf16[64,1024]{1,0:T(8,128)(2,1)S(1)} %pack.1.a_ref), channel_id=1, source_target_pairs={{0,4},{1,3},{2,6},{3,1},{4,0},{5,7},{6,2},{7,5},{8,12},{9,11},{10,... | collective-permute-start | bytes 393224 | tf_op jit(solution)/shard_map/ppermute | solution.py:225
  3.0 0.2 collective-permute-start.4
  3.2 1.1 %collective-permute-start.9 = (bf16[64,1024]{1,0:T(8,128)(2,1)S(1)}, bf16[64,1024]{1,0:T(8,128)(2,1)S(1)}, u32[]{:S(2)}, u32[]{:S(2)}) collective-permute-start(bf16[64,1024]{1,0:T(8,128)(2,1)S(1)} %pack.1.a_ref), channel_id=1, source_target_pairs={{0,24},{1,25},{2,26},{3,27},{4,28},{5,29},{6,30},{7,31},{8,16},{9,... | collective-permute-start | bytes 393224 | tf_op jit(solution)/shard_map/ppermute | solution.py:225
  4.3 1.6 %collective-permute-done.b_ref = bf16[64,1024]{1,0:T(8,128)(2,1)S(1)} collective-permute-done((bf16[64,1024]{1,0:T(8,128)(2,1)S(1)}, bf16[64,1024]{1,0:T(8,128)(2,1)S(1)}, u32[]{:S(2)}, u32[]{:S(2)}) %collective-permute-start) | collective-permute-done | bytes 131104 | tf_op jit(solution)/shard_map/ppermute | solution.py:225
  5.9 1.3 %collective-permute-start.1 = (bf16[128,1024]{1,0:T(8,128)(2,1)S(1)}, bf16[128,1024]{1,0:T(8,128)(2,1)S(1)}, u32[]{:S(2)}, u32[]{:S(2)}) collective-permute-start(bf16[128,1024]{1,0:T(8,128)(2,1)S(1)} %join.4.mine), channel_id=1, source_target_pairs={{0,2},{1,5},{2,0},{3,7},{4,6},{5,1},{6,4},{7,3},{8,10},{9,13},{10,... | collective-permute-start | bytes 786440 | tf_op jit(solution)/shard_map/ppermute | solution.py:225
  7.2 0.0 collective-permute-done.4.a_ref
  7.2 1.2 %collective-permute-start.5 = (bf16[64,1024]{1,0:T(8,128)(2,1)S(1)}, bf16[64,1024]{1,0:T(8,128)(2,1)S(1)}, u32[]{:S(2)}, u32[]{:S(2)}) collective-permute-start(bf16[64,1024]{1,0:T(8,128)(2,1)S(1)} %collective-permute-done.4.a_ref), channel_id=1, source_target_pairs={{0,4},{1,3},{2,6},{3,1},{4,0},{5,7},{6,2},{7,5},{8,12},{9,11},{10,... | collective-permute-start | bytes 393224 | tf_op jit(solution)/shard_map/ppermute | solution.py:225
  8.4 1.6 %collective-permute-done.9.block_ref = bf16[64,1024]{1,0:T(8,128)(2,1)S(1)} collective-permute-done((bf16[64,1024]{1,0:T(8,128)(2,1)S(1)}, bf16[64,1024]{1,0:T(8,128)(2,1)S(1)}, u32[]{:S(2)}, u32[]{:S(2)}) %collective-permute-start.9) | collective-permute-done | bytes 131104 | tf_op jit(solution)/shard_map/ppermute | solution.py:225
  10.1 0.3 collective-permute-start.10
  10.4 3.5 %collective-permute-start.2 = (bf16[128,1024]{1,0:T(8,128)(2,1)S(1)}, bf16[128,1024]{1,0:T(8,128)(2,1)S(1)}, u32[]{:S(2)}, u32[]{:S(2)}) collective-permute-start(bf16[128,1024]{1,0:T(8,128)(2,1)S(1)} %join.4.mine), channel_id=1, source_target_pairs={{0,1},{1,0},{2,3},{3,2},{4,5},{5,4},{6,7},{7,6},{8,9},{9,8},{10,11... | collective-permute-start | bytes 786440 | tf_op jit(solution)/shard_map/ppermute | solution.py:225
  13.9 0.9 %collective-permute-start.14 = (bf16[64,1024]{1,0:T(8,128)(2,1)S(1)}, bf16[64,1024]{1,0:T(8,128)(2,1)S(1)}, u32[]{:S(2)}, u32[]{:S(2)}) collective-permute-start(bf16[64,1024]{1,0:T(8,128)(2,1)S(1)} %hold.6.a_ref), channel_id=1, source_target_pairs={{0,8},{1,9},{2,10},{3,11},{4,12},{5,13},{6,14},{7,15},{8,0},{9,1},... | collective-permute-start | bytes 393224 | tf_op jit(solution)/shard_map/ppermute | solution.py:225
  14.8 0.0 collective-permute-done.5.b_ref
  14.8 0.4 collective-permute-start.6
  15.2 0.0 collective-permute-done.1.second
  15.2 0.0 copy-done
  15.2 0.9 %own.1 = (f32[4,512,128]{2,1,0:T(8,128)S(1)}, f32[4,512,256]{2,1,0:T(8,128)S(1)}) custom-call(bf16[64,4096]{1,0:T(8,128)(2,1)S(1)} %copy-done, bf16[128,1024]{1,0:T(8,128)(2,1)S(1)} %join.4.mine, bf16[128,1024]{1,0:T(8,128)(2,1)S(1)} %collective-permute-done.1.second), custom_call_target="tpu_custom_call" | custom-call | tf_op jit(solution)/shard_map/own/pallas_call | solution.py:207
  16.1 0.0 collective-permute-done.10.b_ref
  16.2 1.5 %collective-permute-start.11 = (bf16[128,1024]{1,0:T(8,128)(2,1)S(1)}, bf16[128,1024]{1,0:T(8,128)(2,1)S(1)}, u32[]{:S(2)}, u32[]{:S(2)}) collective-permute-start(bf16[128,1024]{1,0:T(8,128)(2,1)S(1)} %join.6.refs_0_), channel_id=1, source_target_pairs={{0,2},{1,5},{2,0},{3,7},{4,6},{5,1},{6,4},{7,3},{8,10},{9,13},{10,... | collective-permute-start | bytes 786440 | tf_op jit(solution)/shard_map/ppermute | solution.py:225
  17.6 2.5 %collective-permute-start.7 = (bf16[128,1024]{1,0:T(8,128)(2,1)S(1)}, bf16[128,1024]{1,0:T(8,128)(2,1)S(1)}, u32[]{:S(2)}, u32[]{:S(2)}) collective-permute-start(bf16[128,1024]{1,0:T(8,128)(2,1)S(1)} %join.5.refs_2_), channel_id=1, source_target_pairs={{0,1},{1,0},{2,3},{3,2},{4,5},{5,4},{6,7},{7,6},{8,9},{9,8},{10,11... | collective-permute-start | bytes 786440 | tf_op jit(solution)/shard_map/ppermute | solution.py:225
  20.1 0.0 collective-permute-done.14.a_ref
  20.1 0.7 %collective-permute-start.15 = (bf16[64,1024]{1,0:T(8,128)(2,1)S(1)}, bf16[64,1024]{1,0:T(8,128)(2,1)S(1)}, u32[]{:S(2)}, u32[]{:S(2)}) collective-permute-start(bf16[64,1024]{1,0:T(8,128)(2,1)S(1)} %collective-permute-done.14.a_ref), channel_id=1, source_target_pairs={{0,4},{1,3},{2,6},{3,1},{4,0},{5,7},{6,2},{7,5},{8,12},{9,11},{10,... | collective-permute-start | bytes 393224 | tf_op jit(solution)/shard_map/ppermute | solution.py:225
  20.7 0.0 collective-permute-done.2.refs_0_
  20.7 0.6 %collective-permute-start.3 = (bf16[128,1024]{1,0:T(8,128)(2,1)S(1)}, bf16[128,1024]{1,0:T(8,128)(2,1)S(1)}, u32[]{:S(2)}, u32[]{:S(2)}) collective-permute-start(bf16[128,1024]{1,0:T(8,128)(2,1)S(1)} %collective-permute-done.1.second), channel_id=1, source_target_pairs={{0,1},{1,0},{2,3},{3,2},{4,5},{5,4},{6,7},{7,6},{8,9},{9,8},{10,11... | collective-permute-start | bytes 786440 | tf_op jit(solution)/shard_map/ppermute | solution.py:225
  21.4 0.0 collective-permute-done.6.refs_3_
  21.4 1.8 %collective-permute-start.8 = (bf16[128,1024]{1,0:T(8,128)(2,1)S(1)}, bf16[128,1024]{1,0:T(8,128)(2,1)S(1)}, u32[]{:S(2)}, u32[]{:S(2)}) collective-permute-start(bf16[128,1024]{1,0:T(8,128)(2,1)S(1)} %collective-permute-done.6.refs_3_), channel_id=1, source_target_pairs={{0,1},{1,0},{2,3},{3,2},{4,5},{5,4},{6,7},{7,6},{8,9},{9,8},{10,11... | collective-permute-start | bytes 786440 | tf_op jit(solution)/shard_map/ppermute | solution.py:225
  23.2 2.5 %collective-permute-done.15.b_ref = bf16[64,1024]{1,0:T(8,128)(2,1)S(1)} collective-permute-done((bf16[64,1024]{1,0:T(8,128)(2,1)S(1)}, bf16[64,1024]{1,0:T(8,128)(2,1)S(1)}, u32[]{:S(2)}, u32[]{:S(2)}) %collective-permute-start.15) | collective-permute-done | bytes 131104 | tf_op jit(solution)/shard_map/ppermute | solution.py:225
  25.7 0.0 collective-permute-start.12
  25.7 0.0 collective-permute-done.11.refs_1_
  25.7 1.7 %collective-permute-start.13 = (bf16[128,1024]{1,0:T(8,128)(2,1)S(1)}, bf16[128,1024]{1,0:T(8,128)(2,1)S(1)}, u32[]{:S(2)}, u32[]{:S(2)}) collective-permute-start(bf16[128,1024]{1,0:T(8,128)(2,1)S(1)} %collective-permute-done.11.refs_1_), channel_id=1, source_target_pairs={{0,1},{1,0},{2,3},{3,2},{4,5},{5,4},{6,7},{7,6},{8,9},{9,8},{10,11... | collective-permute-start | bytes 786440 | tf_op jit(solution)/shard_map/ppermute | solution.py:225
  27.4 0.0 collective-permute-done.7.refs_4_
  27.4 1.3 %collective-permute-start.16 = (bf16[128,1024]{1,0:T(8,128)(2,1)S(1)}, bf16[128,1024]{1,0:T(8,128)(2,1)S(1)}, u32[]{:S(2)}, u32[]{:S(2)}) collective-permute-start(bf16[128,1024]{1,0:T(8,128)(2,1)S(1)} %join.7.refs_0_), channel_id=1, source_target_pairs={{0,2},{1,5},{2,0},{3,7},{4,6},{5,1},{6,4},{7,3},{8,10},{9,13},{10,... | collective-permute-start | bytes 786440 | tf_op jit(solution)/shard_map/ppermute | solution.py:225
  28.7 0.0 collective-permute-done.3.refs_1_
  28.7 0.0 collective-permute-start.17
  28.7 0.0 collective-permute-done.8.refs_5_
  28.7 3.1 %other.1 = (f32[4,512,128]{2,1,0:T(8,128)S(1)}, f32[4,512,256]{2,1,0:T(8,128)S(1)}) custom-call(bf16[64,4096]{1,0:T(8,128)(2,1)S(1)} %copy-done, f32[4,512,128]{2,1,0:T(8,128)S(1)} %get-tuple-element.11.peak_in.refs_0_, f32[4,512,256]{2,1,0:T(8,128)S(1)} %get-tuple-element.12.sum_in, ...), custom_call_target="tpu_custom_call", output_to_operand_aliasing={{0}: (1, {}), {1}: (2, {})} | custom-call | tf_op jit(solution)/shard_map/other/pallas_call | solution.py:207
  31.8 0.0 collective-permute-done.12.refs_2_
  31.8 0.0 collective-permute-done.13.refs_3_
  31.8 2.3 %next.1 = (f32[4,512,128]{2,1,0:T(8,128)S(1)}, f32[4,512,256]{2,1,0:T(8,128)S(1)}) custom-call(bf16[64,4096]{1,0:T(8,128)(2,1)S(1)} %copy-done, f32[4,512,128]{2,1,0:T(8,128)S(1)} %get-tuple-element.13.peak_in, f32[4,512,256]{2,1,0:T(8,128)S(1)} %get-tuple-element.14.sum_in, ...), custom_call_target="tpu_custom_call", output_to_operand_aliasing={{0}: (1, {}), {1}: (2, {})} | custom-call | tf_op jit(solution)/shard_map/next/pallas_call | solution.py:207
  34.2 0.0 collective-permute-done.16.block_ref.refs_1_
  34.2 0.6 %collective-permute-start.18 = (bf16[128,1024]{1,0:T(8,128)(2,1)S(1)}, bf16[128,1024]{1,0:T(8,128)(2,1)S(1)}, u32[]{:S(2)}, u32[]{:S(2)}) collective-permute-start(bf16[128,1024]{1,0:T(8,128)(2,1)S(1)} %hold.7), channel_id=1, source_target_pairs={{0,1},{1,0},{2,3},{3,2},{4,5},{5,4},{6,7},{7,6},{8,9},{9,8},{10,11... | collective-permute-start | bytes 786440 | tf_op jit(solution)/shard_map/ppermute | solution.py:225
  34.8 0.0 collective-permute-done.17.refs_2_
  34.8 1.2 %collective-permute-done.18.refs_3_ = bf16[128,1024]{1,0:T(8,128)(2,1)S(1)} collective-permute-done((bf16[128,1024]{1,0:T(8,128)(2,1)S(1)}, bf16[128,1024]{1,0:T(8,128)(2,1)S(1)}, u32[]{:S(2)}, u32[]{:S(2)}) %collective-permute-start.18) | collective-permute-done | bytes 262176 | tf_op jit(solution)/shard_map/ppermute | solution.py:225
  35.9 2.6 %last.1 = bf16[64,4096]{1,0:T(8,128)(2,1)} custom-call(bf16[64,4096]{1,0:T(8,128)(2,1)S(1)} %copy-done, f32[4,512,128]{2,1,0:T(8,128)S(1)} %get-tuple-element.15.refs_0_.peak_in, f32[4,512,256]{2,1,0:T(8,128)S(1)} %get-tuple-element.16.sum_in, bf16[128,1024]{1,0:T(8,128)(2,1)S(1)} %join.7.refs_0_, ...), custom_call_target="tpu_custom_call" | custom-call | tf_op jit(solution)/shard_map/last/pallas_call | solution.py:207
  (9 shorter events, 0.2 us)
Async XLA Ops:
  0.0 0.8 %copy-start.1 = (bf16[64,512]{1,0:T(8,128)(2,1)S(1)}, bf16[64,512]{1,0:T(8,128)(2,1)}, u32[]{:S(2)}) copy-start(bf16[64,512]{1,0:T(8,128)(2,1)} %keys_ref.1) | copy-start | bytes 196612
  0.8 0.8 %copy-start.2 = (bf16[64,512]{1,0:T(8,128)(2,1)S(1)}, bf16[64,512]{1,0:T(8,128)(2,1)}, u32[]{:S(2)}) copy-start(bf16[64,512]{1,0:T(8,128)(2,1)} %values_ref.1) | copy-start | bytes 196612
  1.7 13.5 %copy-start = (bf16[64,4096]{1,0:T(8,128)(2,1)S(1)}, bf16[64,4096]{1,0:T(8,128)(2,1)}, u32[]{:S(2)}) copy-start(bf16[64,4096]{1,0:T(8,128)(2,1)} %q_ref.7) | copy-start | bytes 1572868
  1.7 4.2 %collective-permute-start = (bf16[64,1024]{1,0:T(8,128)(2,1)S(1)}, bf16[64,1024]{1,0:T(8,128)(2,1)S(1)}, u32[]{:S(2)}, u32[]{:S(2)}) collective-permute-start(bf16[64,1024]{1,0:T(8,128)(2,1)S(1)} %pack.1.a_ref), channel_id=1, source_target_pairs={{0,4},{1,3},{2,6},{3,1},{4,0},{5,7},{6,2},{7,5},{8,12},{9,11},{10,... | collective-permute-start | bytes 393224 | tf_op jit(solution)/shard_map/ppermute | solution.py:225
  3.0 4.2 %collective-permute-start.4 = (bf16[64,1024]{1,0:T(8,128)(2,1)S(1)}, bf16[64,1024]{1,0:T(8,128)(2,1)S(1)}, u32[]{:S(2)}, u32[]{:S(2)}) collective-permute-start(bf16[64,1024]{1,0:T(8,128)(2,1)S(1)} %pack.1.a_ref), channel_id=1, source_target_pairs={{0,8},{1,9},{2,10},{3,11},{4,12},{5,13},{6,14},{7,15},{8,0},{9,1},... | collective-permute-start | bytes 393224 | tf_op jit(solution)/shard_map/ppermute | solution.py:225
  3.2 6.8 %collective-permute-start.9 = (bf16[64,1024]{1,0:T(8,128)(2,1)S(1)}, bf16[64,1024]{1,0:T(8,128)(2,1)S(1)}, u32[]{:S(2)}, u32[]{:S(2)}) collective-permute-start(bf16[64,1024]{1,0:T(8,128)(2,1)S(1)} %pack.1.a_ref), channel_id=1, source_target_pairs={{0,24},{1,25},{2,26},{3,27},{4,28},{5,29},{6,30},{7,31},{8,16},{9,... | collective-permute-start | bytes 393224 | tf_op jit(solution)/shard_map/ppermute | solution.py:225
  5.9 9.3 %collective-permute-start.1 = (bf16[128,1024]{1,0:T(8,128)(2,1)S(1)}, bf16[128,1024]{1,0:T(8,128)(2,1)S(1)}, u32[]{:S(2)}, u32[]{:S(2)}) collective-permute-start(bf16[128,1024]{1,0:T(8,128)(2,1)S(1)} %join.4.mine), channel_id=1, source_target_pairs={{0,2},{1,5},{2,0},{3,7},{4,6},{5,1},{6,4},{7,3},{8,10},{9,13},{10,... | collective-permute-start | bytes 786440 | tf_op jit(solution)/shard_map/ppermute | solution.py:225
  7.2 7.6 %collective-permute-start.5 = (bf16[64,1024]{1,0:T(8,128)(2,1)S(1)}, bf16[64,1024]{1,0:T(8,128)(2,1)S(1)}, u32[]{:S(2)}, u32[]{:S(2)}) collective-permute-start(bf16[64,1024]{1,0:T(8,128)(2,1)S(1)} %collective-permute-done.4.a_ref), channel_id=1, source_target_pairs={{0,4},{1,3},{2,6},{3,1},{4,0},{5,7},{6,2},{7,5},{8,12},{9,11},{10,... | collective-permute-start | bytes 393224 | tf_op jit(solution)/shard_map/ppermute | solution.py:225
  10.1 6.1 %collective-permute-start.10 = (bf16[64,1024]{1,0:T(8,128)(2,1)S(1)}, bf16[64,1024]{1,0:T(8,128)(2,1)S(1)}, u32[]{:S(2)}, u32[]{:S(2)}) collective-permute-start(bf16[64,1024]{1,0:T(8,128)(2,1)S(1)} %hold.6.a_ref), channel_id=1, source_target_pairs={{0,4},{1,3},{2,6},{3,1},{4,0},{5,7},{6,2},{7,5},{8,12},{9,11},{10,... | collective-permute-start | bytes 393224 | tf_op jit(solution)/shard_map/ppermute | solution.py:225
  10.4 10.4 %collective-permute-start.2 = (bf16[128,1024]{1,0:T(8,128)(2,1)S(1)}, bf16[128,1024]{1,0:T(8,128)(2,1)S(1)}, u32[]{:S(2)}, u32[]{:S(2)}) collective-permute-start(bf16[128,1024]{1,0:T(8,128)(2,1)S(1)} %join.4.mine), channel_id=1, source_target_pairs={{0,1},{1,0},{2,3},{3,2},{4,5},{5,4},{6,7},{7,6},{8,9},{9,8},{10,11... | collective-permute-start | bytes 786440 | tf_op jit(solution)/shard_map/ppermute | solution.py:225
  13.9 6.2 %collective-permute-start.14 = (bf16[64,1024]{1,0:T(8,128)(2,1)S(1)}, bf16[64,1024]{1,0:T(8,128)(2,1)S(1)}, u32[]{:S(2)}, u32[]{:S(2)}) collective-permute-start(bf16[64,1024]{1,0:T(8,128)(2,1)S(1)} %hold.6.a_ref), channel_id=1, source_target_pairs={{0,8},{1,9},{2,10},{3,11},{4,12},{5,13},{6,14},{7,15},{8,0},{9,1},... | collective-permute-start | bytes 393224 | tf_op jit(solution)/shard_map/ppermute | solution.py:225
  14.8 6.5 %collective-permute-start.6 = (bf16[128,1024]{1,0:T(8,128)(2,1)S(1)}, bf16[128,1024]{1,0:T(8,128)(2,1)S(1)}, u32[]{:S(2)}, u32[]{:S(2)}) collective-permute-start(bf16[128,1024]{1,0:T(8,128)(2,1)S(1)} %join.5.refs_2_), channel_id=1, source_target_pairs={{0,2},{1,5},{2,0},{3,7},{4,6},{5,1},{6,4},{7,3},{8,10},{9,13},{10,... | collective-permute-start | bytes 786440 | tf_op jit(solution)/shard_map/ppermute | solution.py:225
  16.2 9.5 %collective-permute-start.11 = (bf16[128,1024]{1,0:T(8,128)(2,1)S(1)}, bf16[128,1024]{1,0:T(8,128)(2,1)S(1)}, u32[]{:S(2)}, u32[]{:S(2)}) collective-permute-start(bf16[128,1024]{1,0:T(8,128)(2,1)S(1)} %join.6.refs_0_), channel_id=1, source_target_pairs={{0,2},{1,5},{2,0},{3,7},{4,6},{5,1},{6,4},{7,3},{8,10},{9,13},{10,... | collective-permute-start | bytes 786440 | tf_op jit(solution)/shard_map/ppermute | solution.py:225
  17.6 9.8 %collective-permute-start.7 = (bf16[128,1024]{1,0:T(8,128)(2,1)S(1)}, bf16[128,1024]{1,0:T(8,128)(2,1)S(1)}, u32[]{:S(2)}, u32[]{:S(2)}) collective-permute-start(bf16[128,1024]{1,0:T(8,128)(2,1)S(1)} %join.5.refs_2_), channel_id=1, source_target_pairs={{0,1},{1,0},{2,3},{3,2},{4,5},{5,4},{6,7},{7,6},{8,9},{9,8},{10,11... | collective-permute-start | bytes 786440 | tf_op jit(solution)/shard_map/ppermute | solution.py:225
  20.1 5.6 %collective-permute-start.15 = (bf16[64,1024]{1,0:T(8,128)(2,1)S(1)}, bf16[64,1024]{1,0:T(8,128)(2,1)S(1)}, u32[]{:S(2)}, u32[]{:S(2)}) collective-permute-start(bf16[64,1024]{1,0:T(8,128)(2,1)S(1)} %collective-permute-done.14.a_ref), channel_id=1, source_target_pairs={{0,4},{1,3},{2,6},{3,1},{4,0},{5,7},{6,2},{7,5},{8,12},{9,11},{10,... | collective-permute-start | bytes 393224 | tf_op jit(solution)/shard_map/ppermute | solution.py:225
  20.7 8.0 %collective-permute-start.3 = (bf16[128,1024]{1,0:T(8,128)(2,1)S(1)}, bf16[128,1024]{1,0:T(8,128)(2,1)S(1)}, u32[]{:S(2)}, u32[]{:S(2)}) collective-permute-start(bf16[128,1024]{1,0:T(8,128)(2,1)S(1)} %collective-permute-done.1.second), channel_id=1, source_target_pairs={{0,1},{1,0},{2,3},{3,2},{4,5},{5,4},{6,7},{7,6},{8,9},{9,8},{10,11... | collective-permute-start | bytes 786440 | tf_op jit(solution)/shard_map/ppermute | solution.py:225
  21.4 7.4 %collective-permute-start.8 = (bf16[128,1024]{1,0:T(8,128)(2,1)S(1)}, bf16[128,1024]{1,0:T(8,128)(2,1)S(1)}, u32[]{:S(2)}, u32[]{:S(2)}) collective-permute-start(bf16[128,1024]{1,0:T(8,128)(2,1)S(1)} %collective-permute-done.6.refs_3_), channel_id=1, source_target_pairs={{0,1},{1,0},{2,3},{3,2},{4,5},{5,4},{6,7},{7,6},{8,9},{9,8},{10,11... | collective-permute-start | bytes 786440 | tf_op jit(solution)/shard_map/ppermute | solution.py:225
  25.7 6.1 %collective-permute-start.12 = (bf16[128,1024]{1,0:T(8,128)(2,1)S(1)}, bf16[128,1024]{1,0:T(8,128)(2,1)S(1)}, u32[]{:S(2)}, u32[]{:S(2)}) collective-permute-start(bf16[128,1024]{1,0:T(8,128)(2,1)S(1)} %join.6.refs_0_), channel_id=1, source_target_pairs={{0,1},{1,0},{2,3},{3,2},{4,5},{5,4},{6,7},{7,6},{8,9},{9,8},{10,11... | collective-permute-start | bytes 786440 | tf_op jit(solution)/shard_map/ppermute | solution.py:225
  25.7 6.1 %collective-permute-start.13 = (bf16[128,1024]{1,0:T(8,128)(2,1)S(1)}, bf16[128,1024]{1,0:T(8,128)(2,1)S(1)}, u32[]{:S(2)}, u32[]{:S(2)}) collective-permute-start(bf16[128,1024]{1,0:T(8,128)(2,1)S(1)} %collective-permute-done.11.refs_1_), channel_id=1, source_target_pairs={{0,1},{1,0},{2,3},{3,2},{4,5},{5,4},{6,7},{7,6},{8,9},{9,8},{10,11... | collective-permute-start | bytes 786440 | tf_op jit(solution)/shard_map/ppermute | solution.py:225
  27.4 6.7 %collective-permute-start.16 = (bf16[128,1024]{1,0:T(8,128)(2,1)S(1)}, bf16[128,1024]{1,0:T(8,128)(2,1)S(1)}, u32[]{:S(2)}, u32[]{:S(2)}) collective-permute-start(bf16[128,1024]{1,0:T(8,128)(2,1)S(1)} %join.7.refs_0_), channel_id=1, source_target_pairs={{0,2},{1,5},{2,0},{3,7},{4,6},{5,1},{6,4},{7,3},{8,10},{9,13},{10,... | collective-permute-start | bytes 786440 | tf_op jit(solution)/shard_map/ppermute | solution.py:225
  28.7 6.1 %collective-permute-start.17 = (bf16[128,1024]{1,0:T(8,128)(2,1)S(1)}, bf16[128,1024]{1,0:T(8,128)(2,1)S(1)}, u32[]{:S(2)}, u32[]{:S(2)}) collective-permute-start(bf16[128,1024]{1,0:T(8,128)(2,1)S(1)} %join.7.refs_0_), channel_id=1, source_target_pairs={{0,1},{1,0},{2,3},{3,2},{4,5},{5,4},{6,7},{7,6},{8,9},{9,8},{10,11... | collective-permute-start | bytes 786440 | tf_op jit(solution)/shard_map/ppermute | solution.py:225
  34.2 1.7 %collective-permute-start.18 = (bf16[128,1024]{1,0:T(8,128)(2,1)S(1)}, bf16[128,1024]{1,0:T(8,128)(2,1)S(1)}, u32[]{:S(2)}, u32[]{:S(2)}) collective-permute-start(bf16[128,1024]{1,0:T(8,128)(2,1)S(1)} %hold.7), channel_id=1, source_target_pairs={{0,1},{1,0},{2,3},{3,2},{4,5},{5,4},{6,7},{7,6},{8,9},{9,8},{10,11... | collective-permute-start | bytes 786440 | tf_op jit(solution)/shard_map/ppermute | solution.py:225

commit v2 on v1

v2 whole, which is shorter than its diff:
```python
import functools
import math

import jax
import jax.numpy as jnp
from jax import lax
from jax.experimental import pallas as pl
from jax.experimental.pallas import tpu as pltpu
from jax.sharding import PartitionSpec as P

QH = 32
KVH = 4
HD = 128
GROUP = QH // KVH
AXES = ("ctx", "head")
PLANE = 8
FAR = -1e30
FACTOR = math.log2(math.e) / math.sqrt(HD)
VMEM = pl.BlockSpec(memory_space=pltpu.VMEM)
FREE = pl.CostEstimate(flops=0, bytes_accessed=0, transcendentals=0)


def pack_kernel(keys_ref, values_ref, out_ref, sems):
    width = keys_ref.shape[1]
    copies = [
        pltpu.make_async_copy(keys_ref, out_ref.at[:, :width], sems.at[0]),
        pltpu.make_async_copy(values_ref, out_ref.at[:, width:], sems.at[1]),
    ]
    for copy in copies:
        copy.start()
    for copy in copies:
        copy.wait()


def pack(keys, values):
    rows, width = keys.shape
    return pl.pallas_call(
        pack_kernel,
        out_shape=jax.ShapeDtypeStruct((rows, 2 * width), keys.dtype),
        in_specs=[pl.BlockSpec(memory_space=pltpu.HBM)] * 2,
        out_specs=VMEM,
        scratch_shapes=[pltpu.SemaphoreType.DMA((2,))],
        compiler_params=pltpu.CompilerParams(vmem_limit_bytes=2 * 2**20),
        name="pack",
    )(keys, values)


def join_kernel(count, *refs):
    out_ref, rows = refs[-1], 0
    for ref in refs[:count]:
        out_ref[rows : rows + ref.shape[0]] = ref[...]
        rows += ref.shape[0]


def move(kernel, name, blocks, rows, after=()):
    return pl.pallas_call(
        kernel,
        out_shape=jax.ShapeDtypeStruct((rows, blocks[0].shape[1]), blocks[0].dtype),
        in_specs=[VMEM] * len(blocks) + [pl.BlockSpec(memory_space=pl.ANY)] * len(after),
        out_specs=VMEM,
        compiler_params=pltpu.CompilerParams(vmem_limit_bytes=2 * 2**20),
        cost_estimate=FREE,
        name=name,
    )(*blocks, *after)


def join(*blocks, after=()):
    kernel = functools.partial(join_kernel, len(blocks))
    return move(kernel, "join", blocks, sum(b.shape[0] for b in blocks), after)


def hold(block, times=1, after=()):
    for _ in range(times):
        block = join(block, after=after)
    return block


def columns(blocks, at):
    return jnp.concatenate([b[:, at : at + HD] for b in blocks], axis=0)


def weigh(scores, spec, marks):
    if spec[0] == "step":
        return scores + marks[spec]
    rows, cols = marks[spec].shape
    scores = jnp.where(marks[spec][None], scores.reshape(GROUP, rows, cols), FAR)
    return scores.reshape(GROUP * rows, cols)


def make_marks(specs, rows):
    index = lax.axis_index(AXES)
    place, plane = lax.rem(index, PLANE), lax.div(index, PLANE)
    even = lax.rem(place, 2) == 0
    one, two = jnp.where(even, 4, 2), jnp.where(even, 2, 4)
    orders = {"mine": (0, one), "second": (two, 6), "mine_": (1, 1 ^ two), "second_": (1 ^ one, 7)}
    shape = (rows, rows)
    query = place * rows + lax.broadcasted_iota(jnp.int32, shape, 0)
    query = jnp.concatenate([query, query], axis=1)
    key = lax.broadcasted_iota(jnp.int32, shape, 1)
    marks = {}
    for spec in specs:
        if spec[0] == "step":
            marks[spec] = jnp.where((plane ^ spec[1]) < plane, 0.0, FAR)
        else:
            places = [(place ^ o) * rows + key for o in orders[spec[1]]]
            marks[spec] = jnp.concatenate(places, axis=1) <= query
    return marks


def fold_head(h, q_ref, blocks, specs, marks, state):
    queries = jnp.concatenate(
        [q_ref[:, (h * GROUP + g) * HD : (h * GROUP + g + 1) * HD] for g in range(GROUP)], axis=0
    )
    keys = columns(blocks, h * HD)
    values = columns(blocks, (KVH + h) * HD)
    values = jnp.concatenate([values, jnp.ones_like(values)], axis=1)
    scores = lax.dot_general(
        queries, keys, (((1,), (1,)), ((), ())), preferred_element_type=jnp.float32
    )
    parts = [scores[:, at : at + HD] for at in range(0, scores.shape[1], HD)]
    parts = [weigh(part, spec, marks) for part, spec in zip(parts, specs, strict=True)]
    peak = jnp.max(functools.reduce(jnp.maximum, parts), axis=1, keepdims=True)
    peak = jnp.broadcast_to(peak, parts[0].shape)
    if state is not None:
        peak = jnp.maximum(peak, state[0])
    weights = [jnp.exp2((part - peak) * FACTOR).astype(jnp.bfloat16) for part in parts]
    summed = lax.dot_general(
        jnp.concatenate(weights, axis=1), values, (((1,), (0,)), ((), ())),
        preferred_element_type=jnp.float32,
    )
    if state is not None:
        fade = jnp.exp2((state[0] - peak) * FACTOR)
        summed = summed + state[1] * jnp.concatenate([fade, fade], axis=1)
    return peak, summed


def finish_head(h, summed, out_ref):
    result = (summed[:, :HD] / summed[:, HD:]).astype(out_ref.dtype)
    rows = out_ref.shape[0]
    for g in range(GROUP):
        at = (h * GROUP + g) * HD
        out_ref[:, at : at + HD] = result[g * rows : (g + 1) * rows]


def fold_kernel(specs, has_state, last, q_ref, *refs):
    state_refs, refs = (refs[:2], refs[2:]) if has_state else ((), refs)
    blocks, outs = (refs[:-1], refs[-1:]) if last else (refs[:-2], refs[-2:])
    marks = make_marks(specs, q_ref.shape[0])
    for h in range(KVH):
        state = tuple(ref[h] for ref in state_refs) or None
        peak, summed = fold_head(h, q_ref, blocks, specs, marks, state)
        if last:
            finish_head(h, summed, outs[0])
        else:
            outs[0][h], outs[1][h] = peak, summed


def state_shapes(rows):
    return (
        jax.ShapeDtypeStruct((KVH, GROUP * rows, HD), jnp.float32),
        jax.ShapeDtypeStruct((KVH, GROUP * rows, 2 * HD), jnp.float32),
    )


def fold(queries, state, pieces, last=False):
    rows = queries.shape[0]
    blocks = [block for block, _ in pieces]
    specs = tuple(spec for _, block_specs in pieces for spec in block_specs)
    operands = [queries, *state, *blocks]
    out_shape = jax.ShapeDtypeStruct(queries.shape, queries.dtype) if last else state_shapes(rows)
    return pl.pallas_call(
        functools.partial(fold_kernel, specs, bool(state), last),
        out_shape=out_shape,
        in_specs=[VMEM] * len(operands),
        out_specs=VMEM if last else (VMEM, VMEM),
        input_output_aliases={1: 0, 2: 1} if state and not last else {},
        compiler_params=pltpu.CompilerParams(vmem_limit_bytes=32 * 2**20),
        cost_estimate=FREE,
        name=f"fold{len(specs)}{'s' if state else 'n'}{'l' if last else ''}",
    )(*operands)


def planes_path(queries, keys, values, count):
    rows = queries.shape[0]
    own = pack(keys, values)

    def exchange(block, even_bits, odd_bits):
        pairs = [(i, i ^ (odd_bits if i % 2 else even_bits)) for i in range(count)]
        return lax.ppermute(block, AXES, pairs)

    def swap(block):
        return exchange(block, 1, 1)

    def double(block, after=()):
        mine = join(block, exchange(block, 4, 2), after=after)
        return mine, exchange(mine, 2, 4)

    group3 = hold(exchange(own, 3 * PLANE, 3 * PLANE), 3)
    group2 = hold(exchange(group3, PLANE, PLANE), 1)
    mine_own, second_own = ("own", "mine"), ("own", "second")
    mine_swapped, second_swapped = ("own", "mine_"), ("own", "second_")
    mine0, second0 = double(own)
    swapped0 = (swap(mine0), swap(second0))
    state = fold(queries, (), [(mine0, (mine_own,)), (second0, (second_own,))])
    early = (state[0],)
    mine1, second1 = hold(exchange(mine0, PLANE, PLANE), 1), exchange(second0, PLANE, PLANE)
    swapped1 = (swap(mine1), swap(second1))
    state = fold(queries, state, [(swapped0[0], (mine_swapped,)), (swapped0[1], (second_swapped,)), (mine1, (("step", 1),)), (second1, (("step", 1),)), (swapped1[0], (("step", 1),)), (swapped1[1], (("step", 1),))])
    mine3, second3 = double(group3)
    mine2, second2 = double(group2, after=early)
    swapped3 = (swap(mine3), swap(second3))
    state = fold(queries, state, [(mine3, (("step", 3),)), (second3, (("step", 3),)), (swapped3[0], (("step", 3),)), (swapped3[1], (("step", 3),))])
    swapped2 = (swap(mine2), swap(hold(second2, after=(state[0],))))
    pieces = [(mine2, (("step", 2),)), (second2, (("step", 2),)), (swapped2[0], (("step", 2),)), (swapped2[1], (("step", 2),))]
    return fold(queries, state, pieces, last=True)


def span_kernel(pos_ref, q_ref, peak_in, sum_in, kv_ref, peak_ref, sum_ref):
    span, rows = kv_ref.shape[0], q_ref.shape[0]
    first, key_first = pos_ref[0], pos_ref[1] + pl.program_id(0) * span

    @pl.when(pl.program_id(0) == 0)
    def _():
        peak_ref[...] = peak_in[...]
        sum_ref[...] = sum_in[...]

    @pl.when((key_first >= 0) & (key_first < first + rows))
    def _():
        shape = (rows, span)
        key_pos = key_first + lax.broadcasted_iota(jnp.int32, shape, 1)
        allowed = key_pos <= first + lax.broadcasted_iota(jnp.int32, shape, 0)
        specs = [("key", at) for at in range(0, span, HD)]
        marks = {spec: allowed[:, spec[1] : spec[1] + HD] for spec in specs}
        for h in range(KVH):
            state = (peak_ref[h], sum_ref[h])
            peak_ref[h], sum_ref[h] = fold_head(h, q_ref, (kv_ref,), specs, marks, state)


def finish_kernel(sum_ref, out_ref):
    for h in range(KVH):
        finish_head(h, sum_ref[h], out_ref)


def ring_path(queries, keys, values, spans):
    rows = queries.shape[0]
    own = pack(keys, values)
    held = lax.all_gather(own, "head", axis=0, tiled=True)
    span_len = held.shape[0]
    span = math.gcd(span_len, 512)
    shapes = state_shapes(rows)
    ctx = lax.axis_index("ctx")
    first = lax.axis_index(AXES) * rows
    whole = [pl.BlockSpec(s.shape, lambda i, d=len(s.shape): (0,) * d) for s in (queries, *shapes)]
    fold = pl.pallas_call(
        span_kernel,
        out_shape=shapes,
        grid=(span_len // span,),
        in_specs=[
            pl.BlockSpec(memory_space=pltpu.SMEM),
            *whole,
            pl.BlockSpec((span, held.shape[1]), lambda i: (i, 0)),
        ],
        out_specs=tuple(whole[1:]),
        compiler_params=pltpu.CompilerParams(vmem_limit_bytes=48 * 2**20),
        name="span",
    )

    def one_step(step, carry):
        held, state = carry
        following = lax.ppermute(held, "ctx", [(i, (i + 1) % spans) for i in range(spans)])
        place = jnp.where(ctx >= step, (ctx - step) * span_len, -span_len)
        state = fold(jnp.stack([first, place]), queries, *state, held)
        return following, tuple(state)

    state = (jnp.full(shapes[0].shape, FAR, jnp.float32), jnp.zeros(shapes[1].shape, jnp.float32))
    sums = lax.fori_loop(0, spans, one_step, (held, state))[1][1]
    return pl.pallas_call(
        finish_kernel,
        out_shape=jax.ShapeDtypeStruct(queries.shape, queries.dtype),
        in_specs=[pl.BlockSpec(memory_space=pltpu.VMEM)],
        out_specs=pl.BlockSpec(memory_space=pltpu.VMEM),
        name="finish",
    )(sums)


def solution(mesh):
    count = mesh.shape["ctx"] * mesh.shape["head"]
    by_planes = mesh.shape["head"] == 4 and mesh.shape["ctx"] == 8

    def shards(queries, keys, values):
        if by_planes:
            return planes_path(queries, keys, values, count)
        return ring_path(queries, keys, values, mesh.shape["ctx"])

    spec = P(AXES, None)
    return jax.shard_map(
        shards, mesh=mesh, in_specs=(spec, spec, spec), out_specs=spec, check_vma=False
    )
```

time: 38.7 us -> 39.1 us (1.010)
  the two profiles are of different devices: /device:TPU:25 before, /device:TPU:0 now
where the time goes in v2:
time: 39.1 us; the launch traced here: 38.9 us
  starting transfers between devices  20.3 us (52%)
  Pallas kernels  8.98 us (23%)
  waiting for transfers between devices  7.82 us (20%)
  local copies, waits for them, and re-layouts  1.68 us (4%)
    ppermute x18, starting transfers between devices, exchange(): return lax.ppermute(block, AXES, pairs)  20.3 us
    pallas_call x4, Pallas kernels, fold(): pl.pallas_call(functools.partial(fold_kernel, specs, bool(state), last),...  8.81 us
    ppermute x18, waiting for transfers between devices, exchange(): return lax.ppermute(block, AXES, pairs)  7.82 us
    unnamed x6, local copies, waits for them, and re-layouts  1.68 us
  transfers between devices with their start and end apart: 18, of which 6 were waited for; matrix products, arithmetic and copies ran while one was open for 0% of the time, Pallas kernels for 16%

profile of v2, /device:TPU:0, one launch (start us, length us, event | category | flops | bytes accessed | tf_op | source)
XLA Modules:
  0.0 38.9 jit_solution(8455887479942067320)
XLA Ops:
  0.0 0.0 copy-start.1
  0.0 0.8 %copy-done.1 = bf16[64,512]{1,0:T(8,128)(2,1)S(1)} copy-done((bf16[64,512]{1,0:T(8,128)(2,1)S(1)}, bf16[64,512]{1,0:T(8,128)(2,1)}, u32[]{:S(2)}) %copy-start.1) | copy-done | bytes 65560
  0.8 0.0 copy-start.2
  0.8 0.8 %copy-done.2 = bf16[64,512]{1,0:T(8,128)(2,1)S(1)} copy-done((bf16[64,512]{1,0:T(8,128)(2,1)S(1)}, bf16[64,512]{1,0:T(8,128)(2,1)}, u32[]{:S(2)}) %copy-start.2) | copy-done | bytes 65560
  1.7 0.0 copy-start
  1.7 3.0 %collective-permute-start = (bf16[64,1024]{1,0:T(8,128)(2,1)S(1)}, bf16[64,1024]{1,0:T(8,128)(2,1)S(1)}, u32[]{:S(2)}, u32[]{:S(2)}) collective-permute-start(bf16[64,1024]{1,0:T(8,128)(2,1)S(1)} %pack.1.refs_0_), channel_id=1, source_target_pairs={{0,4},{1,3},{2,6},{3,1},{4,0},{5,7},{6,2},{7,5},{8,12},{9,11},{10,... | collective-permute-start | bytes 393224 | tf_op jit(solution)/shard_map/ppermute | solution.py:189
  4.7 3.6 %collective-permute-start.8 = (bf16[64,1024]{1,0:T(8,128)(2,1)S(1)}, bf16[64,1024]{1,0:T(8,128)(2,1)S(1)}, u32[]{:S(2)}, u32[]{:S(2)}) collective-permute-start(bf16[64,1024]{1,0:T(8,128)(2,1)S(1)} %pack.1.refs_0_), channel_id=1, source_target_pairs={{0,24},{1,25},{2,26},{3,27},{4,28},{5,29},{6,30},{7,31},{8,16},{9,... | collective-permute-start | bytes 393224 | tf_op jit(solution)/shard_map/ppermute | solution.py:189
  8.3 0.0 collective-permute-done.refs_1_
  8.4 1.6 %collective-permute-start.1 = (bf16[128,1024]{1,0:T(8,128)(2,1)S(1)}, bf16[128,1024]{1,0:T(8,128)(2,1)S(1)}, u32[]{:S(2)}, u32[]{:S(2)}) collective-permute-start(bf16[128,1024]{1,0:T(8,128)(2,1)S(1)} %join.9.refs_0_), channel_id=1, source_target_pairs={{0,2},{1,5},{2,0},{3,7},{4,6},{5,1},{6,4},{7,3},{8,10},{9,13},{10,... | collective-permute-start | bytes 786440 | tf_op jit(solution)/shard_map/ppermute | solution.py:189
  9.9 1.4 %collective-permute-start.4 = (bf16[128,1024]{1,0:T(8,128)(2,1)S(1)}, bf16[128,1024]{1,0:T(8,128)(2,1)S(1)}, u32[]{:S(2)}, u32[]{:S(2)}) collective-permute-start(bf16[128,1024]{1,0:T(8,128)(2,1)S(1)} %join.9.refs_0_), channel_id=1, source_target_pairs={{0,8},{1,9},{2,10},{3,11},{4,12},{5,13},{6,14},{7,15},{8,0},{9,1},... | collective-permute-start | bytes 786440 | tf_op jit(solution)/shard_map/ppermute | solution.py:189
  11.4 0.3 collective-permute-done.8.refs_0_
  11.7 1.6 %collective-permute-start.9 = (bf16[64,1024]{1,0:T(8,128)(2,1)S(1)}, bf16[64,1024]{1,0:T(8,128)(2,1)S(1)}, u32[]{:S(2)}, u32[]{:S(2)}) collective-permute-start(bf16[64,1024]{1,0:T(8,128)(2,1)S(1)} %join.13.refs_0_), channel_id=1, source_target_pairs={{0,4},{1,3},{2,6},{3,1},{4,0},{5,7},{6,2},{7,5},{8,12},{9,11},{10,... | collective-permute-start | bytes 393224 | tf_op jit(solution)/shard_map/ppermute | solution.py:189
  13.4 2.3 %collective-permute-start.13 = (bf16[64,1024]{1,0:T(8,128)(2,1)S(1)}, bf16[64,1024]{1,0:T(8,128)(2,1)S(1)}, u32[]{:S(2)}, u32[]{:S(2)}) collective-permute-start(bf16[64,1024]{1,0:T(8,128)(2,1)S(1)} %join.13.refs_0_), channel_id=1, source_target_pairs={{0,8},{1,9},{2,10},{3,11},{4,12},{5,13},{6,14},{7,15},{8,0},{9,1},... | collective-permute-start | bytes 393224 | tf_op jit(solution)/shard_map/ppermute | solution.py:189
  15.7 0.5 %collective-permute-done.1.refs_1_ = bf16[128,1024]{1,0:T(8,128)(2,1)S(1)} collective-permute-done((bf16[128,1024]{1,0:T(8,128)(2,1)S(1)}, bf16[128,1024]{1,0:T(8,128)(2,1)S(1)}, u32[]{:S(2)}, u32[]{:S(2)}) %collective-permute-start.1) | collective-permute-done | bytes 262176 | tf_op jit(solution)/shard_map/ppermute | solution.py:189
  16.2 0.5 %collective-permute-start.5 = (bf16[128,1024]{1,0:T(8,128)(2,1)S(1)}, bf16[128,1024]{1,0:T(8,128)(2,1)S(1)}, u32[]{:S(2)}, u32[]{:S(2)}) collective-permute-start(bf16[128,1024]{1,0:T(8,128)(2,1)S(1)} %collective-permute-done.1.refs_1_), channel_id=1, source_target_pairs={{0,8},{1,9},{2,10},{3,11},{4,12},{5,13},{6,14},{7,15},{8,0},{9,1},... | collective-permute-start | bytes 786440 | tf_op jit(solution)/shard_map/ppermute | solution.py:189
  16.7 0.0 collective-permute-start.2
  16.7 0.1 collective-permute-done.9.refs_1_
  16.8 2.5 %collective-permute-start.10 = (bf16[128,1024]{1,0:T(8,128)(2,1)S(1)}, bf16[128,1024]{1,0:T(8,128)(2,1)S(1)}, u32[]{:S(2)}, u32[]{:S(2)}) collective-permute-start(bf16[128,1024]{1,0:T(8,128)(2,1)S(1)} %join.14.refs_2_), channel_id=1, source_target_pairs={{0,2},{1,5},{2,0},{3,7},{4,6},{5,1},{6,4},{7,3},{8,10},{9,13},{10,... | collective-permute-start | bytes 786440 | tf_op jit(solution)/shard_map/ppermute | solution.py:189
  19.3 2.7 %collective-permute-done.13.refs_0_ = bf16[64,1024]{1,0:T(8,128)(2,1)S(1)} collective-permute-done((bf16[64,1024]{1,0:T(8,128)(2,1)S(1)}, bf16[64,1024]{1,0:T(8,128)(2,1)S(1)}, u32[]{:S(2)}, u32[]{:S(2)}) %collective-permute-start.13) | collective-permute-done | bytes 131104 | tf_op jit(solution)/shard_map/ppermute | solution.py:189
  22.0 0.0 collective-permute-start.3
  22.0 0.0 collective-permute-done.4.refs_0_
  22.0 1.4 %collective-permute-start.14 = (bf16[64,1024]{1,0:T(8,128)(2,1)S(1)}, bf16[64,1024]{1,0:T(8,128)(2,1)S(1)}, u32[]{:S(2)}, u32[]{:S(2)}) collective-permute-start(bf16[64,1024]{1,0:T(8,128)(2,1)S(1)} %join.15.refs_0_), channel_id=1, source_target_pairs={{0,4},{1,3},{2,6},{3,1},{4,0},{5,7},{6,2},{7,5},{8,12},{9,11},{10,... | collective-permute-start | bytes 393224 | tf_op jit(solution)/shard_map/ppermute | solution.py:189
  23.4 0.0 copy-done
  23.4 0.9 %fold2n.1 = (f32[4,512,128]{2,1,0:T(8,128)S(1)}, f32[4,512,256]{2,1,0:T(8,128)S(1)}) custom-call(bf16[64,4096]{1,0:T(8,128)(2,1)S(1)} %copy-done, bf16[128,1024]{1,0:T(8,128)(2,1)S(1)} %join.9.refs_0_, bf16[128,1024]{1,0:T(8,128)(2,1)S(1)} %collective-permute-done.1.refs_1_), custom_call_target="tpu_custom_call" | custom-call | tf_op jit(solution)/shard_map/fold2n/pallas_call | solution.py:171
  24.4 2.7 %collective-permute-done.14.refs_1_ = bf16[64,1024]{1,0:T(8,128)(2,1)S(1)} collective-permute-done((bf16[64,1024]{1,0:T(8,128)(2,1)S(1)}, bf16[64,1024]{1,0:T(8,128)(2,1)S(1)}, u32[]{:S(2)}, u32[]{:S(2)}) %collective-permute-start.14) | collective-permute-done | bytes 131104 | tf_op jit(solution)/shard_map/ppermute | solution.py:189
  27.1 0.0 collective-permute-start.6
  27.1 0.0 collective-permute-done.5.refs_5_
  27.1 0.5 %collective-permute-start.7 = (bf16[128,1024]{1,0:T(8,128)(2,1)S(1)}, bf16[128,1024]{1,0:T(8,128)(2,1)S(1)}, u32[]{:S(2)}, u32[]{:S(2)}) collective-permute-start(bf16[128,1024]{1,0:T(8,128)(2,1)S(1)} %collective-permute-done.5.refs_5_), channel_id=1, source_target_pairs={{0,1},{1,0},{2,3},{3,2},{4,5},{5,4},{6,7},{7,6},{8,9},{9,8},{10,11... | collective-permute-start | bytes 786440 | tf_op jit(solution)/shard_map/ppermute | solution.py:189
  27.6 0.0 collective-permute-done.2.refs_2_
  27.6 0.1 collective-permute-start.11
  27.6 0.0 collective-permute-done.10.refs_3_
  27.6 0.4 %collective-permute-start.12 = (bf16[128,1024]{1,0:T(8,128)(2,1)S(1)}, bf16[128,1024]{1,0:T(8,128)(2,1)S(1)}, u32[]{:S(2)}, u32[]{:S(2)}) collective-permute-start(bf16[128,1024]{1,0:T(8,128)(2,1)S(1)} %collective-permute-done.10.refs_3_), channel_id=1, source_target_pairs={{0,1},{1,0},{2,3},{3,2},{4,5},{5,4},{6,7},{7,6},{8,9},{9,8},{10,11... | collective-permute-start | bytes 786440 | tf_op jit(solution)/shard_map/ppermute | solution.py:189
  28.1 0.0 collective-permute-done.3.refs_3_
  28.1 0.6 %collective-permute-start.15 = (bf16[128,1024]{1,0:T(8,128)(2,1)S(1)}, bf16[128,1024]{1,0:T(8,128)(2,1)S(1)}, u32[]{:S(2)}, u32[]{:S(2)}) collective-permute-start(bf16[128,1024]{1,0:T(8,128)(2,1)S(1)} %join.16.refs_2_), channel_id=1, source_target_pairs={{0,2},{1,5},{2,0},{3,7},{4,6},{5,1},{6,4},{7,3},{8,10},{9,13},{10,... | collective-permute-start | bytes 786440 | tf_op jit(solution)/shard_map/ppermute | solution.py:189
  28.7 0.0 collective-permute-done.6.refs_6_
  28.7 0.7 %collective-permute-start.16 = (bf16[128,1024]{1,0:T(8,128)(2,1)S(1)}, bf16[128,1024]{1,0:T(8,128)(2,1)S(1)}, u32[]{:S(2)}, u32[]{:S(2)}) collective-permute-start(bf16[128,1024]{1,0:T(8,128)(2,1)S(1)} %join.16.refs_2_), channel_id=1, source_target_pairs={{0,1},{1,0},{2,3},{3,2},{4,5},{5,4},{6,7},{7,6},{8,9},{9,8},{10,11... | collective-permute-start | bytes 786440 | tf_op jit(solution)/shard_map/ppermute | solution.py:189
  29.3 0.0 collective-permute-done.7.refs_7_
  29.3 3.0 %fold6s.1 = (f32[4,512,128]{2,1,0:T(8,128)S(1)}, f32[4,512,256]{2,1,0:T(8,128)S(1)}) custom-call(bf16[64,4096]{1,0:T(8,128)(2,1)S(1)} %copy-done, f32[4,512,128]{2,1,0:T(8,128)S(1)} %get-tuple-element.11.refs_0_.refs_2_, f32[4,512,256]{2,1,0:T(8,128)S(1)} %get-tuple-element.12.refs_1_, ...), custom_call_target="tpu_custom_call", output_to_operand_aliasing={{0}: (1, {}), {1}: (2, {})} | custom-call | tf_op jit(solution)/shard_map/fold6s/pallas_call | solution.py:171
  32.3 0.0 collective-permute-done.11.refs_4_
  32.4 0.0 collective-permute-done.12.refs_5_
  32.4 2.3 %fold4s.1 = (f32[4,512,128]{2,1,0:T(8,128)S(1)}, f32[4,512,256]{2,1,0:T(8,128)S(1)}) custom-call(bf16[64,4096]{1,0:T(8,128)(2,1)S(1)} %copy-done, f32[4,512,128]{2,1,0:T(8,128)S(1)} %get-tuple-element.13.refs_0_, f32[4,512,256]{2,1,0:T(8,128)S(1)} %get-tuple-element.14.refs_1_, ...), custom_call_target="tpu_custom_call", output_to_operand_aliasing={{0}: (1, {}), {1}: (2, {})} | custom-call | tf_op jit(solution)/shard_map/fold4s/pallas_call | solution.py:171
  34.7 0.0 collective-permute-done.15.refs_0_.refs_3_
  34.7 0.1 collective-permute-start.17
  34.8 0.0 collective-permute-done.16.refs_4_
  34.8 1.5 %collective-permute-done.17.refs_5_ = bf16[128,1024]{1,0:T(8,128)(2,1)S(1)} collective-permute-done((bf16[128,1024]{1,0:T(8,128)(2,1)S(1)}, bf16[128,1024]{1,0:T(8,128)(2,1)S(1)}, u32[]{:S(2)}, u32[]{:S(2)}) %collective-permute-start.17) | collective-permute-done | bytes 262176 | tf_op jit(solution)/shard_map/ppermute | solution.py:189
  36.3 2.6 %fold4sl.1 = bf16[64,4096]{1,0:T(8,128)(2,1)} custom-call(bf16[64,4096]{1,0:T(8,128)(2,1)S(1)} %copy-done, f32[4,512,128]{2,1,0:T(8,128)S(1)} %get-tuple-element.15.refs_1_.refs_0_, f32[4,512,256]{2,1,0:T(8,128)S(1)} %get-tuple-element.16.refs_1_, bf16[128,1024]{1,0:T(8,128)(2,1)S(1)} %join.16.refs_2_, ...), custom_call_target="tpu_custom_call" | custom-call | tf_op jit(solution)/shard_map/fold4sl/pallas_call | solution.py:171
  (10 shorter events, 0.2 us)
Async XLA Ops:
  0.0 0.8 %copy-start.1 = (bf16[64,512]{1,0:T(8,128)(2,1)S(1)}, bf16[64,512]{1,0:T(8,128)(2,1)}, u32[]{:S(2)}) copy-start(bf16[64,512]{1,0:T(8,128)(2,1)} %keys_ref.1) | copy-start | bytes 196612
  0.8 0.8 %copy-start.2 = (bf16[64,512]{1,0:T(8,128)(2,1)S(1)}, bf16[64,512]{1,0:T(8,128)(2,1)}, u32[]{:S(2)}) copy-start(bf16[64,512]{1,0:T(8,128)(2,1)} %values_ref.1) | copy-start | bytes 196612
  1.7 21.8 %copy-start = (bf16[64,4096]{1,0:T(8,128)(2,1)S(1)}, bf16[64,4096]{1,0:T(8,128)(2,1)}, u32[]{:S(2)}) copy-start(bf16[64,4096]{1,0:T(8,128)(2,1)} %q_ref.7) | copy-start | bytes 1572868
  1.7 6.6 %collective-permute-start = (bf16[64,1024]{1,0:T(8,128)(2,1)S(1)}, bf16[64,1024]{1,0:T(8,128)(2,1)S(1)}, u32[]{:S(2)}, u32[]{:S(2)}) collective-permute-start(bf16[64,1024]{1,0:T(8,128)(2,1)S(1)} %pack.1.refs_0_), channel_id=1, source_target_pairs={{0,4},{1,3},{2,6},{3,1},{4,0},{5,7},{6,2},{7,5},{8,12},{9,11},{10,... | collective-permute-start | bytes 393224 | tf_op jit(solution)/shard_map/ppermute | solution.py:189
  4.7 7.0 %collective-permute-start.8 = (bf16[64,1024]{1,0:T(8,128)(2,1)S(1)}, bf16[64,1024]{1,0:T(8,128)(2,1)S(1)}, u32[]{:S(2)}, u32[]{:S(2)}) collective-permute-start(bf16[64,1024]{1,0:T(8,128)(2,1)S(1)} %pack.1.refs_0_), channel_id=1, source_target_pairs={{0,24},{1,25},{2,26},{3,27},{4,28},{5,29},{6,30},{7,31},{8,16},{9,... | collective-permute-start | bytes 393224 | tf_op jit(solution)/shard_map/ppermute | solution.py:189
  8.4 7.8 %collective-permute-start.1 = (bf16[128,1024]{1,0:T(8,128)(2,1)S(1)}, bf16[128,1024]{1,0:T(8,128)(2,1)S(1)}, u32[]{:S(2)}, u32[]{:S(2)}) collective-permute-start(bf16[128,1024]{1,0:T(8,128)(2,1)S(1)} %join.9.refs_0_), channel_id=1, source_target_pairs={{0,2},{1,5},{2,0},{3,7},{4,6},{5,1},{6,4},{7,3},{8,10},{9,13},{10,... | collective-permute-start | bytes 786440 | tf_op jit(solution)/shard_map/ppermute | solution.py:189
  9.9 12.1 %collective-permute-start.4 = (bf16[128,1024]{1,0:T(8,128)(2,1)S(1)}, bf16[128,1024]{1,0:T(8,128)(2,1)S(1)}, u32[]{:S(2)}, u32[]{:S(2)}) collective-permute-start(bf16[128,1024]{1,0:T(8,128)(2,1)S(1)} %join.9.refs_0_), channel_id=1, source_target_pairs={{0,8},{1,9},{2,10},{3,11},{4,12},{5,13},{6,14},{7,15},{8,0},{9,1},... | collective-permute-start | bytes 786440 | tf_op jit(solution)/shard_map/ppermute | solution.py:189
  11.7 5.0 %collective-permute-start.9 = (bf16[64,1024]{1,0:T(8,128)(2,1)S(1)}, bf16[64,1024]{1,0:T(8,128)(2,1)S(1)}, u32[]{:S(2)}, u32[]{:S(2)}) collective-permute-start(bf16[64,1024]{1,0:T(8,128)(2,1)S(1)} %join.13.refs_0_), channel_id=1, source_target_pairs={{0,4},{1,3},{2,6},{3,1},{4,0},{5,7},{6,2},{7,5},{8,12},{9,11},{10,... | collective-permute-start | bytes 393224 | tf_op jit(solution)/shard_map/ppermute | solution.py:189
  13.4 8.6 %collective-permute-start.13 = (bf16[64,1024]{1,0:T(8,128)(2,1)S(1)}, bf16[64,1024]{1,0:T(8,128)(2,1)S(1)}, u32[]{:S(2)}, u32[]{:S(2)}) collective-permute-start(bf16[64,1024]{1,0:T(8,128)(2,1)S(1)} %join.13.refs_0_), channel_id=1, source_target_pairs={{0,8},{1,9},{2,10},{3,11},{4,12},{5,13},{6,14},{7,15},{8,0},{9,1},... | collective-permute-start | bytes 393224 | tf_op jit(solution)/shard_map/ppermute | solution.py:189
  16.2 10.9 %collective-permute-start.5 = (bf16[128,1024]{1,0:T(8,128)(2,1)S(1)}, bf16[128,1024]{1,0:T(8,128)(2,1)S(1)}, u32[]{:S(2)}, u32[]{:S(2)}) collective-permute-start(bf16[128,1024]{1,0:T(8,128)(2,1)S(1)} %collective-permute-done.1.refs_1_), channel_id=1, source_target_pairs={{0,8},{1,9},{2,10},{3,11},{4,12},{5,13},{6,14},{7,15},{8,0},{9,1},... | collective-permute-start | bytes 786440 | tf_op jit(solution)/shard_map/ppermute | solution.py:189
  16.7 10.9 %collective-permute-start.2 = (bf16[128,1024]{1,0:T(8,128)(2,1)S(1)}, bf16[128,1024]{1,0:T(8,128)(2,1)S(1)}, u32[]{:S(2)}, u32[]{:S(2)}) collective-permute-start(bf16[128,1024]{1,0:T(8,128)(2,1)S(1)} %join.9.refs_0_), channel_id=1, source_target_pairs={{0,1},{1,0},{2,3},{3,2},{4,5},{5,4},{6,7},{7,6},{8,9},{9,8},{10,11... | collective-permute-start | bytes 786440 | tf_op jit(solution)/shard_map/ppermute | solution.py:189
  16.8 10.9 %collective-permute-start.10 = (bf16[128,1024]{1,0:T(8,128)(2,1)S(1)}, bf16[128,1024]{1,0:T(8,128)(2,1)S(1)}, u32[]{:S(2)}, u32[]{:S(2)}) collective-permute-start(bf16[128,1024]{1,0:T(8,128)(2,1)S(1)} %join.14.refs_2_), channel_id=1, source_target_pairs={{0,2},{1,5},{2,0},{3,7},{4,6},{5,1},{6,4},{7,3},{8,10},{9,13},{10,... | collective-permute-start | bytes 786440 | tf_op jit(solution)/shard_map/ppermute | solution.py:189
  22.0 6.1 %collective-permute-start.3 = (bf16[128,1024]{1,0:T(8,128)(2,1)S(1)}, bf16[128,1024]{1,0:T(8,128)(2,1)S(1)}, u32[]{:S(2)}, u32[]{:S(2)}) collective-permute-start(bf16[128,1024]{1,0:T(8,128)(2,1)S(1)} %collective-permute-done.1.refs_1_), channel_id=1, source_target_pairs={{0,1},{1,0},{2,3},{3,2},{4,5},{5,4},{6,7},{7,6},{8,9},{9,8},{10,11... | collective-permute-start | bytes 786440 | tf_op jit(solution)/shard_map/ppermute | solution.py:189
  22.0 5.0 %collective-permute-start.14 = (bf16[64,1024]{1,0:T(8,128)(2,1)S(1)}, bf16[64,1024]{1,0:T(8,128)(2,1)S(1)}, u32[]{:S(2)}, u32[]{:S(2)}) collective-permute-start(bf16[64,1024]{1,0:T(8,128)(2,1)S(1)} %join.15.refs_0_), channel_id=1, source_target_pairs={{0,4},{1,3},{2,6},{3,1},{4,0},{5,7},{6,2},{7,5},{8,12},{9,11},{10,... | collective-permute-start | bytes 393224 | tf_op jit(solution)/shard_map/ppermute | solution.py:189
  27.1 1.6 %collective-permute-start.6 = (bf16[128,1024]{1,0:T(8,128)(2,1)S(1)}, bf16[128,1024]{1,0:T(8,128)(2,1)S(1)}, u32[]{:S(2)}, u32[]{:S(2)}) collective-permute-start(bf16[128,1024]{1,0:T(8,128)(2,1)S(1)} %join.10.refs_4_), channel_id=1, source_target_pairs={{0,1},{1,0},{2,3},{3,2},{4,5},{5,4},{6,7},{7,6},{8,9},{9,8},{10,11... | collective-permute-start | bytes 786440 | tf_op jit(solution)/shard_map/ppermute | solution.py:189
  27.1 2.3 %collective-permute-start.7 = (bf16[128,1024]{1,0:T(8,128)(2,1)S(1)}, bf16[128,1024]{1,0:T(8,128)(2,1)S(1)}, u32[]{:S(2)}, u32[]{:S(2)}) collective-permute-start(bf16[128,1024]{1,0:T(8,128)(2,1)S(1)} %collective-permute-done.5.refs_5_), channel_id=1, source_target_pairs={{0,1},{1,0},{2,3},{3,2},{4,5},{5,4},{6,7},{7,6},{8,9},{9,8},{10,11... | collective-permute-start | bytes 786440 | tf_op jit(solution)/shard_map/ppermute | solution.py:189
  27.6 4.8 %collective-permute-start.11 = (bf16[128,1024]{1,0:T(8,128)(2,1)S(1)}, bf16[128,1024]{1,0:T(8,128)(2,1)S(1)}, u32[]{:S(2)}, u32[]{:S(2)}) collective-permute-start(bf16[128,1024]{1,0:T(8,128)(2,1)S(1)} %join.14.refs_2_), channel_id=1, source_target_pairs={{0,1},{1,0},{2,3},{3,2},{4,5},{5,4},{6,7},{7,6},{8,9},{9,8},{10,11... | collective-permute-start | bytes 786440 | tf_op jit(solution)/shard_map/ppermute | solution.py:189
  27.6 4.7 %collective-permute-start.12 = (bf16[128,1024]{1,0:T(8,128)(2,1)S(1)}, bf16[128,1024]{1,0:T(8,128)(2,1)S(1)}, u32[]{:S(2)}, u32[]{:S(2)}) collective-permute-start(bf16[128,1024]{1,0:T(8,128)(2,1)S(1)} %collective-permute-done.10.refs_3_), channel_id=1, source_target_pairs={{0,1},{1,0},{2,3},{3,2},{4,5},{5,4},{6,7},{7,6},{8,9},{9,8},{10,11... | collective-permute-start | bytes 786440 | tf_op jit(solution)/shard_map/ppermute | solution.py:189
  28.1 6.6 %collective-permute-start.15 = (bf16[128,1024]{1,0:T(8,128)(2,1)S(1)}, bf16[128,1024]{1,0:T(8,128)(2,1)S(1)}, u32[]{:S(2)}, u32[]{:S(2)}) collective-permute-start(bf16[128,1024]{1,0:T(8,128)(2,1)S(1)} %join.16.refs_2_), channel_id=1, source_target_pairs={{0,2},{1,5},{2,0},{3,7},{4,6},{5,1},{6,4},{7,3},{8,10},{9,13},{10,... | collective-permute-start | bytes 786440 | tf_op jit(solution)/shard_map/ppermute | solution.py:189
  28.7 6.1 %collective-permute-start.16 = (bf16[128,1024]{1,0:T(8,128)(2,1)S(1)}, bf16[128,1024]{1,0:T(8,128)(2,1)S(1)}, u32[]{:S(2)}, u32[]{:S(2)}) collective-permute-start(bf16[128,1024]{1,0:T(8,128)(2,1)S(1)} %join.16.refs_2_), channel_id=1, source_target_pairs={{0,1},{1,0},{2,3},{3,2},{4,5},{5,4},{6,7},{7,6},{8,9},{9,8},{10,11... | collective-permute-start | bytes 786440 | tf_op jit(solution)/shard_map/ppermute | solution.py:189
  34.7 1.6 %collective-permute-start.17 = (bf16[128,1024]{1,0:T(8,128)(2,1)S(1)}, bf16[128,1024]{1,0:T(8,128)(2,1)S(1)}, u32[]{:S(2)}, u32[]{:S(2)}) collective-permute-start(bf16[128,1024]{1,0:T(8,128)(2,1)S(1)} %join.17), channel_id=1, source_target_pairs={{0,1},{1,0},{2,3},{3,2},{4,5},{5,4},{6,7},{7,6},{8,9},{9,8},{10,11... | collective-permute-start | bytes 786440 | tf_op jit(solution)/shard_map/ppermute | solution.py:189

commit v3 on v2

--- a/solution.py
+++ b/solution.py
@@ -80,6 +80,8 @@
 
 
 def weigh(scores, spec, marks):
+    if spec not in marks:
+        return scores
     if spec[0] == "step":
         return scores + marks[spec]
     rows, cols = marks[spec].shape
@@ -146,13 +148,29 @@
     state_refs, refs = (refs[:2], refs[2:]) if has_state else ((), refs)
     blocks, outs = (refs[:-1], refs[-1:]) if last else (refs[:-2], refs[-2:])
     marks = make_marks(specs, q_ref.shape[0])
-    for h in range(KVH):
-        state = tuple(ref[h] for ref in state_refs) or None
-        peak, summed = fold_head(h, q_ref, blocks, specs, marks, state)
-        if last:
-            finish_head(h, summed, outs[0])
-        else:
-            outs[0][h], outs[1][h] = peak, summed
+    steps = {spec for spec in specs if spec[0] == "step"}
+    single = len(steps) == 1 and steps == set(specs) and has_state
+
+    def work():
+        for h in range(KVH):
+            state = tuple(ref[h] for ref in state_refs) or None
+            peak, summed = fold_head(h, q_ref, blocks, specs, {} if single else marks, state)
+            if last:
+                finish_head(h, summed, outs[0])
+            else:
+                outs[0][h], outs[1][h] = peak, summed
+
+    if not single:
+        work()
+        return
+    valid = marks[specs[0]] == 0.0
+    pl.when(valid)(work)
+    if last:
+
+        @pl.when(jnp.logical_not(valid))
+        def _():
+            for h in range(KVH):
+                finish_head(h, state_refs[1][h], outs[0])
 
 
 def state_shapes(rows):
@@ -196,23 +214,25 @@
         return mine, exchange(mine, 2, 4)
 
     group3 = hold(exchange(own, 3 * PLANE, 3 * PLANE), 3)
-    group2 = hold(exchange(group3, PLANE, PLANE), 1)
-    mine_own, second_own = ("own", "mine"), ("own", "second")
-    mine_swapped, second_swapped = ("own", "mine_"), ("own", "second_")
+    group2 = hold(exchange(group3, PLANE, PLANE))
+    of_own = (("own", "mine"),), (("own", "second"),), (("own", "mine_"),), (("own", "second_"),)
+    of_1, of_2, of_3 = ((("step", step),) for step in (1, 2, 3))
+
     mine0, second0 = double(own)
-    swapped0 = (swap(mine0), swap(second0))
-    state = fold(queries, (), [(mine0, (mine_own,)), (second0, (second_own,))])
+    swapped0 = [swap(mine0), swap(second0)]
+    state = fold(queries, (), list(zip([mine0, second0], of_own)))
     early = (state[0],)
-    mine1, second1 = hold(exchange(mine0, PLANE, PLANE), 1), exchange(second0, PLANE, PLANE)
-    swapped1 = (swap(mine1), swap(second1))
-    state = fold(queries, state, [(swapped0[0], (mine_swapped,)), (swapped0[1], (second_swapped,)), (mine1, (("step", 1),)), (second1, (("step", 1),)), (swapped1[0], (("step", 1),)), (swapped1[1], (("step", 1),))])
+
+    mine1, second1 = hold(exchange(mine0, PLANE, PLANE)), exchange(second0, PLANE, PLANE)
     mine3, second3 = double(group3)
+    from1 = [mine1, second1, swap(mine1), swap(second1)]
+    from3 = [mine3, second3, swap(mine3), swap(second3)]
+    state = fold(queries, state, list(zip(swapped0 + from1, [*of_own[2:], *[of_1] * 4])))
+    state = fold(queries, state, list(zip(from3, [of_3] * 4)))
+
     mine2, second2 = double(group2, after=early)
-    swapped3 = (swap(mine3), swap(second3))
-    state = fold(queries, state, [(mine3, (("step", 3),)), (second3, (("step", 3),)), (swapped3[0], (("step", 3),)), (swapped3[1], (("step", 3),))])
-    swapped2 = (swap(mine2), swap(hold(second2, after=(state[0],))))
-    pieces = [(mine2, (("step", 2),)), (second2, (("step", 2),)), (swapped2[0], (("step", 2),)), (swapped2[1], (("step", 2),))]
-    return fold(queries, state, pieces, last=True)
+    pieces = [mine2, second2, swap(mine2), swap(hold(second2, after=(state[0],)))]
+    return fold(queries, state, [(piece, of_2) for piece in pieces], last=True)
 
 
 def span_kernel(pos_ref, q_ref, peak_in, sum_in, kv_ref, peak_ref, sum_ref):

time: 39.1 us -> 38 us (0.972)
  the two profiles are of different devices: /device:TPU:0 before, /device:TPU:25 now
where the time goes in v3:
time: 38 us; the launch traced here: 37.8 us
  starting transfers between devices  15.8 us (42%)
  waiting for transfers between devices  11.1 us (29%)
  Pallas kernels  8.97 us (24%)
  local copies, waits for them, and re-layouts  1.68 us (4%)
    ppermute x18, starting transfers between devices, exchange(): return lax.ppermute(block, AXES, pairs)  15.8 us
    ppermute x18, waiting for transfers between devices, exchange(): return lax.ppermute(block, AXES, pairs)  11.1 us
    pallas_call x4, Pallas kernels, fold(): pl.pallas_call(functools.partial(fold_kernel, specs, bool(state), last),...  8.81 us
    unnamed x6, local copies, waits for them, and re-layouts  1.68 us
  transfers between devices with their start and end apart: 18, of which 6 were waited for; matrix products, arithmetic and copies ran while one was open for 0% of the time, Pallas kernels for 17%

profile of v3, /device:TPU:25, one launch (start us, length us, event | category | flops | bytes accessed | tf_op | source)
XLA Modules:
  0.0 37.8 jit_solution(1099850609817706616)
XLA Ops:
  0.0 0.0 copy-start.1
  0.0 0.8 %copy-done.1 = bf16[64,512]{1,0:T(8,128)(2,1)S(1)} copy-done((bf16[64,512]{1,0:T(8,128)(2,1)S(1)}, bf16[64,512]{1,0:T(8,128)(2,1)}, u32[]{:S(2)}) %copy-start.1) | copy-done | bytes 65560
  0.8 0.0 copy-start.2
  0.8 0.8 %copy-done.2 = bf16[64,512]{1,0:T(8,128)(2,1)S(1)} copy-done((bf16[64,512]{1,0:T(8,128)(2,1)S(1)}, bf16[64,512]{1,0:T(8,128)(2,1)}, u32[]{:S(2)}) %copy-start.2) | copy-done | bytes 65560
  1.7 0.0 copy-start
  1.7 1.3 %collective-permute-start = (bf16[64,1024]{1,0:T(8,128)(2,1)S(1)}, bf16[64,1024]{1,0:T(8,128)(2,1)S(1)}, u32[]{:S(2)}, u32[]{:S(2)}) collective-permute-start(bf16[64,1024]{1,0:T(8,128)(2,1)S(1)} %pack.1.refs_0_), channel_id=1, source_target_pairs={{0,4},{1,3},{2,6},{3,1},{4,0},{5,7},{6,2},{7,5},{8,12},{9,11},{10,... | collective-permute-start | bytes 393224 | tf_op jit(solution)/shard_map/ppermute | solution.py:207
  3.0 0.0 collective-permute-start.8
  3.0 2.9 %collective-permute-done.refs_1_ = bf16[64,1024]{1,0:T(8,128)(2,1)S(1)} collective-permute-done((bf16[64,1024]{1,0:T(8,128)(2,1)S(1)}, bf16[64,1024]{1,0:T(8,128)(2,1)S(1)}, u32[]{:S(2)}, u32[]{:S(2)}) %collective-permute-start) | collective-permute-done | bytes 131104 | tf_op jit(solution)/shard_map/ppermute | solution.py:207
  5.9 1.3 %collective-permute-start.1 = (bf16[128,1024]{1,0:T(8,128)(2,1)S(1)}, bf16[128,1024]{1,0:T(8,128)(2,1)S(1)}, u32[]{:S(2)}, u32[]{:S(2)}) collective-permute-start(bf16[128,1024]{1,0:T(8,128)(2,1)S(1)} %join.9.refs_0_), channel_id=1, source_target_pairs={{0,2},{1,5},{2,0},{3,7},{4,6},{5,1},{6,4},{7,3},{8,10},{9,13},{10,... | collective-permute-start | bytes 786440 | tf_op jit(solution)/shard_map/ppermute | solution.py:207
  7.2 0.2 collective-permute-start.4
  7.4 1.6 %collective-permute-done.8.refs_0_ = bf16[64,1024]{1,0:T(8,128)(2,1)S(1)} collective-permute-done((bf16[64,1024]{1,0:T(8,128)(2,1)S(1)}, bf16[64,1024]{1,0:T(8,128)(2,1)S(1)}, u32[]{:S(2)}, u32[]{:S(2)}) %collective-permute-start.8) | collective-permute-done | bytes 131104 | tf_op jit(solution)/shard_map/ppermute | solution.py:207
  9.0 0.1 collective-permute-start.9
  9.1 0.9 %collective-permute-start.13 = (bf16[64,1024]{1,0:T(8,128)(2,1)S(1)}, bf16[64,1024]{1,0:T(8,128)(2,1)S(1)}, u32[]{:S(2)}, u32[]{:S(2)}) collective-permute-start(bf16[64,1024]{1,0:T(8,128)(2,1)S(1)} %join.13.refs_0_), channel_id=1, source_target_pairs={{0,8},{1,9},{2,10},{3,11},{4,12},{5,13},{6,14},{7,15},{8,0},{9,1},... | collective-permute-start | bytes 393224 | tf_op jit(solution)/shard_map/ppermute | solution.py:207
  10.0 1.5 %collective-permute-done.1.refs_1_ = bf16[128,1024]{1,0:T(8,128)(2,1)S(1)} collective-permute-done((bf16[128,1024]{1,0:T(8,128)(2,1)S(1)}, bf16[128,1024]{1,0:T(8,128)(2,1)S(1)}, u32[]{:S(2)}, u32[]{:S(2)}) %collective-permute-start.1) | collective-permute-done | bytes 262176 | tf_op jit(solution)/shard_map/ppermute | solution.py:207
  11.5 0.2 collective-permute-start.5
  11.7 4.1 %collective-permute-start.2 = (bf16[128,1024]{1,0:T(8,128)(2,1)S(1)}, bf16[128,1024]{1,0:T(8,128)(2,1)S(1)}, u32[]{:S(2)}, u32[]{:S(2)}) collective-permute-start(bf16[128,1024]{1,0:T(8,128)(2,1)S(1)} %join.9.refs_0_), channel_id=1, source_target_pairs={{0,1},{1,0},{2,3},{3,2},{4,5},{5,4},{6,7},{7,6},{8,9},{9,8},{10,11... | collective-permute-start | bytes 786440 | tf_op jit(solution)/shard_map/ppermute | solution.py:207
  15.7 0.0 collective-permute-done.9.refs_1_
  15.8 0.4 %collective-permute-start.10 = (bf16[128,1024]{1,0:T(8,128)(2,1)S(1)}, bf16[128,1024]{1,0:T(8,128)(2,1)S(1)}, u32[]{:S(2)}, u32[]{:S(2)}) collective-permute-start(bf16[128,1024]{1,0:T(8,128)(2,1)S(1)} %join.14.refs_2_), channel_id=1, source_target_pairs={{0,2},{1,5},{2,0},{3,7},{4,6},{5,1},{6,4},{7,3},{8,10},{9,13},{10,... | collective-permute-start | bytes 786440 | tf_op jit(solution)/shard_map/ppermute | solution.py:207
  16.2 1.0 %collective-permute-done.13.refs_0_ = bf16[64,1024]{1,0:T(8,128)(2,1)S(1)} collective-permute-done((bf16[64,1024]{1,0:T(8,128)(2,1)S(1)}, bf16[64,1024]{1,0:T(8,128)(2,1)S(1)}, u32[]{:S(2)}, u32[]{:S(2)}) %collective-permute-start.13) | collective-permute-done | bytes 131104 | tf_op jit(solution)/shard_map/ppermute | solution.py:207
  17.2 3.9 %collective-permute-start.3 = (bf16[128,1024]{1,0:T(8,128)(2,1)S(1)}, bf16[128,1024]{1,0:T(8,128)(2,1)S(1)}, u32[]{:S(2)}, u32[]{:S(2)}) collective-permute-start(bf16[128,1024]{1,0:T(8,128)(2,1)S(1)} %collective-permute-done.1.refs_1_), channel_id=1, source_target_pairs={{0,1},{1,0},{2,3},{3,2},{4,5},{5,4},{6,7},{7,6},{8,9},{9,8},{10,11... | collective-permute-start | bytes 786440 | tf_op jit(solution)/shard_map/ppermute | solution.py:207
  21.1 0.0 collective-permute-done.4.refs_0_
  21.1 0.3 collective-permute-start.14
  21.4 0.0 copy-done
  21.4 0.9 %fold2n.1 = (f32[4,512,128]{2,1,0:T(8,128)S(1)}, f32[4,512,256]{2,1,0:T(8,128)S(1)}) custom-call(bf16[64,4096]{1,0:T(8,128)(2,1)S(1)} %copy-done, bf16[128,1024]{1,0:T(8,128)(2,1)S(1)} %join.9.refs_0_, bf16[128,1024]{1,0:T(8,128)(2,1)S(1)} %collective-permute-done.1.refs_1_), custom_call_target="tpu_custom_call" | custom-call | tf_op jit(solution)/shard_map/fold2n/pallas_call | solution.py:189
  22.3 3.0 %collective-permute-done.14.refs_1_ = bf16[64,1024]{1,0:T(8,128)(2,1)S(1)} collective-permute-done((bf16[64,1024]{1,0:T(8,128)(2,1)S(1)}, bf16[64,1024]{1,0:T(8,128)(2,1)S(1)}, u32[]{:S(2)}, u32[]{:S(2)}) %collective-permute-start.14) | collective-permute-done | bytes 131104 | tf_op jit(solution)/shard_map/ppermute | solution.py:207
  25.3 0.9 %collective-permute-start.6 = (bf16[128,1024]{1,0:T(8,128)(2,1)S(1)}, bf16[128,1024]{1,0:T(8,128)(2,1)S(1)}, u32[]{:S(2)}, u32[]{:S(2)}) collective-permute-start(bf16[128,1024]{1,0:T(8,128)(2,1)S(1)} %join.10.refs_4_), channel_id=1, source_target_pairs={{0,1},{1,0},{2,3},{3,2},{4,5},{5,4},{6,7},{7,6},{8,9},{9,8},{10,11... | collective-permute-start | bytes 786440 | tf_op jit(solution)/shard_map/ppermute | solution.py:207
  26.2 0.0 collective-permute-done.5.refs_5_
  26.2 0.0 collective-permute-start.7
  26.2 0.0 collective-permute-done.2.refs_2_
  26.2 0.5 %collective-permute-start.11 = (bf16[128,1024]{1,0:T(8,128)(2,1)S(1)}, bf16[128,1024]{1,0:T(8,128)(2,1)S(1)}, u32[]{:S(2)}, u32[]{:S(2)}) collective-permute-start(bf16[128,1024]{1,0:T(8,128)(2,1)S(1)} %join.14.refs_2_), channel_id=1, source_target_pairs={{0,1},{1,0},{2,3},{3,2},{4,5},{5,4},{6,7},{7,6},{8,9},{9,8},{10,11... | collective-permute-start | bytes 786440 | tf_op jit(solution)/shard_map/ppermute | solution.py:207
  26.7 0.0 collective-permute-done.10.refs_3_
  26.7 0.1 collective-permute-start.12
  26.8 0.0 collective-permute-done.3.refs_3_
  26.8 1.3 %collective-permute-start.15 = (bf16[128,1024]{1,0:T(8,128)(2,1)S(1)}, bf16[128,1024]{1,0:T(8,128)(2,1)S(1)}, u32[]{:S(2)}, u32[]{:S(2)}) collective-permute-start(bf16[128,1024]{1,0:T(8,128)(2,1)S(1)} %join.16.refs_2_), channel_id=1, source_target_pairs={{0,2},{1,5},{2,0},{3,7},{4,6},{5,1},{6,4},{7,3},{8,10},{9,13},{10,... | collective-permute-start | bytes 786440 | tf_op jit(solution)/shard_map/ppermute | solution.py:207
  28.1 0.0 collective-permute-done.6.refs_6_
  28.1 0.0 collective-permute-start.16
  28.1 0.0 collective-permute-done.7.refs_7_
  28.1 3.0 %fold6s.1 = (f32[4,512,128]{2,1,0:T(8,128)S(1)}, f32[4,512,256]{2,1,0:T(8,128)S(1)}) custom-call(bf16[64,4096]{1,0:T(8,128)(2,1)S(1)} %copy-done, f32[4,512,128]{2,1,0:T(8,128)S(1)} %get-tuple-element.11.refs_0_.refs_2_, f32[4,512,256]{2,1,0:T(8,128)S(1)} %get-tuple-element.12.refs_1_, ...), custom_call_target="tpu_custom_call", output_to_operand_aliasing={{0}: (1, {}), {1}: (2, {})} | custom-call | tf_op jit(solution)/shard_map/fold6s/pallas_call | solution.py:189
  31.1 0.0 collective-permute-done.11.refs_4_
  31.1 0.0 collective-permute-done.12.refs_5_
  31.1 2.3 %fold4s.1 = (f32[4,512,128]{2,1,0:T(8,128)S(1)}, f32[4,512,256]{2,1,0:T(8,128)S(1)}) custom-call(bf16[64,4096]{1,0:T(8,128)(2,1)S(1)} %copy-done, f32[4,512,128]{2,1,0:T(8,128)S(1)} %get-tuple-element.13.refs_0_, f32[4,512,256]{2,1,0:T(8,128)S(1)} %get-tuple-element.14.refs_1_, ...), custom_call_target="tpu_custom_call", output_to_operand_aliasing={{0}: (1, {}), {1}: (2, {})} | custom-call | tf_op jit(solution)/shard_map/fold4s/pallas_call | solution.py:189
  33.4 0.0 collective-permute-done.15.refs_0_.refs_3_
  33.5 0.6 %collective-permute-start.17 = (bf16[128,1024]{1,0:T(8,128)(2,1)S(1)}, bf16[128,1024]{1,0:T(8,128)(2,1)S(1)}, u32[]{:S(2)}, u32[]{:S(2)}) collective-permute-start(bf16[128,1024]{1,0:T(8,128)(2,1)S(1)} %join.17), channel_id=1, source_target_pairs={{0,1},{1,0},{2,3},{3,2},{4,5},{5,4},{6,7},{7,6},{8,9},{9,8},{10,11... | collective-permute-start | bytes 786440 | tf_op jit(solution)/shard_map/ppermute | solution.py:207
  34.0 0.0 collective-permute-done.16.refs_4_
  34.0 1.2 %collective-permute-done.17.refs_5_ = bf16[128,1024]{1,0:T(8,128)(2,1)S(1)} collective-permute-done((bf16[128,1024]{1,0:T(8,128)(2,1)S(1)}, bf16[128,1024]{1,0:T(8,128)(2,1)S(1)}, u32[]{:S(2)}, u32[]{:S(2)}) %collective-permute-start.17) | collective-permute-done | bytes 262176 | tf_op jit(solution)/shard_map/ppermute | solution.py:207
  35.2 2.6 %fold4sl.1 = bf16[64,4096]{1,0:T(8,128)(2,1)} custom-call(bf16[64,4096]{1,0:T(8,128)(2,1)S(1)} %copy-done, f32[4,512,128]{2,1,0:T(8,128)S(1)} %get-tuple-element.15.refs_1_.refs_0_, f32[4,512,256]{2,1,0:T(8,128)S(1)} %get-tuple-element.16.refs_1_, bf16[128,1024]{1,0:T(8,128)(2,1)S(1)} %join.16.refs_2_, ...), custom_call_target="tpu_custom_call" | custom-call | tf_op jit(solution)/shard_map/fold4sl/pallas_call | solution.py:189
  (10 shorter events, 0.2 us)
Async XLA Ops:
  0.0 0.8 %copy-start.1 = (bf16[64,512]{1,0:T(8,128)(2,1)S(1)}, bf16[64,512]{1,0:T(8,128)(2,1)}, u32[]{:S(2)}) copy-start(bf16[64,512]{1,0:T(8,128)(2,1)} %keys_ref.1) | copy-start | bytes 196612
  0.8 0.8 %copy-start.2 = (bf16[64,512]{1,0:T(8,128)(2,1)S(1)}, bf16[64,512]{1,0:T(8,128)(2,1)}, u32[]{:S(2)}) copy-start(bf16[64,512]{1,0:T(8,128)(2,1)} %values_ref.1) | copy-start | bytes 196612
  1.7 19.7 %copy-start = (bf16[64,4096]{1,0:T(8,128)(2,1)S(1)}, bf16[64,4096]{1,0:T(8,128)(2,1)}, u32[]{:S(2)}) copy-start(bf16[64,4096]{1,0:T(8,128)(2,1)} %q_ref.7) | copy-start | bytes 1572868
  1.7 4.2 %collective-permute-start = (bf16[64,1024]{1,0:T(8,128)(2,1)S(1)}, bf16[64,1024]{1,0:T(8,128)(2,1)S(1)}, u32[]{:S(2)}, u32[]{:S(2)}) collective-permute-start(bf16[64,1024]{1,0:T(8,128)(2,1)S(1)} %pack.1.refs_0_), channel_id=1, source_target_pairs={{0,4},{1,3},{2,6},{3,1},{4,0},{5,7},{6,2},{7,5},{8,12},{9,11},{10,... | collective-permute-start | bytes 393224 | tf_op jit(solution)/shard_map/ppermute | solution.py:207
  3.0 6.0 %collective-permute-start.8 = (bf16[64,1024]{1,0:T(8,128)(2,1)S(1)}, bf16[64,1024]{1,0:T(8,128)(2,1)S(1)}, u32[]{:S(2)}, u32[]{:S(2)}) collective-permute-start(bf16[64,1024]{1,0:T(8,128)(2,1)S(1)} %pack.1.refs_0_), channel_id=1, source_target_pairs={{0,24},{1,25},{2,26},{3,27},{4,28},{5,29},{6,30},{7,31},{8,16},{9,... | collective-permute-start | bytes 393224 | tf_op jit(solution)/shard_map/ppermute | solution.py:207
  5.9 5.6 %collective-permute-start.1 = (bf16[128,1024]{1,0:T(8,128)(2,1)S(1)}, bf16[128,1024]{1,0:T(8,128)(2,1)S(1)}, u32[]{:S(2)}, u32[]{:S(2)}) collective-permute-start(bf16[128,1024]{1,0:T(8,128)(2,1)S(1)} %join.9.refs_0_), channel_id=1, source_target_pairs={{0,2},{1,5},{2,0},{3,7},{4,6},{5,1},{6,4},{7,3},{8,10},{9,13},{10,... | collective-permute-start | bytes 786440 | tf_op jit(solution)/shard_map/ppermute | solution.py:207
  7.2 13.9 %collective-permute-start.4 = (bf16[128,1024]{1,0:T(8,128)(2,1)S(1)}, bf16[128,1024]{1,0:T(8,128)(2,1)S(1)}, u32[]{:S(2)}, u32[]{:S(2)}) collective-permute-start(bf16[128,1024]{1,0:T(8,128)(2,1)S(1)} %join.9.refs_0_), channel_id=1, source_target_pairs={{0,8},{1,9},{2,10},{3,11},{4,12},{5,13},{6,14},{7,15},{8,0},{9,1},... | collective-permute-start | bytes 786440 | tf_op jit(solution)/shard_map/ppermute | solution.py:207
  9.0 6.7 %collective-permute-start.9 = (bf16[64,1024]{1,0:T(8,128)(2,1)S(1)}, bf16[64,1024]{1,0:T(8,128)(2,1)S(1)}, u32[]{:S(2)}, u32[]{:S(2)}) collective-permute-start(bf16[64,1024]{1,0:T(8,128)(2,1)S(1)} %join.13.refs_0_), channel_id=1, source_target_pairs={{0,4},{1,3},{2,6},{3,1},{4,0},{5,7},{6,2},{7,5},{8,12},{9,11},{10,... | collective-permute-start | bytes 393224 | tf_op jit(solution)/shard_map/ppermute | solution.py:207
  9.1 8.1 %collective-permute-start.13 = (bf16[64,1024]{1,0:T(8,128)(2,1)S(1)}, bf16[64,1024]{1,0:T(8,128)(2,1)S(1)}, u32[]{:S(2)}, u32[]{:S(2)}) collective-permute-start(bf16[64,1024]{1,0:T(8,128)(2,1)S(1)} %join.13.refs_0_), channel_id=1, source_target_pairs={{0,8},{1,9},{2,10},{3,11},{4,12},{5,13},{6,14},{7,15},{8,0},{9,1},... | collective-permute-start | bytes 393224 | tf_op jit(solution)/shard_map/ppermute | solution.py:207
  11.5 14.6 %collective-permute-start.5 = (bf16[128,1024]{1,0:T(8,128)(2,1)S(1)}, bf16[128,1024]{1,0:T(8,128)(2,1)S(1)}, u32[]{:S(2)}, u32[]{:S(2)}) collective-permute-start(bf16[128,1024]{1,0:T(8,128)(2,1)S(1)} %collective-permute-done.1.refs_1_), channel_id=1, source_target_pairs={{0,8},{1,9},{2,10},{3,11},{4,12},{5,13},{6,14},{7,15},{8,0},{9,1},... | collective-permute-start | bytes 786440 | tf_op jit(solution)/shard_map/ppermute | solution.py:207
  11.7 14.5 %collective-permute-start.2 = (bf16[128,1024]{1,0:T(8,128)(2,1)S(1)}, bf16[128,1024]{1,0:T(8,128)(2,1)S(1)}, u32[]{:S(2)}, u32[]{:S(2)}) collective-permute-start(bf16[128,1024]{1,0:T(8,128)(2,1)S(1)} %join.9.refs_0_), channel_id=1, source_target_pairs={{0,1},{1,0},{2,3},{3,2},{4,5},{5,4},{6,7},{7,6},{8,9},{9,8},{10,11... | collective-permute-start | bytes 786440 | tf_op jit(solution)/shard_map/ppermute | solution.py:207
  15.8 10.9 %collective-permute-start.10 = (bf16[128,1024]{1,0:T(8,128)(2,1)S(1)}, bf16[128,1024]{1,0:T(8,128)(2,1)S(1)}, u32[]{:S(2)}, u32[]{:S(2)}) collective-permute-start(bf16[128,1024]{1,0:T(8,128)(2,1)S(1)} %join.14.refs_2_), channel_id=1, source_target_pairs={{0,2},{1,5},{2,0},{3,7},{4,6},{5,1},{6,4},{7,3},{8,10},{9,13},{10,... | collective-permute-start | bytes 786440 | tf_op jit(solution)/shard_map/ppermute | solution.py:207
  17.2 9.6 %collective-permute-start.3 = (bf16[128,1024]{1,0:T(8,128)(2,1)S(1)}, bf16[128,1024]{1,0:T(8,128)(2,1)S(1)}, u32[]{:S(2)}, u32[]{:S(2)}) collective-permute-start(bf16[128,1024]{1,0:T(8,128)(2,1)S(1)} %collective-permute-done.1.refs_1_), channel_id=1, source_target_pairs={{0,1},{1,0},{2,3},{3,2},{4,5},{5,4},{6,7},{7,6},{8,9},{9,8},{10,11... | collective-permute-start | bytes 786440 | tf_op jit(solution)/shard_map/ppermute | solution.py:207
  21.1 4.2 %collective-permute-start.14 = (bf16[64,1024]{1,0:T(8,128)(2,1)S(1)}, bf16[64,1024]{1,0:T(8,128)(2,1)S(1)}, u32[]{:S(2)}, u32[]{:S(2)}) collective-permute-start(bf16[64,1024]{1,0:T(8,128)(2,1)S(1)} %join.15.refs_0_), channel_id=1, source_target_pairs={{0,4},{1,3},{2,6},{3,1},{4,0},{5,7},{6,2},{7,5},{8,12},{9,11},{10,... | collective-permute-start | bytes 393224 | tf_op jit(solution)/shard_map/ppermute | solution.py:207
  25.3 2.8 %collective-permute-start.6 = (bf16[128,1024]{1,0:T(8,128)(2,1)S(1)}, bf16[128,1024]{1,0:T(8,128)(2,1)S(1)}, u32[]{:S(2)}, u32[]{:S(2)}) collective-permute-start(bf16[128,1024]{1,0:T(8,128)(2,1)S(1)} %join.10.refs_4_), channel_id=1, source_target_pairs={{0,1},{1,0},{2,3},{3,2},{4,5},{5,4},{6,7},{7,6},{8,9},{9,8},{10,11... | collective-permute-start | bytes 786440 | tf_op jit(solution)/shard_map/ppermute | solution.py:207
  26.2 1.9 %collective-permute-start.7 = (bf16[128,1024]{1,0:T(8,128)(2,1)S(1)}, bf16[128,1024]{1,0:T(8,128)(2,1)S(1)}, u32[]{:S(2)}, u32[]{:S(2)}) collective-permute-start(bf16[128,1024]{1,0:T(8,128)(2,1)S(1)} %collective-permute-done.5.refs_5_), channel_id=1, source_target_pairs={{0,1},{1,0},{2,3},{3,2},{4,5},{5,4},{6,7},{7,6},{8,9},{9,8},{10,11... | collective-permute-start | bytes 786440 | tf_op jit(solution)/shard_map/ppermute | solution.py:207
  26.2 4.9 %collective-permute-start.11 = (bf16[128,1024]{1,0:T(8,128)(2,1)S(1)}, bf16[128,1024]{1,0:T(8,128)(2,1)S(1)}, u32[]{:S(2)}, u32[]{:S(2)}) collective-permute-start(bf16[128,1024]{1,0:T(8,128)(2,1)S(1)} %join.14.refs_2_), channel_id=1, source_target_pairs={{0,1},{1,0},{2,3},{3,2},{4,5},{5,4},{6,7},{7,6},{8,9},{9,8},{10,11... | collective-permute-start | bytes 786440 | tf_op jit(solution)/shard_map/ppermute | solution.py:207
  26.7 4.4 %collective-permute-start.12 = (bf16[128,1024]{1,0:T(8,128)(2,1)S(1)}, bf16[128,1024]{1,0:T(8,128)(2,1)S(1)}, u32[]{:S(2)}, u32[]{:S(2)}) collective-permute-start(bf16[128,1024]{1,0:T(8,128)(2,1)S(1)} %collective-permute-done.10.refs_3_), channel_id=1, source_target_pairs={{0,1},{1,0},{2,3},{3,2},{4,5},{5,4},{6,7},{7,6},{8,9},{9,8},{10,11... | collective-permute-start | bytes 786440 | tf_op jit(solution)/shard_map/ppermute | solution.py:207
  26.8 6.7 %collective-permute-start.15 = (bf16[128,1024]{1,0:T(8,128)(2,1)S(1)}, bf16[128,1024]{1,0:T(8,128)(2,1)S(1)}, u32[]{:S(2)}, u32[]{:S(2)}) collective-permute-start(bf16[128,1024]{1,0:T(8,128)(2,1)S(1)} %join.16.refs_2_), channel_id=1, source_target_pairs={{0,2},{1,5},{2,0},{3,7},{4,6},{5,1},{6,4},{7,3},{8,10},{9,13},{10,... | collective-permute-start | bytes 786440 | tf_op jit(solution)/shard_map/ppermute | solution.py:207
  28.1 6.0 %collective-permute-start.16 = (bf16[128,1024]{1,0:T(8,128)(2,1)S(1)}, bf16[128,1024]{1,0:T(8,128)(2,1)S(1)}, u32[]{:S(2)}, u32[]{:S(2)}) collective-permute-start(bf16[128,1024]{1,0:T(8,128)(2,1)S(1)} %join.16.refs_2_), channel_id=1, source_target_pairs={{0,1},{1,0},{2,3},{3,2},{4,5},{5,4},{6,7},{7,6},{8,9},{9,8},{10,11... | collective-permute-start | bytes 786440 | tf_op jit(solution)/shard_map/ppermute | solution.py:207
  33.5 1.7 %collective-permute-start.17 = (bf16[128,1024]{1,0:T(8,128)(2,1)S(1)}, bf16[128,1024]{1,0:T(8,128)(2,1)S(1)}, u32[]{:S(2)}, u32[]{:S(2)}) collective-permute-start(bf16[128,1024]{1,0:T(8,128)(2,1)S(1)} %join.17), channel_id=1, source_target_pairs={{0,1},{1,0},{2,3},{3,2},{4,5},{5,4},{6,7},{7,6},{8,9},{9,8},{10,11... | collective-permute-start | bytes 786440 | tf_op jit(solution)/shard_map/ppermute | solution.py:207

commit v4 on v3

--- a/solution.py
+++ b/solution.py
@@ -125,7 +125,7 @@
     peak = jnp.broadcast_to(peak, parts[0].shape)
     if state is not None:
         peak = jnp.maximum(peak, state[0])
-    weights = [jnp.exp2((part - peak) * FACTOR).astype(jnp.bfloat16) for part in parts]
+    weights = [jnp.exp2(((part - peak) * FACTOR).astype(jnp.bfloat16)) for part in parts]
     summed = lax.dot_general(
         jnp.concatenate(weights, axis=1), values, (((1,), (0,)), ((), ())),
         preferred_element_type=jnp.float32,

time: 38 us -> 38.1 us (level)
  no operation moved by 1% of the time
where the time goes in v4:
time: 38.1 us; the launch traced here: 37.9 us
  starting transfers between devices  15.8 us (41%)
  waiting for transfers between devices  11.1 us (29%)
  Pallas kernels  9.06 us (24%)
  local copies, waits for them, and re-layouts  1.68 us (4%)
    ppermute x18, starting transfers between devices, exchange(): return lax.ppermute(block, AXES, pairs)  15.8 us
    ppermute x18, waiting for transfers between devices, exchange(): return lax.ppermute(block, AXES, pairs)  11.1 us
    pallas_call x4, Pallas kernels, fold(): pl.pallas_call(functools.partial(fold_kernel, specs, bool(state), last),...  8.9 us
    unnamed x6, local copies, waits for them, and re-layouts  1.68 us
  transfers between devices with their start and end apart: 18, of which 6 were waited for; matrix products, arithmetic and copies ran while one was open for 0% of the time, Pallas kernels for 17%

profile of v4, /device:TPU:25, one launch (start us, length us, event | category | flops | bytes accessed | tf_op | source)
XLA Modules:
  0.0 37.9 jit_solution(12278331265912952954)
XLA Ops:
  0.0 0.0 copy-start.1
  0.0 0.8 %copy-done.1 = bf16[64,512]{1,0:T(8,128)(2,1)S(1)} copy-done((bf16[64,512]{1,0:T(8,128)(2,1)S(1)}, bf16[64,512]{1,0:T(8,128)(2,1)}, u32[]{:S(2)}) %copy-start.1) | copy-done | bytes 65560
  0.8 0.0 copy-start.2
  0.8 0.8 %copy-done.2 = bf16[64,512]{1,0:T(8,128)(2,1)S(1)} copy-done((bf16[64,512]{1,0:T(8,128)(2,1)S(1)}, bf16[64,512]{1,0:T(8,128)(2,1)}, u32[]{:S(2)}) %copy-start.2) | copy-done | bytes 65560
  1.7 0.0 copy-start
  1.7 1.3 %collective-permute-start = (bf16[64,1024]{1,0:T(8,128)(2,1)S(1)}, bf16[64,1024]{1,0:T(8,128)(2,1)S(1)}, u32[]{:S(2)}, u32[]{:S(2)}) collective-permute-start(bf16[64,1024]{1,0:T(8,128)(2,1)S(1)} %pack.1.refs_0_), channel_id=1, source_target_pairs={{0,4},{1,3},{2,6},{3,1},{4,0},{5,7},{6,2},{7,5},{8,12},{9,11},{10,... | collective-permute-start | bytes 393224 | tf_op jit(solution)/shard_map/ppermute | solution.py:207
  3.0 0.0 collective-permute-start.8
  3.0 2.9 %collective-permute-done.refs_1_ = bf16[64,1024]{1,0:T(8,128)(2,1)S(1)} collective-permute-done((bf16[64,1024]{1,0:T(8,128)(2,1)S(1)}, bf16[64,1024]{1,0:T(8,128)(2,1)S(1)}, u32[]{:S(2)}, u32[]{:S(2)}) %collective-permute-start) | collective-permute-done | bytes 131104 | tf_op jit(solution)/shard_map/ppermute | solution.py:207
  5.9 1.3 %collective-permute-start.1 = (bf16[128,1024]{1,0:T(8,128)(2,1)S(1)}, bf16[128,1024]{1,0:T(8,128)(2,1)S(1)}, u32[]{:S(2)}, u32[]{:S(2)}) collective-permute-start(bf16[128,1024]{1,0:T(8,128)(2,1)S(1)} %join.9.refs_0_), channel_id=1, source_target_pairs={{0,2},{1,5},{2,0},{3,7},{4,6},{5,1},{6,4},{7,3},{8,10},{9,13},{10,... | collective-permute-start | bytes 786440 | tf_op jit(solution)/shard_map/ppermute | solution.py:207
  7.2 0.2 collective-permute-start.4
  7.4 1.6 %collective-permute-done.8.refs_0_ = bf16[64,1024]{1,0:T(8,128)(2,1)S(1)} collective-permute-done((bf16[64,1024]{1,0:T(8,128)(2,1)S(1)}, bf16[64,1024]{1,0:T(8,128)(2,1)S(1)}, u32[]{:S(2)}, u32[]{:S(2)}) %collective-permute-start.8) | collective-permute-done | bytes 131104 | tf_op jit(solution)/shard_map/ppermute | solution.py:207
  9.0 0.1 collective-permute-start.9
  9.1 0.9 %collective-permute-start.13 = (bf16[64,1024]{1,0:T(8,128)(2,1)S(1)}, bf16[64,1024]{1,0:T(8,128)(2,1)S(1)}, u32[]{:S(2)}, u32[]{:S(2)}) collective-permute-start(bf16[64,1024]{1,0:T(8,128)(2,1)S(1)} %join.13.refs_0_), channel_id=1, source_target_pairs={{0,8},{1,9},{2,10},{3,11},{4,12},{5,13},{6,14},{7,15},{8,0},{9,1},... | collective-permute-start | bytes 393224 | tf_op jit(solution)/shard_map/ppermute | solution.py:207
  10.0 1.5 %collective-permute-done.1.refs_1_ = bf16[128,1024]{1,0:T(8,128)(2,1)S(1)} collective-permute-done((bf16[128,1024]{1,0:T(8,128)(2,1)S(1)}, bf16[128,1024]{1,0:T(8,128)(2,1)S(1)}, u32[]{:S(2)}, u32[]{:S(2)}) %collective-permute-start.1) | collective-permute-done | bytes 262176 | tf_op jit(solution)/shard_map/ppermute | solution.py:207
  11.5 0.2 collective-permute-start.5
  11.7 4.1 %collective-permute-start.2 = (bf16[128,1024]{1,0:T(8,128)(2,1)S(1)}, bf16[128,1024]{1,0:T(8,128)(2,1)S(1)}, u32[]{:S(2)}, u32[]{:S(2)}) collective-permute-start(bf16[128,1024]{1,0:T(8,128)(2,1)S(1)} %join.9.refs_0_), channel_id=1, source_target_pairs={{0,1},{1,0},{2,3},{3,2},{4,5},{5,4},{6,7},{7,6},{8,9},{9,8},{10,11... | collective-permute-start | bytes 786440 | tf_op jit(solution)/shard_map/ppermute | solution.py:207
  15.7 0.0 collective-permute-done.9.refs_1_
  15.8 0.4 %collective-permute-start.10 = (bf16[128,1024]{1,0:T(8,128)(2,1)S(1)}, bf16[128,1024]{1,0:T(8,128)(2,1)S(1)}, u32[]{:S(2)}, u32[]{:S(2)}) collective-permute-start(bf16[128,1024]{1,0:T(8,128)(2,1)S(1)} %join.14.refs_2_), channel_id=1, source_target_pairs={{0,2},{1,5},{2,0},{3,7},{4,6},{5,1},{6,4},{7,3},{8,10},{9,13},{10,... | collective-permute-start | bytes 786440 | tf_op jit(solution)/shard_map/ppermute | solution.py:207
  16.2 1.0 %collective-permute-done.13.refs_0_ = bf16[64,1024]{1,0:T(8,128)(2,1)S(1)} collective-permute-done((bf16[64,1024]{1,0:T(8,128)(2,1)S(1)}, bf16[64,1024]{1,0:T(8,128)(2,1)S(1)}, u32[]{:S(2)}, u32[]{:S(2)}) %collective-permute-start.13) | collective-permute-done | bytes 131104 | tf_op jit(solution)/shard_map/ppermute | solution.py:207
  17.2 3.9 %collective-permute-start.3 = (bf16[128,1024]{1,0:T(8,128)(2,1)S(1)}, bf16[128,1024]{1,0:T(8,128)(2,1)S(1)}, u32[]{:S(2)}, u32[]{:S(2)}) collective-permute-start(bf16[128,1024]{1,0:T(8,128)(2,1)S(1)} %collective-permute-done.1.refs_1_), channel_id=1, source_target_pairs={{0,1},{1,0},{2,3},{3,2},{4,5},{5,4},{6,7},{7,6},{8,9},{9,8},{10,11... | collective-permute-start | bytes 786440 | tf_op jit(solution)/shard_map/ppermute | solution.py:207
  21.1 0.0 collective-permute-done.4.refs_0_
  21.1 0.3 collective-permute-start.14
  21.4 0.0 copy-done
  21.4 0.9 %fold2n.1 = (f32[4,512,128]{2,1,0:T(8,128)S(1)}, f32[4,512,256]{2,1,0:T(8,128)S(1)}) custom-call(bf16[64,4096]{1,0:T(8,128)(2,1)S(1)} %copy-done, bf16[128,1024]{1,0:T(8,128)(2,1)S(1)} %join.9.refs_0_, bf16[128,1024]{1,0:T(8,128)(2,1)S(1)} %collective-permute-done.1.refs_1_), custom_call_target="tpu_custom_call" | custom-call | tf_op jit(solution)/shard_map/fold2n/pallas_call | solution.py:189
  22.3 3.0 %collective-permute-done.14.refs_1_ = bf16[64,1024]{1,0:T(8,128)(2,1)S(1)} collective-permute-done((bf16[64,1024]{1,0:T(8,128)(2,1)S(1)}, bf16[64,1024]{1,0:T(8,128)(2,1)S(1)}, u32[]{:S(2)}, u32[]{:S(2)}) %collective-permute-start.14) | collective-permute-done | bytes 131104 | tf_op jit(solution)/shard_map/ppermute | solution.py:207
  25.3 0.9 %collective-permute-start.6 = (bf16[128,1024]{1,0:T(8,128)(2,1)S(1)}, bf16[128,1024]{1,0:T(8,128)(2,1)S(1)}, u32[]{:S(2)}, u32[]{:S(2)}) collective-permute-start(bf16[128,1024]{1,0:T(8,128)(2,1)S(1)} %join.10.refs_4_), channel_id=1, source_target_pairs={{0,1},{1,0},{2,3},{3,2},{4,5},{5,4},{6,7},{7,6},{8,9},{9,8},{10,11... | collective-permute-start | bytes 786440 | tf_op jit(solution)/shard_map/ppermute | solution.py:207
  26.2 0.0 collective-permute-done.5.refs_5_
  26.2 0.0 collective-permute-start.7
  26.2 0.0 collective-permute-done.2.refs_2_
  26.2 0.5 %collective-permute-start.11 = (bf16[128,1024]{1,0:T(8,128)(2,1)S(1)}, bf16[128,1024]{1,0:T(8,128)(2,1)S(1)}, u32[]{:S(2)}, u32[]{:S(2)}) collective-permute-start(bf16[128,1024]{1,0:T(8,128)(2,1)S(1)} %join.14.refs_2_), channel_id=1, source_target_pairs={{0,1},{1,0},{2,3},{3,2},{4,5},{5,4},{6,7},{7,6},{8,9},{9,8},{10,11... | collective-permute-start | bytes 786440 | tf_op jit(solution)/shard_map/ppermute | solution.py:207
  26.7 0.0 collective-permute-done.10.refs_3_
  26.7 0.1 collective-permute-start.12
  26.8 0.0 collective-permute-done.3.refs_3_
  26.8 1.3 %collective-permute-start.15 = (bf16[128,1024]{1,0:T(8,128)(2,1)S(1)}, bf16[128,1024]{1,0:T(8,128)(2,1)S(1)}, u32[]{:S(2)}, u32[]{:S(2)}) collective-permute-start(bf16[128,1024]{1,0:T(8,128)(2,1)S(1)} %join.16.refs_2_), channel_id=1, source_target_pairs={{0,2},{1,5},{2,0},{3,7},{4,6},{5,1},{6,4},{7,3},{8,10},{9,13},{10,... | collective-permute-start | bytes 786440 | tf_op jit(solution)/shard_map/ppermute | solution.py:207
  28.1 0.0 collective-permute-done.6.refs_6_
  28.1 0.0 collective-permute-start.16
  28.1 0.0 collective-permute-done.7.refs_7_
  28.1 3.0 %fold6s.1 = (f32[4,512,128]{2,1,0:T(8,128)S(1)}, f32[4,512,256]{2,1,0:T(8,128)S(1)}) custom-call(bf16[64,4096]{1,0:T(8,128)(2,1)S(1)} %copy-done, f32[4,512,128]{2,1,0:T(8,128)S(1)} %get-tuple-element.11.refs_0_.refs_2_, f32[4,512,256]{2,1,0:T(8,128)S(1)} %get-tuple-element.12.refs_1_, ...), custom_call_target="tpu_custom_call", output_to_operand_aliasing={{0}: (1, {}), {1}: (2, {})} | custom-call | tf_op jit(solution)/shard_map/fold6s/pallas_call | solution.py:189
  31.1 0.0 collective-permute-done.11.refs_4_
  31.1 0.0 collective-permute-done.12.refs_5_
  31.1 2.3 %fold4s.1 = (f32[4,512,128]{2,1,0:T(8,128)S(1)}, f32[4,512,256]{2,1,0:T(8,128)S(1)}) custom-call(bf16[64,4096]{1,0:T(8,128)(2,1)S(1)} %copy-done, f32[4,512,128]{2,1,0:T(8,128)S(1)} %get-tuple-element.13.refs_0_, f32[4,512,256]{2,1,0:T(8,128)S(1)} %get-tuple-element.14.refs_1_, ...), custom_call_target="tpu_custom_call", output_to_operand_aliasing={{0}: (1, {}), {1}: (2, {})} | custom-call | tf_op jit(solution)/shard_map/fold4s/pallas_call | solution.py:189
  33.4 0.0 collective-permute-done.15.refs_0_.refs_3_
  33.5 0.6 %collective-permute-start.17 = (bf16[128,1024]{1,0:T(8,128)(2,1)S(1)}, bf16[128,1024]{1,0:T(8,128)(2,1)S(1)}, u32[]{:S(2)}, u32[]{:S(2)}) collective-permute-start(bf16[128,1024]{1,0:T(8,128)(2,1)S(1)} %join.17), channel_id=1, source_target_pairs={{0,1},{1,0},{2,3},{3,2},{4,5},{5,4},{6,7},{7,6},{8,9},{9,8},{10,11... | collective-permute-start | bytes 786440 | tf_op jit(solution)/shard_map/ppermute | solution.py:207
  34.0 0.0 collective-permute-done.16.refs_4_
  34.0 1.2 %collective-permute-done.17.refs_5_ = bf16[128,1024]{1,0:T(8,128)(2,1)S(1)} collective-permute-done((bf16[128,1024]{1,0:T(8,128)(2,1)S(1)}, bf16[128,1024]{1,0:T(8,128)(2,1)S(1)}, u32[]{:S(2)}, u32[]{:S(2)}) %collective-permute-start.17) | collective-permute-done | bytes 262176 | tf_op jit(solution)/shard_map/ppermute | solution.py:207
  35.2 2.7 %fold4sl.1 = bf16[64,4096]{1,0:T(8,128)(2,1)} custom-call(bf16[64,4096]{1,0:T(8,128)(2,1)S(1)} %copy-done, f32[4,512,128]{2,1,0:T(8,128)S(1)} %get-tuple-element.15.refs_1_.refs_0_, f32[4,512,256]{2,1,0:T(8,128)S(1)} %get-tuple-element.16.refs_1_, bf16[128,1024]{1,0:T(8,128)(2,1)S(1)} %join.16.refs_2_, ...), custom_call_target="tpu_custom_call" | custom-call | tf_op jit(solution)/shard_map/fold4sl/pallas_call | solution.py:189
  (10 shorter events, 0.2 us)
Async XLA Ops:
  0.0 0.8 %copy-start.1 = (bf16[64,512]{1,0:T(8,128)(2,1)S(1)}, bf16[64,512]{1,0:T(8,128)(2,1)}, u32[]{:S(2)}) copy-start(bf16[64,512]{1,0:T(8,128)(2,1)} %keys_ref.1) | copy-start | bytes 196612
  0.8 0.8 %copy-start.2 = (bf16[64,512]{1,0:T(8,128)(2,1)S(1)}, bf16[64,512]{1,0:T(8,128)(2,1)}, u32[]{:S(2)}) copy-start(bf16[64,512]{1,0:T(8,128)(2,1)} %values_ref.1) | copy-start | bytes 196612
  1.7 19.7 %copy-start = (bf16[64,4096]{1,0:T(8,128)(2,1)S(1)}, bf16[64,4096]{1,0:T(8,128)(2,1)}, u32[]{:S(2)}) copy-start(bf16[64,4096]{1,0:T(8,128)(2,1)} %q_ref.7) | copy-start | bytes 1572868
  1.7 4.2 %collective-permute-start = (bf16[64,1024]{1,0:T(8,128)(2,1)S(1)}, bf16[64,1024]{1,0:T(8,128)(2,1)S(1)}, u32[]{:S(2)}, u32[]{:S(2)}) collective-permute-start(bf16[64,1024]{1,0:T(8,128)(2,1)S(1)} %pack.1.refs_0_), channel_id=1, source_target_pairs={{0,4},{1,3},{2,6},{3,1},{4,0},{5,7},{6,2},{7,5},{8,12},{9,11},{10,... | collective-permute-start | bytes 393224 | tf_op jit(solution)/shard_map/ppermute | solution.py:207
  3.0 6.0 %collective-permute-start.8 = (bf16[64,1024]{1,0:T(8,128)(2,1)S(1)}, bf16[64,1024]{1,0:T(8,128)(2,1)S(1)}, u32[]{:S(2)}, u32[]{:S(2)}) collective-permute-start(bf16[64,1024]{1,0:T(8,128)(2,1)S(1)} %pack.1.refs_0_), channel_id=1, source_target_pairs={{0,24},{1,25},{2,26},{3,27},{4,28},{5,29},{6,30},{7,31},{8,16},{9,... | collective-permute-start | bytes 393224 | tf_op jit(solution)/shard_map/ppermute | solution.py:207
  5.9 5.6 %collective-permute-start.1 = (bf16[128,1024]{1,0:T(8,128)(2,1)S(1)}, bf16[128,1024]{1,0:T(8,128)(2,1)S(1)}, u32[]{:S(2)}, u32[]{:S(2)}) collective-permute-start(bf16[128,1024]{1,0:T(8,128)(2,1)S(1)} %join.9.refs_0_), channel_id=1, source_target_pairs={{0,2},{1,5},{2,0},{3,7},{4,6},{5,1},{6,4},{7,3},{8,10},{9,13},{10,... | collective-permute-start | bytes 786440 | tf_op jit(solution)/shard_map/ppermute | solution.py:207
  7.2 13.9 %collective-permute-start.4 = (bf16[128,1024]{1,0:T(8,128)(2,1)S(1)}, bf16[128,1024]{1,0:T(8,128)(2,1)S(1)}, u32[]{:S(2)}, u32[]{:S(2)}) collective-permute-start(bf16[128,1024]{1,0:T(8,128)(2,1)S(1)} %join.9.refs_0_), channel_id=1, source_target_pairs={{0,8},{1,9},{2,10},{3,11},{4,12},{5,13},{6,14},{7,15},{8,0},{9,1},... | collective-permute-start | bytes 786440 | tf_op jit(solution)/shard_map/ppermute | solution.py:207
  9.0 6.7 %collective-permute-start.9 = (bf16[64,1024]{1,0:T(8,128)(2,1)S(1)}, bf16[64,1024]{1,0:T(8,128)(2,1)S(1)}, u32[]{:S(2)}, u32[]{:S(2)}) collective-permute-start(bf16[64,1024]{1,0:T(8,128)(2,1)S(1)} %join.13.refs_0_), channel_id=1, source_target_pairs={{0,4},{1,3},{2,6},{3,1},{4,0},{5,7},{6,2},{7,5},{8,12},{9,11},{10,... | collective-permute-start | bytes 393224 | tf_op jit(solution)/shard_map/ppermute | solution.py:207
  9.1 8.1 %collective-permute-start.13 = (bf16[64,1024]{1,0:T(8,128)(2,1)S(1)}, bf16[64,1024]{1,0:T(8,128)(2,1)S(1)}, u32[]{:S(2)}, u32[]{:S(2)}) collective-permute-start(bf16[64,1024]{1,0:T(8,128)(2,1)S(1)} %join.13.refs_0_), channel_id=1, source_target_pairs={{0,8},{1,9},{2,10},{3,11},{4,12},{5,13},{6,14},{7,15},{8,0},{9,1},... | collective-permute-start | bytes 393224 | tf_op jit(solution)/shard_map/ppermute | solution.py:207
  11.5 14.6 %collective-permute-start.5 = (bf16[128,1024]{1,0:T(8,128)(2,1)S(1)}, bf16[128,1024]{1,0:T(8,128)(2,1)S(1)}, u32[]{:S(2)}, u32[]{:S(2)}) collective-permute-start(bf16[128,1024]{1,0:T(8,128)(2,1)S(1)} %collective-permute-done.1.refs_1_), channel_id=1, source_target_pairs={{0,8},{1,9},{2,10},{3,11},{4,12},{5,13},{6,14},{7,15},{8,0},{9,1},... | collective-permute-start | bytes 786440 | tf_op jit(solution)/shard_map/ppermute | solution.py:207
  11.7 14.5 %collective-permute-start.2 = (bf16[128,1024]{1,0:T(8,128)(2,1)S(1)}, bf16[128,1024]{1,0:T(8,128)(2,1)S(1)}, u32[]{:S(2)}, u32[]{:S(2)}) collective-permute-start(bf16[128,1024]{1,0:T(8,128)(2,1)S(1)} %join.9.refs_0_), channel_id=1, source_target_pairs={{0,1},{1,0},{2,3},{3,2},{4,5},{5,4},{6,7},{7,6},{8,9},{9,8},{10,11... | collective-permute-start | bytes 786440 | tf_op jit(solution)/shard_map/ppermute | solution.py:207
  15.8 10.9 %collective-permute-start.10 = (bf16[128,1024]{1,0:T(8,128)(2,1)S(1)}, bf16[128,1024]{1,0:T(8,128)(2,1)S(1)}, u32[]{:S(2)}, u32[]{:S(2)}) collective-permute-start(bf16[128,1024]{1,0:T(8,128)(2,1)S(1)} %join.14.refs_2_), channel_id=1, source_target_pairs={{0,2},{1,5},{2,0},{3,7},{4,6},{5,1},{6,4},{7,3},{8,10},{9,13},{10,... | collective-permute-start | bytes 786440 | tf_op jit(solution)/shard_map/ppermute | solution.py:207
  17.2 9.6 %collective-permute-start.3 = (bf16[128,1024]{1,0:T(8,128)(2,1)S(1)}, bf16[128,1024]{1,0:T(8,128)(2,1)S(1)}, u32[]{:S(2)}, u32[]{:S(2)}) collective-permute-start(bf16[128,1024]{1,0:T(8,128)(2,1)S(1)} %collective-permute-done.1.refs_1_), channel_id=1, source_target_pairs={{0,1},{1,0},{2,3},{3,2},{4,5},{5,4},{6,7},{7,6},{8,9},{9,8},{10,11... | collective-permute-start | bytes 786440 | tf_op jit(solution)/shard_map/ppermute | solution.py:207
  21.1 4.2 %collective-permute-start.14 = (bf16[64,1024]{1,0:T(8,128)(2,1)S(1)}, bf16[64,1024]{1,0:T(8,128)(2,1)S(1)}, u32[]{:S(2)}, u32[]{:S(2)}) collective-permute-start(bf16[64,1024]{1,0:T(8,128)(2,1)S(1)} %join.15.refs_0_), channel_id=1, source_target_pairs={{0,4},{1,3},{2,6},{3,1},{4,0},{5,7},{6,2},{7,5},{8,12},{9,11},{10,... | collective-permute-start | bytes 393224 | tf_op jit(solution)/shard_map/ppermute | solution.py:207
  25.3 2.8 %collective-permute-start.6 = (bf16[128,1024]{1,0:T(8,128)(2,1)S(1)}, bf16[128,1024]{1,0:T(8,128)(2,1)S(1)}, u32[]{:S(2)}, u32[]{:S(2)}) collective-permute-start(bf16[128,1024]{1,0:T(8,128)(2,1)S(1)} %join.10.refs_4_), channel_id=1, source_target_pairs={{0,1},{1,0},{2,3},{3,2},{4,5},{5,4},{6,7},{7,6},{8,9},{9,8},{10,11... | collective-permute-start | bytes 786440 | tf_op jit(solution)/shard_map/ppermute | solution.py:207
  26.2 1.9 %collective-permute-start.7 = (bf16[128,1024]{1,0:T(8,128)(2,1)S(1)}, bf16[128,1024]{1,0:T(8,128)(2,1)S(1)}, u32[]{:S(2)}, u32[]{:S(2)}) collective-permute-start(bf16[128,1024]{1,0:T(8,128)(2,1)S(1)} %collective-permute-done.5.refs_5_), channel_id=1, source_target_pairs={{0,1},{1,0},{2,3},{3,2},{4,5},{5,4},{6,7},{7,6},{8,9},{9,8},{10,11... | collective-permute-start | bytes 786440 | tf_op jit(solution)/shard_map/ppermute | solution.py:207
  26.2 4.9 %collective-permute-start.11 = (bf16[128,1024]{1,0:T(8,128)(2,1)S(1)}, bf16[128,1024]{1,0:T(8,128)(2,1)S(1)}, u32[]{:S(2)}, u32[]{:S(2)}) collective-permute-start(bf16[128,1024]{1,0:T(8,128)(2,1)S(1)} %join.14.refs_2_), channel_id=1, source_target_pairs={{0,1},{1,0},{2,3},{3,2},{4,5},{5,4},{6,7},{7,6},{8,9},{9,8},{10,11... | collective-permute-start | bytes 786440 | tf_op jit(solution)/shard_map/ppermute | solution.py:207
  26.7 4.4 %collective-permute-start.12 = (bf16[128,1024]{1,0:T(8,128)(2,1)S(1)}, bf16[128,1024]{1,0:T(8,128)(2,1)S(1)}, u32[]{:S(2)}, u32[]{:S(2)}) collective-permute-start(bf16[128,1024]{1,0:T(8,128)(2,1)S(1)} %collective-permute-done.10.refs_3_), channel_id=1, source_target_pairs={{0,1},{1,0},{2,3},{3,2},{4,5},{5,4},{6,7},{7,6},{8,9},{9,8},{10,11... | collective-permute-start | bytes 786440 | tf_op jit(solution)/shard_map/ppermute | solution.py:207
  26.8 6.7 %collective-permute-start.15 = (bf16[128,1024]{1,0:T(8,128)(2,1)S(1)}, bf16[128,1024]{1,0:T(8,128)(2,1)S(1)}, u32[]{:S(2)}, u32[]{:S(2)}) collective-permute-start(bf16[128,1024]{1,0:T(8,128)(2,1)S(1)} %join.16.refs_2_), channel_id=1, source_target_pairs={{0,2},{1,5},{2,0},{3,7},{4,6},{5,1},{6,4},{7,3},{8,10},{9,13},{10,... | collective-permute-start | bytes 786440 | tf_op jit(solution)/shard_map/ppermute | solution.py:207
  28.1 6.0 %collective-permute-start.16 = (bf16[128,1024]{1,0:T(8,128)(2,1)S(1)}, bf16[128,1024]{1,0:T(8,128)(2,1)S(1)}, u32[]{:S(2)}, u32[]{:S(2)}) collective-permute-start(bf16[128,1024]{1,0:T(8,128)(2,1)S(1)} %join.16.refs_2_), channel_id=1, source_target_pairs={{0,1},{1,0},{2,3},{3,2},{4,5},{5,4},{6,7},{7,6},{8,9},{9,8},{10,11... | collective-permute-start | bytes 786440 | tf_op jit(solution)/shard_map/ppermute | solution.py:207
  33.5 1.7 %collective-permute-start.17 = (bf16[128,1024]{1,0:T(8,128)(2,1)S(1)}, bf16[128,1024]{1,0:T(8,128)(2,1)S(1)}, u32[]{:S(2)}, u32[]{:S(2)}) collective-permute-start(bf16[128,1024]{1,0:T(8,128)(2,1)S(1)} %join.17), channel_id=1, source_target_pairs={{0,1},{1,0},{2,3},{3,2},{4,5},{5,4},{6,7},{7,6},{8,9},{9,8},{10,11... | collective-permute-start | bytes 786440 | tf_op jit(solution)/shard_map/ppermute | solution.py:207

commit v5 on v3

--- a/solution.py
+++ b/solution.py
@@ -224,13 +224,13 @@
     early = (state[0],)
 
     mine1, second1 = hold(exchange(mine0, PLANE, PLANE)), exchange(second0, PLANE, PLANE)
-    mine3, second3 = double(group3)
+    mine3, second3 = double(group3, after=early)
     from1 = [mine1, second1, swap(mine1), swap(second1)]
     from3 = [mine3, second3, swap(mine3), swap(second3)]
-    state = fold(queries, state, list(zip(swapped0 + from1, [*of_own[2:], *[of_1] * 4])))
-    state = fold(queries, state, list(zip(from3, [of_3] * 4)))
-
-    mine2, second2 = double(group2, after=early)
+    pieces = list(zip(swapped0 + from1 + from3, [*of_own[2:], *[of_1] * 4, *[of_3] * 4]))
+    state = fold(queries, state, pieces)
+
+    mine2, second2 = double(group2)
     pieces = [mine2, second2, swap(mine2), swap(hold(second2, after=(state[0],)))]
     return fold(queries, state, [(piece, of_2) for piece in pieces], last=True)
 

time: 38 us -> 36.6 us (0.963)
  waiting for transfers between devices: 11.1 us -> 9.31 us
  local copies, waits for them, and re-layouts: 1.68 us -> 2.72 us
  Pallas kernels: 8.97 us -> 8.24 us
    ppermute x18, waiting for transfers between devices: 11.1 us -> 9.31 us  [exchange(): return lax.ppermute(block, AXES, pairs)]
    unnamed x6, local copies, waits for them, and re-layouts: 1.68 us -> 2.72 us
    pallas_call x4 -> x3, Pallas kernels: 8.81 us -> 8.07 us  [fold(): pl.pallas_call(functools.partial(fold_kernel, specs, bool(state), last),...]
  transfers between devices with their start and end apart: 18 -> 18, of which waited for: 6 -> 4; matrix products, arithmetic and copies ran while one was open for 0% -> 0% of each run, Pallas kernels for 17% -> 16%
where the time goes in v5:
time: 36.6 us; the launch traced here: 36 us
  starting transfers between devices  15.6 us (43%)
  waiting for transfers between devices  9.31 us (25%)
  Pallas kernels  8.24 us (23%)
  local copies, waits for them, and re-layouts  2.72 us (7%)
    ppermute x18, starting transfers between devices, exchange(): return lax.ppermute(block, AXES, pairs)  15.6 us
    ppermute x18, waiting for transfers between devices, exchange(): return lax.ppermute(block, AXES, pairs)  9.31 us
    pallas_call x3, Pallas kernels, fold(): pl.pallas_call(functools.partial(fold_kernel, specs, bool(state), last),...  8.07 us
    unnamed x6, local copies, waits for them, and re-layouts  2.72 us
  transfers between devices with their start and end apart: 18, of which 4 were waited for; matrix products, arithmetic and copies ran while one was open for 0% of the time, Pallas kernels for 16%

profile of v5, /device:TPU:25, one launch (start us, length us, event | category | flops | bytes accessed | tf_op | source)
XLA Modules:
  0.0 36.0 jit_solution(14896120430579476702)
XLA Ops:
  0.0 0.0 copy-start.1
  0.0 0.8 %copy-done.1 = bf16[64,512]{1,0:T(8,128)(2,1)S(1)} copy-done((bf16[64,512]{1,0:T(8,128)(2,1)S(1)}, bf16[64,512]{1,0:T(8,128)(2,1)}, u32[]{:S(2)}) %copy-start.1) | copy-done | bytes 65560
  0.8 0.0 copy-start.2
  0.8 0.8 %copy-done.2 = bf16[64,512]{1,0:T(8,128)(2,1)S(1)} copy-done((bf16[64,512]{1,0:T(8,128)(2,1)S(1)}, bf16[64,512]{1,0:T(8,128)(2,1)}, u32[]{:S(2)}) %copy-start.2) | copy-done | bytes 65560
  1.7 1.3 %collective-permute-start = (bf16[64,1024]{1,0:T(8,128)(2,1)S(1)}, bf16[64,1024]{1,0:T(8,128)(2,1)S(1)}, u32[]{:S(2)}, u32[]{:S(2)}) collective-permute-start(bf16[64,1024]{1,0:T(8,128)(2,1)S(1)} %pack.1.refs_0_), channel_id=1, source_target_pairs={{0,4},{1,3},{2,6},{3,1},{4,0},{5,7},{6,2},{7,5},{8,12},{9,11},{10,... | collective-permute-start | bytes 393224 | tf_op jit(solution)/shard_map/ppermute | solution.py:207
  3.0 0.0 collective-permute-start.8
  3.0 2.9 %collective-permute-done.refs_1_ = bf16[64,1024]{1,0:T(8,128)(2,1)S(1)} collective-permute-done((bf16[64,1024]{1,0:T(8,128)(2,1)S(1)}, bf16[64,1024]{1,0:T(8,128)(2,1)S(1)}, u32[]{:S(2)}, u32[]{:S(2)}) %collective-permute-start) | collective-permute-done | bytes 131104 | tf_op jit(solution)/shard_map/ppermute | solution.py:207
  5.9 1.3 %collective-permute-start.1 = (bf16[128,1024]{1,0:T(8,128)(2,1)S(1)}, bf16[128,1024]{1,0:T(8,128)(2,1)S(1)}, u32[]{:S(2)}, u32[]{:S(2)}) collective-permute-start(bf16[128,1024]{1,0:T(8,128)(2,1)S(1)} %join.9.refs_0_), channel_id=1, source_target_pairs={{0,2},{1,5},{2,0},{3,7},{4,6},{5,1},{6,4},{7,3},{8,10},{9,13},{10,... | collective-permute-start | bytes 786440 | tf_op jit(solution)/shard_map/ppermute | solution.py:207
  7.2 0.2 collective-permute-start.4
  7.4 1.6 %collective-permute-done.8.refs_0_ = bf16[64,1024]{1,0:T(8,128)(2,1)S(1)} collective-permute-done((bf16[64,1024]{1,0:T(8,128)(2,1)S(1)}, bf16[64,1024]{1,0:T(8,128)(2,1)S(1)}, u32[]{:S(2)}, u32[]{:S(2)}) %collective-permute-start.8) | collective-permute-done | bytes 131104 | tf_op jit(solution)/shard_map/ppermute | solution.py:207
  9.0 0.1 collective-permute-start.9
  9.1 0.9 %collective-permute-start.13 = (bf16[64,1024]{1,0:T(8,128)(2,1)S(1)}, bf16[64,1024]{1,0:T(8,128)(2,1)S(1)}, u32[]{:S(2)}, u32[]{:S(2)}) collective-permute-start(bf16[64,1024]{1,0:T(8,128)(2,1)S(1)} %join.13.refs_0_), channel_id=1, source_target_pairs={{0,8},{1,9},{2,10},{3,11},{4,12},{5,13},{6,14},{7,15},{8,0},{9,1},... | collective-permute-start | bytes 393224 | tf_op jit(solution)/shard_map/ppermute | solution.py:207
  10.0 3.8 %collective-permute-start.2 = (bf16[128,1024]{1,0:T(8,128)(2,1)S(1)}, bf16[128,1024]{1,0:T(8,128)(2,1)S(1)}, u32[]{:S(2)}, u32[]{:S(2)}) collective-permute-start(bf16[128,1024]{1,0:T(8,128)(2,1)S(1)} %join.9.refs_0_), channel_id=1, source_target_pairs={{0,1},{1,0},{2,3},{3,2},{4,5},{5,4},{6,7},{7,6},{8,9},{9,8},{10,11... | collective-permute-start | bytes 786440 | tf_op jit(solution)/shard_map/ppermute | solution.py:207
  13.8 0.0 collective-permute-done.1.refs_1_
  13.8 0.0 copy-start
  13.8 1.0 %copy-done = bf16[64,4096]{1,0:T(8,128)(2,1)S(1)} copy-done((bf16[64,4096]{1,0:T(8,128)(2,1)S(1)}, bf16[64,4096]{1,0:T(8,128)(2,1)}, u32[]{:S(2)}) %copy-start) | copy-done | bytes 524312
  14.9 0.9 %fold2n.1 = (f32[4,512,128]{2,1,0:T(8,128)S(1)}, f32[4,512,256]{2,1,0:T(8,128)S(1)}) custom-call(bf16[64,4096]{1,0:T(8,128)(2,1)S(1)} %copy-done, bf16[128,1024]{1,0:T(8,128)(2,1)S(1)} %join.9.refs_0_, bf16[128,1024]{1,0:T(8,128)(2,1)S(1)} %collective-permute-done.1.refs_1_), custom_call_target="tpu_custom_call" | custom-call | tf_op jit(solution)/shard_map/fold2n/pallas_call | solution.py:189
  15.8 0.0 collective-permute-done.9.refs_1_
  15.8 0.4 %collective-permute-start.10 = (bf16[128,1024]{1,0:T(8,128)(2,1)S(1)}, bf16[128,1024]{1,0:T(8,128)(2,1)S(1)}, u32[]{:S(2)}, u32[]{:S(2)}) collective-permute-start(bf16[128,1024]{1,0:T(8,128)(2,1)S(1)} %join.14.refs_8_), channel_id=1, source_target_pairs={{0,2},{1,5},{2,0},{3,7},{4,6},{5,1},{6,4},{7,3},{8,10},{9,13},{10,... | collective-permute-start | bytes 786440 | tf_op jit(solution)/shard_map/ppermute | solution.py:207
  16.2 1.0 %collective-permute-start.5 = (bf16[128,1024]{1,0:T(8,128)(2,1)S(1)}, bf16[128,1024]{1,0:T(8,128)(2,1)S(1)}, u32[]{:S(2)}, u32[]{:S(2)}) collective-permute-start(bf16[128,1024]{1,0:T(8,128)(2,1)S(1)} %collective-permute-done.1.refs_1_), channel_id=1, source_target_pairs={{0,8},{1,9},{2,10},{3,11},{4,12},{5,13},{6,14},{7,15},{8,0},{9,1},... | collective-permute-start | bytes 786440 | tf_op jit(solution)/shard_map/ppermute | solution.py:207
  17.2 0.0 collective-permute-done.13.refs_0_
  17.2 2.1 %collective-permute-start.11 = (bf16[128,1024]{1,0:T(8,128)(2,1)S(1)}, bf16[128,1024]{1,0:T(8,128)(2,1)S(1)}, u32[]{:S(2)}, u32[]{:S(2)}) collective-permute-start(bf16[128,1024]{1,0:T(8,128)(2,1)S(1)} %join.14.refs_8_), channel_id=1, source_target_pairs={{0,1},{1,0},{2,3},{3,2},{4,5},{5,4},{6,7},{7,6},{8,9},{9,8},{10,11... | collective-permute-start | bytes 786440 | tf_op jit(solution)/shard_map/ppermute | solution.py:207
  19.4 0.0 collective-permute-done.4.refs_0_
  19.4 1.6 %collective-permute-start.14 = (bf16[64,1024]{1,0:T(8,128)(2,1)S(1)}, bf16[64,1024]{1,0:T(8,128)(2,1)S(1)}, u32[]{:S(2)}, u32[]{:S(2)}) collective-permute-start(bf16[64,1024]{1,0:T(8,128)(2,1)S(1)} %join.15.refs_0_), channel_id=1, source_target_pairs={{0,4},{1,3},{2,6},{3,1},{4,0},{5,7},{6,2},{7,5},{8,12},{9,11},{10,... | collective-permute-start | bytes 393224 | tf_op jit(solution)/shard_map/ppermute | solution.py:207
  21.0 0.0 collective-permute-done.2.refs_2_
  21.0 0.1 collective-permute-start.6
  21.1 3.6 %collective-permute-done.14.refs_1_ = bf16[64,1024]{1,0:T(8,128)(2,1)S(1)} collective-permute-done((bf16[64,1024]{1,0:T(8,128)(2,1)S(1)}, bf16[64,1024]{1,0:T(8,128)(2,1)S(1)}, u32[]{:S(2)}, u32[]{:S(2)}) %collective-permute-start.14) | collective-permute-done | bytes 131104 | tf_op jit(solution)/shard_map/ppermute | solution.py:207
  24.7 0.0 collective-permute-start.3
  24.7 0.0 collective-permute-done.10.refs_9_
  24.7 0.5 %collective-permute-start.12 = (bf16[128,1024]{1,0:T(8,128)(2,1)S(1)}, bf16[128,1024]{1,0:T(8,128)(2,1)S(1)}, u32[]{:S(2)}, u32[]{:S(2)}) collective-permute-start(bf16[128,1024]{1,0:T(8,128)(2,1)S(1)} %collective-permute-done.10.refs_9_), channel_id=1, source_target_pairs={{0,1},{1,0},{2,3},{3,2},{4,5},{5,4},{6,7},{7,6},{8,9},{9,8},{10,11... | collective-permute-start | bytes 786440 | tf_op jit(solution)/shard_map/ppermute | solution.py:207
  25.2 0.0 collective-permute-done.5.refs_5_
  25.2 0.1 collective-permute-start.7
  25.3 0.0 collective-permute-done.11.refs_10_
  25.3 1.2 %collective-permute-start.15 = (bf16[128,1024]{1,0:T(8,128)(2,1)S(1)}, bf16[128,1024]{1,0:T(8,128)(2,1)S(1)}, u32[]{:S(2)}, u32[]{:S(2)}) collective-permute-start(bf16[128,1024]{1,0:T(8,128)(2,1)S(1)} %join.16.refs_2_), channel_id=1, source_target_pairs={{0,2},{1,5},{2,0},{3,7},{4,6},{5,1},{6,4},{7,3},{8,10},{9,13},{10,... | collective-permute-start | bytes 786440 | tf_op jit(solution)/shard_map/ppermute | solution.py:207
  26.5 0.0 collective-permute-done.3.refs_3_
  26.5 0.6 %collective-permute-start.16 = (bf16[128,1024]{1,0:T(8,128)(2,1)S(1)}, bf16[128,1024]{1,0:T(8,128)(2,1)S(1)}, u32[]{:S(2)}, u32[]{:S(2)}) collective-permute-start(bf16[128,1024]{1,0:T(8,128)(2,1)S(1)} %join.16.refs_2_), channel_id=1, source_target_pairs={{0,1},{1,0},{2,3},{3,2},{4,5},{5,4},{6,7},{7,6},{8,9},{9,8},{10,11... | collective-permute-start | bytes 786440 | tf_op jit(solution)/shard_map/ppermute | solution.py:207
  27.2 0.0 collective-permute-done.6.refs_6_
  27.2 0.0 collective-permute-done.12.refs_11_
  27.2 0.0 collective-permute-done.7.refs_7_
  27.2 4.6 %fold10s.1 = (f32[4,512,128]{2,1,0:T(8,128)S(1)}, f32[4,512,256]{2,1,0:T(8,128)S(1)}) custom-call(bf16[64,4096]{1,0:T(8,128)(2,1)S(1)} %copy-done, f32[4,512,128]{2,1,0:T(8,128)S(1)} %get-tuple-element.9.refs_2_.refs_0_, f32[4,512,256]{2,1,0:T(8,128)S(1)} %get-tuple-element.10.refs_1_, ...), custom_call_target="tpu_custom_call", output_to_operand_aliasing={{0}: (1, {}), {1}: (2, {})} | custom-call | tf_op jit(solution)/shard_map/fold10s/pallas_call | solution.py:189
  31.8 0.0 collective-permute-done.15.refs_0_.refs_3_
  31.8 0.5 %collective-permute-start.17 = (bf16[128,1024]{1,0:T(8,128)(2,1)S(1)}, bf16[128,1024]{1,0:T(8,128)(2,1)S(1)}, u32[]{:S(2)}, u32[]{:S(2)}) collective-permute-start(bf16[128,1024]{1,0:T(8,128)(2,1)S(1)} %join.17), channel_id=1, source_target_pairs={{0,1},{1,0},{2,3},{3,2},{4,5},{5,4},{6,7},{7,6},{8,9},{9,8},{10,11... | collective-permute-start | bytes 786440 | tf_op jit(solution)/shard_map/ppermute | solution.py:207
  32.3 0.0 collective-permute-done.16.refs_4_
  32.3 1.2 %collective-permute-done.17.refs_5_ = bf16[128,1024]{1,0:T(8,128)(2,1)S(1)} collective-permute-done((bf16[128,1024]{1,0:T(8,128)(2,1)S(1)}, bf16[128,1024]{1,0:T(8,128)(2,1)S(1)}, u32[]{:S(2)}, u32[]{:S(2)}) %collective-permute-start.17) | collective-permute-done | bytes 262176 | tf_op jit(solution)/shard_map/ppermute | solution.py:207
  33.5 2.6 %fold4sl.1 = bf16[64,4096]{1,0:T(8,128)(2,1)} custom-call(bf16[64,4096]{1,0:T(8,128)(2,1)S(1)} %copy-done, f32[4,512,128]{2,1,0:T(8,128)S(1)} %get-tuple-element.11.refs_1_.refs_0_, f32[4,512,256]{2,1,0:T(8,128)S(1)} %get-tuple-element.12.refs_1_, bf16[128,1024]{1,0:T(8,128)(2,1)S(1)} %join.16.refs_2_, ...), custom_call_target="tpu_custom_call" | custom-call | tf_op jit(solution)/shard_map/fold4sl/pallas_call | solution.py:189
  (10 shorter events, 0.2 us)
Async XLA Ops:
  0.0 0.8 %copy-start.1 = (bf16[64,512]{1,0:T(8,128)(2,1)S(1)}, bf16[64,512]{1,0:T(8,128)(2,1)}, u32[]{:S(2)}) copy-start(bf16[64,512]{1,0:T(8,128)(2,1)} %keys_ref.1) | copy-start | bytes 196612
  0.8 0.8 %copy-start.2 = (bf16[64,512]{1,0:T(8,128)(2,1)S(1)}, bf16[64,512]{1,0:T(8,128)(2,1)}, u32[]{:S(2)}) copy-start(bf16[64,512]{1,0:T(8,128)(2,1)} %values_ref.1) | copy-start | bytes 196612
  1.7 4.2 %collective-permute-start = (bf16[64,1024]{1,0:T(8,128)(2,1)S(1)}, bf16[64,1024]{1,0:T(8,128)(2,1)S(1)}, u32[]{:S(2)}, u32[]{:S(2)}) collective-permute-start(bf16[64,1024]{1,0:T(8,128)(2,1)S(1)} %pack.1.refs_0_), channel_id=1, source_target_pairs={{0,4},{1,3},{2,6},{3,1},{4,0},{5,7},{6,2},{7,5},{8,12},{9,11},{10,... | collective-permute-start | bytes 393224 | tf_op jit(solution)/shard_map/ppermute | solution.py:207
  3.0 6.0 %collective-permute-start.8 = (bf16[64,1024]{1,0:T(8,128)(2,1)S(1)}, bf16[64,1024]{1,0:T(8,128)(2,1)S(1)}, u32[]{:S(2)}, u32[]{:S(2)}) collective-permute-start(bf16[64,1024]{1,0:T(8,128)(2,1)S(1)} %pack.1.refs_0_), channel_id=1, source_target_pairs={{0,24},{1,25},{2,26},{3,27},{4,28},{5,29},{6,30},{7,31},{8,16},{9,... | collective-permute-start | bytes 393224 | tf_op jit(solution)/shard_map/ppermute | solution.py:207
  5.9 7.9 %collective-permute-start.1 = (bf16[128,1024]{1,0:T(8,128)(2,1)S(1)}, bf16[128,1024]{1,0:T(8,128)(2,1)S(1)}, u32[]{:S(2)}, u32[]{:S(2)}) collective-permute-start(bf16[128,1024]{1,0:T(8,128)(2,1)S(1)} %join.9.refs_0_), channel_id=1, source_target_pairs={{0,2},{1,5},{2,0},{3,7},{4,6},{5,1},{6,4},{7,3},{8,10},{9,13},{10,... | collective-permute-start | bytes 786440 | tf_op jit(solution)/shard_map/ppermute | solution.py:207
  7.2 12.2 %collective-permute-start.4 = (bf16[128,1024]{1,0:T(8,128)(2,1)S(1)}, bf16[128,1024]{1,0:T(8,128)(2,1)S(1)}, u32[]{:S(2)}, u32[]{:S(2)}) collective-permute-start(bf16[128,1024]{1,0:T(8,128)(2,1)S(1)} %join.9.refs_0_), channel_id=1, source_target_pairs={{0,8},{1,9},{2,10},{3,11},{4,12},{5,13},{6,14},{7,15},{8,0},{9,1},... | collective-permute-start | bytes 786440 | tf_op jit(solution)/shard_map/ppermute | solution.py:207
  9.0 6.7 %collective-permute-start.9 = (bf16[64,1024]{1,0:T(8,128)(2,1)S(1)}, bf16[64,1024]{1,0:T(8,128)(2,1)S(1)}, u32[]{:S(2)}, u32[]{:S(2)}) collective-permute-start(bf16[64,1024]{1,0:T(8,128)(2,1)S(1)} %join.13.refs_0_), channel_id=1, source_target_pairs={{0,4},{1,3},{2,6},{3,1},{4,0},{5,7},{6,2},{7,5},{8,12},{9,11},{10,... | collective-permute-start | bytes 393224 | tf_op jit(solution)/shard_map/ppermute | solution.py:207
  9.1 8.1 %collective-permute-start.13 = (bf16[64,1024]{1,0:T(8,128)(2,1)S(1)}, bf16[64,1024]{1,0:T(8,128)(2,1)S(1)}, u32[]{:S(2)}, u32[]{:S(2)}) collective-permute-start(bf16[64,1024]{1,0:T(8,128)(2,1)S(1)} %join.13.refs_0_), channel_id=1, source_target_pairs={{0,8},{1,9},{2,10},{3,11},{4,12},{5,13},{6,14},{7,15},{8,0},{9,1},... | collective-permute-start | bytes 393224 | tf_op jit(solution)/shard_map/ppermute | solution.py:207
  10.0 11.0 %collective-permute-start.2 = (bf16[128,1024]{1,0:T(8,128)(2,1)S(1)}, bf16[128,1024]{1,0:T(8,128)(2,1)S(1)}, u32[]{:S(2)}, u32[]{:S(2)}) collective-permute-start(bf16[128,1024]{1,0:T(8,128)(2,1)S(1)} %join.9.refs_0_), channel_id=1, source_target_pairs={{0,1},{1,0},{2,3},{3,2},{4,5},{5,4},{6,7},{7,6},{8,9},{9,8},{10,11... | collective-permute-start | bytes 786440 | tf_op jit(solution)/shard_map/ppermute | solution.py:207
  13.8 1.0 %copy-start = (bf16[64,4096]{1,0:T(8,128)(2,1)S(1)}, bf16[64,4096]{1,0:T(8,128)(2,1)}, u32[]{:S(2)}) copy-start(bf16[64,4096]{1,0:T(8,128)(2,1)} %q_ref.5) | copy-start | bytes 1572868
  15.8 8.9 %collective-permute-start.10 = (bf16[128,1024]{1,0:T(8,128)(2,1)S(1)}, bf16[128,1024]{1,0:T(8,128)(2,1)S(1)}, u32[]{:S(2)}, u32[]{:S(2)}) collective-permute-start(bf16[128,1024]{1,0:T(8,128)(2,1)S(1)} %join.14.refs_8_), channel_id=1, source_target_pairs={{0,2},{1,5},{2,0},{3,7},{4,6},{5,1},{6,4},{7,3},{8,10},{9,13},{10,... | collective-permute-start | bytes 786440 | tf_op jit(solution)/shard_map/ppermute | solution.py:207
  16.2 9.0 %collective-permute-start.5 = (bf16[128,1024]{1,0:T(8,128)(2,1)S(1)}, bf16[128,1024]{1,0:T(8,128)(2,1)S(1)}, u32[]{:S(2)}, u32[]{:S(2)}) collective-permute-start(bf16[128,1024]{1,0:T(8,128)(2,1)S(1)} %collective-permute-done.1.refs_1_), channel_id=1, source_target_pairs={{0,8},{1,9},{2,10},{3,11},{4,12},{5,13},{6,14},{7,15},{8,0},{9,1},... | collective-permute-start | bytes 786440 | tf_op jit(solution)/shard_map/ppermute | solution.py:207
  17.2 8.1 %collective-permute-start.11 = (bf16[128,1024]{1,0:T(8,128)(2,1)S(1)}, bf16[128,1024]{1,0:T(8,128)(2,1)S(1)}, u32[]{:S(2)}, u32[]{:S(2)}) collective-permute-start(bf16[128,1024]{1,0:T(8,128)(2,1)S(1)} %join.14.refs_8_), channel_id=1, source_target_pairs={{0,1},{1,0},{2,3},{3,2},{4,5},{5,4},{6,7},{7,6},{8,9},{9,8},{10,11... | collective-permute-start | bytes 786440 | tf_op jit(solution)/shard_map/ppermute | solution.py:207
  19.4 5.4 %collective-permute-start.14 = (bf16[64,1024]{1,0:T(8,128)(2,1)S(1)}, bf16[64,1024]{1,0:T(8,128)(2,1)S(1)}, u32[]{:S(2)}, u32[]{:S(2)}) collective-permute-start(bf16[64,1024]{1,0:T(8,128)(2,1)S(1)} %join.15.refs_0_), channel_id=1, source_target_pairs={{0,4},{1,3},{2,6},{3,1},{4,0},{5,7},{6,2},{7,5},{8,12},{9,11},{10,... | collective-permute-start | bytes 393224 | tf_op jit(solution)/shard_map/ppermute | solution.py:207
  21.0 6.1 %collective-permute-start.6 = (bf16[128,1024]{1,0:T(8,128)(2,1)S(1)}, bf16[128,1024]{1,0:T(8,128)(2,1)S(1)}, u32[]{:S(2)}, u32[]{:S(2)}) collective-permute-start(bf16[128,1024]{1,0:T(8,128)(2,1)S(1)} %join.10.refs_4_), channel_id=1, source_target_pairs={{0,1},{1,0},{2,3},{3,2},{4,5},{5,4},{6,7},{7,6},{8,9},{9,8},{10,11... | collective-permute-start | bytes 786440 | tf_op jit(solution)/shard_map/ppermute | solution.py:207
  24.7 1.8 %collective-permute-start.3 = (bf16[128,1024]{1,0:T(8,128)(2,1)S(1)}, bf16[128,1024]{1,0:T(8,128)(2,1)S(1)}, u32[]{:S(2)}, u32[]{:S(2)}) collective-permute-start(bf16[128,1024]{1,0:T(8,128)(2,1)S(1)} %collective-permute-done.1.refs_1_), channel_id=1, source_target_pairs={{0,1},{1,0},{2,3},{3,2},{4,5},{5,4},{6,7},{7,6},{8,9},{9,8},{10,11... | collective-permute-start | bytes 786440 | tf_op jit(solution)/shard_map/ppermute | solution.py:207
  24.7 2.4 %collective-permute-start.12 = (bf16[128,1024]{1,0:T(8,128)(2,1)S(1)}, bf16[128,1024]{1,0:T(8,128)(2,1)S(1)}, u32[]{:S(2)}, u32[]{:S(2)}) collective-permute-start(bf16[128,1024]{1,0:T(8,128)(2,1)S(1)} %collective-permute-done.10.refs_9_), channel_id=1, source_target_pairs={{0,1},{1,0},{2,3},{3,2},{4,5},{5,4},{6,7},{7,6},{8,9},{9,8},{10,11... | collective-permute-start | bytes 786440 | tf_op jit(solution)/shard_map/ppermute | solution.py:207
  25.2 1.9 %collective-permute-start.7 = (bf16[128,1024]{1,0:T(8,128)(2,1)S(1)}, bf16[128,1024]{1,0:T(8,128)(2,1)S(1)}, u32[]{:S(2)}, u32[]{:S(2)}) collective-permute-start(bf16[128,1024]{1,0:T(8,128)(2,1)S(1)} %collective-permute-done.5.refs_5_), channel_id=1, source_target_pairs={{0,1},{1,0},{2,3},{3,2},{4,5},{5,4},{6,7},{7,6},{8,9},{9,8},{10,11... | collective-permute-start | bytes 786440 | tf_op jit(solution)/shard_map/ppermute | solution.py:207
  25.3 6.4 %collective-permute-start.15 = (bf16[128,1024]{1,0:T(8,128)(2,1)S(1)}, bf16[128,1024]{1,0:T(8,128)(2,1)S(1)}, u32[]{:S(2)}, u32[]{:S(2)}) collective-permute-start(bf16[128,1024]{1,0:T(8,128)(2,1)S(1)} %join.16.refs_2_), channel_id=1, source_target_pairs={{0,2},{1,5},{2,0},{3,7},{4,6},{5,1},{6,4},{7,3},{8,10},{9,13},{10,... | collective-permute-start | bytes 786440 | tf_op jit(solution)/shard_map/ppermute | solution.py:207
  26.5 5.8 %collective-permute-start.16 = (bf16[128,1024]{1,0:T(8,128)(2,1)S(1)}, bf16[128,1024]{1,0:T(8,128)(2,1)S(1)}, u32[]{:S(2)}, u32[]{:S(2)}) collective-permute-start(bf16[128,1024]{1,0:T(8,128)(2,1)S(1)} %join.16.refs_2_), channel_id=1, source_target_pairs={{0,1},{1,0},{2,3},{3,2},{4,5},{5,4},{6,7},{7,6},{8,9},{9,8},{10,11... | collective-permute-start | bytes 786440 | tf_op jit(solution)/shard_map/ppermute | solution.py:207
  31.8 1.7 %collective-permute-start.17 = (bf16[128,1024]{1,0:T(8,128)(2,1)S(1)}, bf16[128,1024]{1,0:T(8,128)(2,1)S(1)}, u32[]{:S(2)}, u32[]{:S(2)}) collective-permute-start(bf16[128,1024]{1,0:T(8,128)(2,1)S(1)} %join.17), channel_id=1, source_target_pairs={{0,1},{1,0},{2,3},{3,2},{4,5},{5,4},{6,7},{7,6},{8,9},{9,8},{10,11... | collective-permute-start | bytes 786440 | tf_op jit(solution)/shard_map/ppermute | solution.py:207

commit v6 on v5

--- a/solution.py
+++ b/solution.py
@@ -43,6 +43,25 @@
         compiler_params=pltpu.CompilerParams(vmem_limit_bytes=2 * 2**20),
         name="pack",
     )(keys, values)
+
+
+def stage_kernel(queries_ref, own_ref, out_ref, sem):
+    copy = pltpu.make_async_copy(queries_ref, out_ref, sem)
+    copy.start()
+    copy.wait()
+
+
+def stage(queries, own):
+    return pl.pallas_call(
+        stage_kernel,
+        out_shape=jax.ShapeDtypeStruct(queries.shape, queries.dtype),
+        in_specs=[pl.BlockSpec(memory_space=pltpu.HBM), pl.BlockSpec(memory_space=pl.ANY)],
+        out_specs=VMEM,
+        scratch_shapes=[pltpu.SemaphoreType.DMA(())],
+        compiler_params=pltpu.CompilerParams(vmem_limit_bytes=2 * 2**20),
+        cost_estimate=FREE,
+        name="stage",
+    )(queries, own)
 
 
 def join_kernel(count, *refs):
@@ -201,6 +220,7 @@
 def planes_path(queries, keys, values, count):
     rows = queries.shape[0]
     own = pack(keys, values)
+    queries = stage(queries, own)
 
     def exchange(block, even_bits, odd_bits):
         pairs = [(i, i ^ (odd_bits if i % 2 else even_bits)) for i in range(count)]

time: 36.6 us -> 36.4 us (level)
  no operation moved by 1% of the time
where the time goes in v6:
time: 36.4 us; the launch traced here: 35.8 us
  starting transfers between devices  15.6 us (43%)
  waiting for transfers between devices  9.02 us (25%)
  Pallas kernels  8.28 us (23%)
  local copies, waits for them, and re-layouts  2.72 us (7%)
    ppermute x18, starting transfers between devices, exchange(): return lax.ppermute(block, AXES, pairs)  15.6 us
    ppermute x18, waiting for transfers between devices, exchange(): return lax.ppermute(block, AXES, pairs)  9.02 us
    pallas_call x3, Pallas kernels, fold(): pl.pallas_call(functools.partial(fold_kernel, specs, bool(state), last),...  8.07 us
    unnamed x6, local copies, waits for them, and re-layouts  2.72 us
  transfers between devices with their start and end apart: 18, of which 4 were waited for; matrix products, arithmetic and copies ran while one was open for 0% of the time, Pallas kernels for 16%

profile of v6, /device:TPU:25, one launch (start us, length us, event | category | flops | bytes accessed | tf_op | source)
XLA Modules:
  0.0 35.8 jit_solution(5705037391175255150)
XLA Ops:
  0.0 0.0 copy-start.1
  0.0 0.8 %copy-done.1 = bf16[64,512]{1,0:T(8,128)(2,1)S(1)} copy-done((bf16[64,512]{1,0:T(8,128)(2,1)S(1)}, bf16[64,512]{1,0:T(8,128)(2,1)}, u32[]{:S(2)}) %copy-start.1) | copy-done | bytes 65560
  0.8 0.0 copy-start.2
  0.8 0.8 %copy-done.2 = bf16[64,512]{1,0:T(8,128)(2,1)S(1)} copy-done((bf16[64,512]{1,0:T(8,128)(2,1)S(1)}, bf16[64,512]{1,0:T(8,128)(2,1)}, u32[]{:S(2)}) %copy-start.2) | copy-done | bytes 65560
  1.7 1.3 %collective-permute-start = (bf16[64,1024]{1,0:T(8,128)(2,1)S(1)}, bf16[64,1024]{1,0:T(8,128)(2,1)S(1)}, u32[]{:S(2)}, u32[]{:S(2)}) collective-permute-start(bf16[64,1024]{1,0:T(8,128)(2,1)S(1)} %pack.1.own_ref.refs_0_), channel_id=1, source_target_pairs={{0,4},{1,3},{2,6},{3,1},{4,0},{5,7},{6,2},{7,5},{8,12},{9,11},{10,... | collective-permute-start | bytes 393224 | tf_op jit(solution)/shard_map/ppermute | solution.py:227
  3.0 0.0 collective-permute-start.8
  3.0 2.9 %collective-permute-done.refs_1_ = bf16[64,1024]{1,0:T(8,128)(2,1)S(1)} collective-permute-done((bf16[64,1024]{1,0:T(8,128)(2,1)S(1)}, bf16[64,1024]{1,0:T(8,128)(2,1)S(1)}, u32[]{:S(2)}, u32[]{:S(2)}) %collective-permute-start) | collective-permute-done | bytes 131104 | tf_op jit(solution)/shard_map/ppermute | solution.py:227
  5.9 1.3 %collective-permute-start.1 = (bf16[128,1024]{1,0:T(8,128)(2,1)S(1)}, bf16[128,1024]{1,0:T(8,128)(2,1)S(1)}, u32[]{:S(2)}, u32[]{:S(2)}) collective-permute-start(bf16[128,1024]{1,0:T(8,128)(2,1)S(1)} %join.9.refs_0_), channel_id=1, source_target_pairs={{0,2},{1,5},{2,0},{3,7},{4,6},{5,1},{6,4},{7,3},{8,10},{9,13},{10,... | collective-permute-start | bytes 786440 | tf_op jit(solution)/shard_map/ppermute | solution.py:227
  7.2 0.2 collective-permute-start.4
  7.4 1.6 %collective-permute-done.8.refs_0_ = bf16[64,1024]{1,0:T(8,128)(2,1)S(1)} collective-permute-done((bf16[64,1024]{1,0:T(8,128)(2,1)S(1)}, bf16[64,1024]{1,0:T(8,128)(2,1)S(1)}, u32[]{:S(2)}, u32[]{:S(2)}) %collective-permute-start.8) | collective-permute-done | bytes 131104 | tf_op jit(solution)/shard_map/ppermute | solution.py:227
  9.0 0.1 collective-permute-start.9
  9.1 0.9 %collective-permute-start.13 = (bf16[64,1024]{1,0:T(8,128)(2,1)S(1)}, bf16[64,1024]{1,0:T(8,128)(2,1)S(1)}, u32[]{:S(2)}, u32[]{:S(2)}) collective-permute-start(bf16[64,1024]{1,0:T(8,128)(2,1)S(1)} %join.13.refs_0_), channel_id=1, source_target_pairs={{0,8},{1,9},{2,10},{3,11},{4,12},{5,13},{6,14},{7,15},{8,0},{9,1},... | collective-permute-start | bytes 393224 | tf_op jit(solution)/shard_map/ppermute | solution.py:227
  10.0 0.0 copy-start
  10.0 1.0 %copy-done = bf16[64,4096]{1,0:T(8,128)(2,1)S(1)} copy-done((bf16[64,4096]{1,0:T(8,128)(2,1)S(1)}, bf16[64,4096]{1,0:T(8,128)(2,1)}, u32[]{:S(2)}) %copy-start) | copy-done | bytes 524312
  11.1 3.8 %collective-permute-start.2 = (bf16[128,1024]{1,0:T(8,128)(2,1)S(1)}, bf16[128,1024]{1,0:T(8,128)(2,1)S(1)}, u32[]{:S(2)}, u32[]{:S(2)}) collective-permute-start(bf16[128,1024]{1,0:T(8,128)(2,1)S(1)} %join.9.refs_0_), channel_id=1, source_target_pairs={{0,1},{1,0},{2,3},{3,2},{4,5},{5,4},{6,7},{7,6},{8,9},{9,8},{10,11... | collective-permute-start | bytes 786440 | tf_op jit(solution)/shard_map/ppermute | solution.py:227
  15.0 0.0 collective-permute-done.1.refs_1_
  15.0 0.9 %fold2n.1 = (f32[4,512,128]{2,1,0:T(8,128)S(1)}, f32[4,512,256]{2,1,0:T(8,128)S(1)}) custom-call(bf16[64,4096]{1,0:T(8,128)(2,1)S(1)} %stage.1.q_ref, bf16[128,1024]{1,0:T(8,128)(2,1)S(1)} %join.9.refs_0_, bf16[128,1024]{1,0:T(8,128)(2,1)S(1)} %collective-permute-done.1.refs_1_), custom_call_target="tpu_custom_call" | custom-call | tf_op jit(solution)/shard_map/fold2n/pallas_call | solution.py:208
  15.9 0.0 collective-permute-done.9.refs_1_
  15.9 0.3 collective-permute-start.10
  16.2 1.1 %collective-permute-start.5 = (bf16[128,1024]{1,0:T(8,128)(2,1)S(1)}, bf16[128,1024]{1,0:T(8,128)(2,1)S(1)}, u32[]{:S(2)}, u32[]{:S(2)}) collective-permute-start(bf16[128,1024]{1,0:T(8,128)(2,1)S(1)} %collective-permute-done.1.refs_1_), channel_id=1, source_target_pairs={{0,8},{1,9},{2,10},{3,11},{4,12},{5,13},{6,14},{7,15},{8,0},{9,1},... | collective-permute-start | bytes 786440 | tf_op jit(solution)/shard_map/ppermute | solution.py:227
  17.3 0.0 collective-permute-done.13.refs_0_
  17.3 2.0 %collective-permute-start.11 = (bf16[128,1024]{1,0:T(8,128)(2,1)S(1)}, bf16[128,1024]{1,0:T(8,128)(2,1)S(1)}, u32[]{:S(2)}, u32[]{:S(2)}) collective-permute-start(bf16[128,1024]{1,0:T(8,128)(2,1)S(1)} %join.14.refs_8_), channel_id=1, source_target_pairs={{0,1},{1,0},{2,3},{3,2},{4,5},{5,4},{6,7},{7,6},{8,9},{9,8},{10,11... | collective-permute-start | bytes 786440 | tf_op jit(solution)/shard_map/ppermute | solution.py:227
  19.4 0.0 collective-permute-done.4.refs_0_
  19.4 1.6 %collective-permute-start.14 = (bf16[64,1024]{1,0:T(8,128)(2,1)S(1)}, bf16[64,1024]{1,0:T(8,128)(2,1)S(1)}, u32[]{:S(2)}, u32[]{:S(2)}) collective-permute-start(bf16[64,1024]{1,0:T(8,128)(2,1)S(1)} %join.15.refs_0_), channel_id=1, source_target_pairs={{0,4},{1,3},{2,6},{3,1},{4,0},{5,7},{6,2},{7,5},{8,12},{9,11},{10,... | collective-permute-start | bytes 393224 | tf_op jit(solution)/shard_map/ppermute | solution.py:227
  21.0 0.0 collective-permute-done.2.refs_2_
  21.0 0.1 collective-permute-start.6
  21.1 3.0 %collective-permute-done.14.refs_1_ = bf16[64,1024]{1,0:T(8,128)(2,1)S(1)} collective-permute-done((bf16[64,1024]{1,0:T(8,128)(2,1)S(1)}, bf16[64,1024]{1,0:T(8,128)(2,1)S(1)}, u32[]{:S(2)}, u32[]{:S(2)}) %collective-permute-start.14) | collective-permute-done | bytes 131104 | tf_op jit(solution)/shard_map/ppermute | solution.py:227
  24.1 0.3 collective-permute-start.3
  24.4 0.0 collective-permute-done.10.refs_9_
  24.4 0.2 collective-permute-start.12
  24.6 0.0 collective-permute-done.5.refs_5_
  24.6 0.4 %collective-permute-start.7 = (bf16[128,1024]{1,0:T(8,128)(2,1)S(1)}, bf16[128,1024]{1,0:T(8,128)(2,1)S(1)}, u32[]{:S(2)}, u32[]{:S(2)}) collective-permute-start(bf16[128,1024]{1,0:T(8,128)(2,1)S(1)} %collective-permute-done.5.refs_5_), channel_id=1, source_target_pairs={{0,1},{1,0},{2,3},{3,2},{4,5},{5,4},{6,7},{7,6},{8,9},{9,8},{10,11... | collective-permute-start | bytes 786440 | tf_op jit(solution)/shard_map/ppermute | solution.py:227
  25.0 0.0 collective-permute-done.11.refs_10_
  25.0 1.3 %collective-permute-start.15 = (bf16[128,1024]{1,0:T(8,128)(2,1)S(1)}, bf16[128,1024]{1,0:T(8,128)(2,1)S(1)}, u32[]{:S(2)}, u32[]{:S(2)}) collective-permute-start(bf16[128,1024]{1,0:T(8,128)(2,1)S(1)} %join.16.refs_2_), channel_id=1, source_target_pairs={{0,2},{1,5},{2,0},{3,7},{4,6},{5,1},{6,4},{7,3},{8,10},{9,13},{10,... | collective-permute-start | bytes 786440 | tf_op jit(solution)/shard_map/ppermute | solution.py:227
  26.3 0.0 collective-permute-done.3.refs_3_
  26.3 0.7 %collective-permute-start.16 = (bf16[128,1024]{1,0:T(8,128)(2,1)S(1)}, bf16[128,1024]{1,0:T(8,128)(2,1)S(1)}, u32[]{:S(2)}, u32[]{:S(2)}) collective-permute-start(bf16[128,1024]{1,0:T(8,128)(2,1)S(1)} %join.16.refs_2_), channel_id=1, source_target_pairs={{0,1},{1,0},{2,3},{3,2},{4,5},{5,4},{6,7},{7,6},{8,9},{9,8},{10,11... | collective-permute-start | bytes 786440 | tf_op jit(solution)/shard_map/ppermute | solution.py:227
  26.9 0.0 collective-permute-done.6.refs_6_
  26.9 0.0 collective-permute-done.12.refs_11_
  26.9 0.0 collective-permute-done.7.refs_7_
  27.0 4.6 %fold10s.1 = (f32[4,512,128]{2,1,0:T(8,128)S(1)}, f32[4,512,256]{2,1,0:T(8,128)S(1)}) custom-call(bf16[64,4096]{1,0:T(8,128)(2,1)S(1)} %stage.1.q_ref, f32[4,512,128]{2,1,0:T(8,128)S(1)} %get-tuple-element.9.refs_2_.refs_0_, f32[4,512,256]{2,1,0:T(8,128)S(1)} %get-tuple-element.10.refs_1_, ...), custom_call_target="tpu_custom_call", output_to_operand_aliasing={{0}: (1, {}), {1}: (2, {})} | custom-call | tf_op jit(solution)/shard_map/fold10s/pallas_call | solution.py:208
  31.6 0.0 collective-permute-done.15.refs_0_.refs_3_
  31.6 0.1 collective-permute-start.17
  31.7 0.0 collective-permute-done.16.refs_4_
  31.7 1.5 %collective-permute-done.17.refs_5_ = bf16[128,1024]{1,0:T(8,128)(2,1)S(1)} collective-permute-done((bf16[128,1024]{1,0:T(8,128)(2,1)S(1)}, bf16[128,1024]{1,0:T(8,128)(2,1)S(1)}, u32[]{:S(2)}, u32[]{:S(2)}) %collective-permute-start.17) | collective-permute-done | bytes 262176 | tf_op jit(solution)/shard_map/ppermute | solution.py:227
  33.2 2.6 %fold4sl.1 = bf16[64,4096]{1,0:T(8,128)(2,1)} custom-call(bf16[64,4096]{1,0:T(8,128)(2,1)S(1)} %stage.1.q_ref, f32[4,512,128]{2,1,0:T(8,128)S(1)} %get-tuple-element.11.refs_1_.refs_0_, f32[4,512,256]{2,1,0:T(8,128)S(1)} %get-tuple-element.12.refs_1_, bf16[128,1024]{1,0:T(8,128)(2,1)S(1)} %join.16.refs_2_, ...), custom_call_target="tpu_custom_call" | custom-call | tf_op jit(solution)/shard_map/fold4sl/pallas_call | solution.py:208
  (11 shorter events, 0.2 us)
Async XLA Ops:
  0.0 0.8 %copy-start.1 = (bf16[64,512]{1,0:T(8,128)(2,1)S(1)}, bf16[64,512]{1,0:T(8,128)(2,1)}, u32[]{:S(2)}) copy-start(bf16[64,512]{1,0:T(8,128)(2,1)} %keys_ref.1) | copy-start | bytes 196612
  0.8 0.8 %copy-start.2 = (bf16[64,512]{1,0:T(8,128)(2,1)S(1)}, bf16[64,512]{1,0:T(8,128)(2,1)}, u32[]{:S(2)}) copy-start(bf16[64,512]{1,0:T(8,128)(2,1)} %values_ref.1) | copy-start | bytes 196612
  1.7 4.2 %collective-permute-start = (bf16[64,1024]{1,0:T(8,128)(2,1)S(1)}, bf16[64,1024]{1,0:T(8,128)(2,1)S(1)}, u32[]{:S(2)}, u32[]{:S(2)}) collective-permute-start(bf16[64,1024]{1,0:T(8,128)(2,1)S(1)} %pack.1.own_ref.refs_0_), channel_id=1, source_target_pairs={{0,4},{1,3},{2,6},{3,1},{4,0},{5,7},{6,2},{7,5},{8,12},{9,11},{10,... | collective-permute-start | bytes 393224 | tf_op jit(solution)/shard_map/ppermute | solution.py:227
  3.0 6.0 %collective-permute-start.8 = (bf16[64,1024]{1,0:T(8,128)(2,1)S(1)}, bf16[64,1024]{1,0:T(8,128)(2,1)S(1)}, u32[]{:S(2)}, u32[]{:S(2)}) collective-permute-start(bf16[64,1024]{1,0:T(8,128)(2,1)S(1)} %pack.1.own_ref.refs_0_), channel_id=1, source_target_pairs={{0,24},{1,25},{2,26},{3,27},{4,28},{5,29},{6,30},{7,31},{8,16},{9,... | collective-permute-start | bytes 393224 | tf_op jit(solution)/shard_map/ppermute | solution.py:227
  5.9 9.0 %collective-permute-start.1 = (bf16[128,1024]{1,0:T(8,128)(2,1)S(1)}, bf16[128,1024]{1,0:T(8,128)(2,1)S(1)}, u32[]{:S(2)}, u32[]{:S(2)}) collective-permute-start(bf16[128,1024]{1,0:T(8,128)(2,1)S(1)} %join.9.refs_0_), channel_id=1, source_target_pairs={{0,2},{1,5},{2,0},{3,7},{4,6},{5,1},{6,4},{7,3},{8,10},{9,13},{10,... | collective-permute-start | bytes 786440 | tf_op jit(solution)/shard_map/ppermute | solution.py:227
  7.2 12.2 %collective-permute-start.4 = (bf16[128,1024]{1,0:T(8,128)(2,1)S(1)}, bf16[128,1024]{1,0:T(8,128)(2,1)S(1)}, u32[]{:S(2)}, u32[]{:S(2)}) collective-permute-start(bf16[128,1024]{1,0:T(8,128)(2,1)S(1)} %join.9.refs_0_), channel_id=1, source_target_pairs={{0,8},{1,9},{2,10},{3,11},{4,12},{5,13},{6,14},{7,15},{8,0},{9,1},... | collective-permute-start | bytes 786440 | tf_op jit(solution)/shard_map/ppermute | solution.py:227
  9.0 6.8 %collective-permute-start.9 = (bf16[64,1024]{1,0:T(8,128)(2,1)S(1)}, bf16[64,1024]{1,0:T(8,128)(2,1)S(1)}, u32[]{:S(2)}, u32[]{:S(2)}) collective-permute-start(bf16[64,1024]{1,0:T(8,128)(2,1)S(1)} %join.13.refs_0_), channel_id=1, source_target_pairs={{0,4},{1,3},{2,6},{3,1},{4,0},{5,7},{6,2},{7,5},{8,12},{9,11},{10,... | collective-permute-start | bytes 393224 | tf_op jit(solution)/shard_map/ppermute | solution.py:227
  9.1 8.2 %collective-permute-start.13 = (bf16[64,1024]{1,0:T(8,128)(2,1)S(1)}, bf16[64,1024]{1,0:T(8,128)(2,1)S(1)}, u32[]{:S(2)}, u32[]{:S(2)}) collective-permute-start(bf16[64,1024]{1,0:T(8,128)(2,1)S(1)} %join.13.refs_0_), channel_id=1, source_target_pairs={{0,8},{1,9},{2,10},{3,11},{4,12},{5,13},{6,14},{7,15},{8,0},{9,1},... | collective-permute-start | bytes 393224 | tf_op jit(solution)/shard_map/ppermute | solution.py:227
  10.0 1.0 %copy-start = (bf16[64,4096]{1,0:T(8,128)(2,1)S(1)}, bf16[64,4096]{1,0:T(8,128)(2,1)}, u32[]{:S(2)}) copy-start(bf16[64,4096]{1,0:T(8,128)(2,1)} %queries_ref.1) | copy-start | bytes 1572868
  11.1 9.9 %collective-permute-start.2 = (bf16[128,1024]{1,0:T(8,128)(2,1)S(1)}, bf16[128,1024]{1,0:T(8,128)(2,1)S(1)}, u32[]{:S(2)}, u32[]{:S(2)}) collective-permute-start(bf16[128,1024]{1,0:T(8,128)(2,1)S(1)} %join.9.refs_0_), channel_id=1, source_target_pairs={{0,1},{1,0},{2,3},{3,2},{4,5},{5,4},{6,7},{7,6},{8,9},{9,8},{10,11... | collective-permute-start | bytes 786440 | tf_op jit(solution)/shard_map/ppermute | solution.py:227
  15.9 8.5 %collective-permute-start.10 = (bf16[128,1024]{1,0:T(8,128)(2,1)S(1)}, bf16[128,1024]{1,0:T(8,128)(2,1)S(1)}, u32[]{:S(2)}, u32[]{:S(2)}) collective-permute-start(bf16[128,1024]{1,0:T(8,128)(2,1)S(1)} %join.14.refs_8_), channel_id=1, source_target_pairs={{0,2},{1,5},{2,0},{3,7},{4,6},{5,1},{6,4},{7,3},{8,10},{9,13},{10,... | collective-permute-start | bytes 786440 | tf_op jit(solution)/shard_map/ppermute | solution.py:227
  16.2 8.4 %collective-permute-start.5 = (bf16[128,1024]{1,0:T(8,128)(2,1)S(1)}, bf16[128,1024]{1,0:T(8,128)(2,1)S(1)}, u32[]{:S(2)}, u32[]{:S(2)}) collective-permute-start(bf16[128,1024]{1,0:T(8,128)(2,1)S(1)} %collective-permute-done.1.refs_1_), channel_id=1, source_target_pairs={{0,8},{1,9},{2,10},{3,11},{4,12},{5,13},{6,14},{7,15},{8,0},{9,1},... | collective-permute-start | bytes 786440 | tf_op jit(solution)/shard_map/ppermute | solution.py:227
  17.3 7.7 %collective-permute-start.11 = (bf16[128,1024]{1,0:T(8,128)(2,1)S(1)}, bf16[128,1024]{1,0:T(8,128)(2,1)S(1)}, u32[]{:S(2)}, u32[]{:S(2)}) collective-permute-start(bf16[128,1024]{1,0:T(8,128)(2,1)S(1)} %join.14.refs_8_), channel_id=1, source_target_pairs={{0,1},{1,0},{2,3},{3,2},{4,5},{5,4},{6,7},{7,6},{8,9},{9,8},{10,11... | collective-permute-start | bytes 786440 | tf_op jit(solution)/shard_map/ppermute | solution.py:227
  19.4 4.7 %collective-permute-start.14 = (bf16[64,1024]{1,0:T(8,128)(2,1)S(1)}, bf16[64,1024]{1,0:T(8,128)(2,1)S(1)}, u32[]{:S(2)}, u32[]{:S(2)}) collective-permute-start(bf16[64,1024]{1,0:T(8,128)(2,1)S(1)} %join.15.refs_0_), channel_id=1, source_target_pairs={{0,4},{1,3},{2,6},{3,1},{4,0},{5,7},{6,2},{7,5},{8,12},{9,11},{10,... | collective-permute-start | bytes 393224 | tf_op jit(solution)/shard_map/ppermute | solution.py:227
  21.0 5.9 %collective-permute-start.6 = (bf16[128,1024]{1,0:T(8,128)(2,1)S(1)}, bf16[128,1024]{1,0:T(8,128)(2,1)S(1)}, u32[]{:S(2)}, u32[]{:S(2)}) collective-permute-start(bf16[128,1024]{1,0:T(8,128)(2,1)S(1)} %join.10.refs_4_), channel_id=1, source_target_pairs={{0,1},{1,0},{2,3},{3,2},{4,5},{5,4},{6,7},{7,6},{8,9},{9,8},{10,11... | collective-permute-start | bytes 786440 | tf_op jit(solution)/shard_map/ppermute | solution.py:227
  24.1 2.2 %collective-permute-start.3 = (bf16[128,1024]{1,0:T(8,128)(2,1)S(1)}, bf16[128,1024]{1,0:T(8,128)(2,1)S(1)}, u32[]{:S(2)}, u32[]{:S(2)}) collective-permute-start(bf16[128,1024]{1,0:T(8,128)(2,1)S(1)} %collective-permute-done.1.refs_1_), channel_id=1, source_target_pairs={{0,1},{1,0},{2,3},{3,2},{4,5},{5,4},{6,7},{7,6},{8,9},{9,8},{10,11... | collective-permute-start | bytes 786440 | tf_op jit(solution)/shard_map/ppermute | solution.py:227
  24.4 2.5 %collective-permute-start.12 = (bf16[128,1024]{1,0:T(8,128)(2,1)S(1)}, bf16[128,1024]{1,0:T(8,128)(2,1)S(1)}, u32[]{:S(2)}, u32[]{:S(2)}) collective-permute-start(bf16[128,1024]{1,0:T(8,128)(2,1)S(1)} %collective-permute-done.10.refs_9_), channel_id=1, source_target_pairs={{0,1},{1,0},{2,3},{3,2},{4,5},{5,4},{6,7},{7,6},{8,9},{9,8},{10,11... | collective-permute-start | bytes 786440 | tf_op jit(solution)/shard_map/ppermute | solution.py:227
  24.6 2.3 %collective-permute-start.7 = (bf16[128,1024]{1,0:T(8,128)(2,1)S(1)}, bf16[128,1024]{1,0:T(8,128)(2,1)S(1)}, u32[]{:S(2)}, u32[]{:S(2)}) collective-permute-start(bf16[128,1024]{1,0:T(8,128)(2,1)S(1)} %collective-permute-done.5.refs_5_), channel_id=1, source_target_pairs={{0,1},{1,0},{2,3},{3,2},{4,5},{5,4},{6,7},{7,6},{8,9},{9,8},{10,11... | collective-permute-start | bytes 786440 | tf_op jit(solution)/shard_map/ppermute | solution.py:227
  25.0 6.6 %collective-permute-start.15 = (bf16[128,1024]{1,0:T(8,128)(2,1)S(1)}, bf16[128,1024]{1,0:T(8,128)(2,1)S(1)}, u32[]{:S(2)}, u32[]{:S(2)}) collective-permute-start(bf16[128,1024]{1,0:T(8,128)(2,1)S(1)} %join.16.refs_2_), channel_id=1, source_target_pairs={{0,2},{1,5},{2,0},{3,7},{4,6},{5,1},{6,4},{7,3},{8,10},{9,13},{10,... | collective-permute-start | bytes 786440 | tf_op jit(solution)/shard_map/ppermute | solution.py:227
  26.3 5.4 %collective-permute-start.16 = (bf16[128,1024]{1,0:T(8,128)(2,1)S(1)}, bf16[128,1024]{1,0:T(8,128)(2,1)S(1)}, u32[]{:S(2)}, u32[]{:S(2)}) collective-permute-start(bf16[128,1024]{1,0:T(8,128)(2,1)S(1)} %join.16.refs_2_), channel_id=1, source_target_pairs={{0,1},{1,0},{2,3},{3,2},{4,5},{5,4},{6,7},{7,6},{8,9},{9,8},{10,11... | collective-permute-start | bytes 786440 | tf_op jit(solution)/shard_map/ppermute | solution.py:227
  31.6 1.6 %collective-permute-start.17 = (bf16[128,1024]{1,0:T(8,128)(2,1)S(1)}, bf16[128,1024]{1,0:T(8,128)(2,1)S(1)}, u32[]{:S(2)}, u32[]{:S(2)}) collective-permute-start(bf16[128,1024]{1,0:T(8,128)(2,1)S(1)} %join.17), channel_id=1, source_target_pairs={{0,1},{1,0},{2,3},{3,2},{4,5},{5,4},{6,7},{7,6},{8,9},{9,8},{10,11... | collective-permute-start | bytes 786440 | tf_op jit(solution)/shard_map/ppermute | solution.py:227

commit v7 on v6

--- a/solution.py
+++ b/solution.py
@@ -170,14 +170,32 @@
     steps = {spec for spec in specs if spec[0] == "step"}
     single = len(steps) == 1 and steps == set(specs) and has_state
 
-    def work():
+    def work(some=None, state_from=state_refs, used=None):
+        some = range(len(specs)) if some is None else some
+        some_blocks, some_specs = [blocks[i] for i in some], [specs[i] for i in some]
+        used = ({} if single else marks) if used is None else used
         for h in range(KVH):
-            state = tuple(ref[h] for ref in state_refs) or None
-            peak, summed = fold_head(h, q_ref, blocks, specs, {} if single else marks, state)
+            state = tuple(ref[h] for ref in state_from) or None
+            peak, summed = fold_head(h, q_ref, some_blocks, some_specs, used, state)
             if last:
                 finish_head(h, summed, outs[0])
             else:
                 outs[0][h], outs[1][h] = peak, summed
+
+    if len(steps) > 1 and has_state and not last:
+        own_marks = {spec: mark for spec, mark in marks.items() if spec not in steps}
+        valid = {spec: marks[spec] == 0.0 for spec in sorted(steps)}
+        every = functools.reduce(jnp.logical_and, valid.values())
+        pl.when(every)(lambda: work(used=own_marks))
+
+        @pl.when(jnp.logical_not(every))
+        def _():
+            work([i for i, spec in enumerate(specs) if spec not in steps], used=own_marks)
+            for step, earlier in valid.items():
+                some = [i for i, spec in enumerate(specs) if spec == step]
+                pl.when(earlier)(functools.partial(work, some, outs, own_marks))
+
+        return
 
     if not single:
         work()

time: 36.4 us -> 36.4 us (level)
  no operation moved by 1% of the time
where the time goes in v7:
time: 36.4 us; the launch traced here: 35.9 us
  starting transfers between devices  15.6 us (43%)
  waiting for transfers between devices  9.02 us (25%)
  Pallas kernels  8.39 us (23%)
  local copies, waits for them, and re-layouts  2.72 us (7%)
    ppermute x18, starting transfers between devices, exchange(): return lax.ppermute(block, AXES, pairs)  15.6 us
    ppermute x18, waiting for transfers between devices, exchange(): return lax.ppermute(block, AXES, pairs)  9.02 us
    pallas_call x3, Pallas kernels, fold(): pl.pallas_call(functools.partial(fold_kernel, specs, bool(state), last),...  8.18 us
    unnamed x6, local copies, waits for them, and re-layouts  2.72 us
  transfers between devices with their start and end apart: 18, of which 4 were waited for; matrix products, arithmetic and copies ran while one was open for 0% of the time, Pallas kernels for 16%

profile of v7, /device:TPU:25, one launch (start us, length us, event | category | flops | bytes accessed | tf_op | source)
XLA Modules:
  0.0 35.9 jit_solution(8671394102063295165)
XLA Ops:
  0.0 0.0 copy-start.1
  0.0 0.8 %copy-done.1 = bf16[64,512]{1,0:T(8,128)(2,1)S(1)} copy-done((bf16[64,512]{1,0:T(8,128)(2,1)S(1)}, bf16[64,512]{1,0:T(8,128)(2,1)}, u32[]{:S(2)}) %copy-start.1) | copy-done | bytes 65560
  0.8 0.0 copy-start.2
  0.8 0.8 %copy-done.2 = bf16[64,512]{1,0:T(8,128)(2,1)S(1)} copy-done((bf16[64,512]{1,0:T(8,128)(2,1)S(1)}, bf16[64,512]{1,0:T(8,128)(2,1)}, u32[]{:S(2)}) %copy-start.2) | copy-done | bytes 65560
  1.7 1.3 %collective-permute-start = (bf16[64,1024]{1,0:T(8,128)(2,1)S(1)}, bf16[64,1024]{1,0:T(8,128)(2,1)S(1)}, u32[]{:S(2)}, u32[]{:S(2)}) collective-permute-start(bf16[64,1024]{1,0:T(8,128)(2,1)S(1)} %pack.1.own_ref.refs_0_), channel_id=1, source_target_pairs={{0,4},{1,3},{2,6},{3,1},{4,0},{5,7},{6,2},{7,5},{8,12},{9,11},{10,... | collective-permute-start | bytes 393224 | tf_op jit(solution)/shard_map/ppermute | solution.py:245
  3.0 0.0 collective-permute-start.8
  3.0 2.9 %collective-permute-done.refs_1_ = bf16[64,1024]{1,0:T(8,128)(2,1)S(1)} collective-permute-done((bf16[64,1024]{1,0:T(8,128)(2,1)S(1)}, bf16[64,1024]{1,0:T(8,128)(2,1)S(1)}, u32[]{:S(2)}, u32[]{:S(2)}) %collective-permute-start) | collective-permute-done | bytes 131104 | tf_op jit(solution)/shard_map/ppermute | solution.py:245
  5.9 1.3 %collective-permute-start.1 = (bf16[128,1024]{1,0:T(8,128)(2,1)S(1)}, bf16[128,1024]{1,0:T(8,128)(2,1)S(1)}, u32[]{:S(2)}, u32[]{:S(2)}) collective-permute-start(bf16[128,1024]{1,0:T(8,128)(2,1)S(1)} %join.9.refs_0_), channel_id=1, source_target_pairs={{0,2},{1,5},{2,0},{3,7},{4,6},{5,1},{6,4},{7,3},{8,10},{9,13},{10,... | collective-permute-start | bytes 786440 | tf_op jit(solution)/shard_map/ppermute | solution.py:245
  7.2 0.2 collective-permute-start.4
  7.4 1.6 %collective-permute-done.8.refs_0_ = bf16[64,1024]{1,0:T(8,128)(2,1)S(1)} collective-permute-done((bf16[64,1024]{1,0:T(8,128)(2,1)S(1)}, bf16[64,1024]{1,0:T(8,128)(2,1)S(1)}, u32[]{:S(2)}, u32[]{:S(2)}) %collective-permute-start.8) | collective-permute-done | bytes 131104 | tf_op jit(solution)/shard_map/ppermute | solution.py:245
  9.0 0.1 collective-permute-start.9
  9.1 0.9 %collective-permute-start.13 = (bf16[64,1024]{1,0:T(8,128)(2,1)S(1)}, bf16[64,1024]{1,0:T(8,128)(2,1)S(1)}, u32[]{:S(2)}, u32[]{:S(2)}) collective-permute-start(bf16[64,1024]{1,0:T(8,128)(2,1)S(1)} %join.13.refs_0_), channel_id=1, source_target_pairs={{0,8},{1,9},{2,10},{3,11},{4,12},{5,13},{6,14},{7,15},{8,0},{9,1},... | collective-permute-start | bytes 393224 | tf_op jit(solution)/shard_map/ppermute | solution.py:245
  10.0 0.0 copy-start
  10.0 1.0 %copy-done = bf16[64,4096]{1,0:T(8,128)(2,1)S(1)} copy-done((bf16[64,4096]{1,0:T(8,128)(2,1)S(1)}, bf16[64,4096]{1,0:T(8,128)(2,1)}, u32[]{:S(2)}) %copy-start) | copy-done | bytes 524312
  11.1 3.8 %collective-permute-start.2 = (bf16[128,1024]{1,0:T(8,128)(2,1)S(1)}, bf16[128,1024]{1,0:T(8,128)(2,1)S(1)}, u32[]{:S(2)}, u32[]{:S(2)}) collective-permute-start(bf16[128,1024]{1,0:T(8,128)(2,1)S(1)} %join.9.refs_0_), channel_id=1, source_target_pairs={{0,1},{1,0},{2,3},{3,2},{4,5},{5,4},{6,7},{7,6},{8,9},{9,8},{10,11... | collective-permute-start | bytes 786440 | tf_op jit(solution)/shard_map/ppermute | solution.py:245
  15.0 0.0 collective-permute-done.1.refs_1_
  15.0 0.9 %fold2n.1 = (f32[4,512,128]{2,1,0:T(8,128)S(1)}, f32[4,512,256]{2,1,0:T(8,128)S(1)}) custom-call(bf16[64,4096]{1,0:T(8,128)(2,1)S(1)} %stage.1.q_ref, bf16[128,1024]{1,0:T(8,128)(2,1)S(1)} %join.9.refs_0_, bf16[128,1024]{1,0:T(8,128)(2,1)S(1)} %collective-permute-done.1.refs_1_), custom_call_target="tpu_custom_call" | custom-call | tf_op jit(solution)/shard_map/fold2n/pallas_call | solution.py:226
  15.9 0.0 collective-permute-done.9.refs_1_
  15.9 0.3 collective-permute-start.10
  16.2 1.1 %collective-permute-start.5 = (bf16[128,1024]{1,0:T(8,128)(2,1)S(1)}, bf16[128,1024]{1,0:T(8,128)(2,1)S(1)}, u32[]{:S(2)}, u32[]{:S(2)}) collective-permute-start(bf16[128,1024]{1,0:T(8,128)(2,1)S(1)} %collective-permute-done.1.refs_1_), channel_id=1, source_target_pairs={{0,8},{1,9},{2,10},{3,11},{4,12},{5,13},{6,14},{7,15},{8,0},{9,1},... | collective-permute-start | bytes 786440 | tf_op jit(solution)/shard_map/ppermute | solution.py:245
  17.3 0.0 collective-permute-done.13.refs_0_
  17.3 2.0 %collective-permute-start.11 = (bf16[128,1024]{1,0:T(8,128)(2,1)S(1)}, bf16[128,1024]{1,0:T(8,128)(2,1)S(1)}, u32[]{:S(2)}, u32[]{:S(2)}) collective-permute-start(bf16[128,1024]{1,0:T(8,128)(2,1)S(1)} %join.14.refs_8_), channel_id=1, source_target_pairs={{0,1},{1,0},{2,3},{3,2},{4,5},{5,4},{6,7},{7,6},{8,9},{9,8},{10,11... | collective-permute-start | bytes 786440 | tf_op jit(solution)/shard_map/ppermute | solution.py:245
  19.4 0.0 collective-permute-done.4.refs_0_
  19.4 1.6 %collective-permute-start.14 = (bf16[64,1024]{1,0:T(8,128)(2,1)S(1)}, bf16[64,1024]{1,0:T(8,128)(2,1)S(1)}, u32[]{:S(2)}, u32[]{:S(2)}) collective-permute-start(bf16[64,1024]{1,0:T(8,128)(2,1)S(1)} %join.15.refs_0_), channel_id=1, source_target_pairs={{0,4},{1,3},{2,6},{3,1},{4,0},{5,7},{6,2},{7,5},{8,12},{9,11},{10,... | collective-permute-start | bytes 393224 | tf_op jit(solution)/shard_map/ppermute | solution.py:245
  21.0 0.0 collective-permute-done.2.refs_2_
  21.0 0.1 collective-permute-start.6
  21.1 3.0 %collective-permute-done.14.refs_1_ = bf16[64,1024]{1,0:T(8,128)(2,1)S(1)} collective-permute-done((bf16[64,1024]{1,0:T(8,128)(2,1)S(1)}, bf16[64,1024]{1,0:T(8,128)(2,1)S(1)}, u32[]{:S(2)}, u32[]{:S(2)}) %collective-permute-start.14) | collective-permute-done | bytes 131104 | tf_op jit(solution)/shard_map/ppermute | solution.py:245
  24.1 0.3 collective-permute-start.3
  24.4 0.0 collective-permute-done.10.refs_9_
  24.4 0.2 collective-permute-start.12
  24.6 0.0 collective-permute-done.5.refs_5_
  24.6 0.4 %collective-permute-start.7 = (bf16[128,1024]{1,0:T(8,128)(2,1)S(1)}, bf16[128,1024]{1,0:T(8,128)(2,1)S(1)}, u32[]{:S(2)}, u32[]{:S(2)}) collective-permute-start(bf16[128,1024]{1,0:T(8,128)(2,1)S(1)} %collective-permute-done.5.refs_5_), channel_id=1, source_target_pairs={{0,1},{1,0},{2,3},{3,2},{4,5},{5,4},{6,7},{7,6},{8,9},{9,8},{10,11... | collective-permute-start | bytes 786440 | tf_op jit(solution)/shard_map/ppermute | solution.py:245
  25.0 0.0 collective-permute-done.11.refs_10_
  25.0 1.3 %collective-permute-start.15 = (bf16[128,1024]{1,0:T(8,128)(2,1)S(1)}, bf16[128,1024]{1,0:T(8,128)(2,1)S(1)}, u32[]{:S(2)}, u32[]{:S(2)}) collective-permute-start(bf16[128,1024]{1,0:T(8,128)(2,1)S(1)} %join.16.refs_2_), channel_id=1, source_target_pairs={{0,2},{1,5},{2,0},{3,7},{4,6},{5,1},{6,4},{7,3},{8,10},{9,13},{10,... | collective-permute-start | bytes 786440 | tf_op jit(solution)/shard_map/ppermute | solution.py:245
  26.3 0.0 collective-permute-done.3.refs_3_
  26.3 0.7 %collective-permute-start.16 = (bf16[128,1024]{1,0:T(8,128)(2,1)S(1)}, bf16[128,1024]{1,0:T(8,128)(2,1)S(1)}, u32[]{:S(2)}, u32[]{:S(2)}) collective-permute-start(bf16[128,1024]{1,0:T(8,128)(2,1)S(1)} %join.16.refs_2_), channel_id=1, source_target_pairs={{0,1},{1,0},{2,3},{3,2},{4,5},{5,4},{6,7},{7,6},{8,9},{9,8},{10,11... | collective-permute-start | bytes 786440 | tf_op jit(solution)/shard_map/ppermute | solution.py:245
  26.9 0.0 collective-permute-done.6.refs_6_
  26.9 0.0 collective-permute-done.12.refs_11_
  26.9 0.0 collective-permute-done.7.refs_7_
  27.0 4.7 %fold10s.1 = (f32[4,512,128]{2,1,0:T(8,128)S(1)}, f32[4,512,256]{2,1,0:T(8,128)S(1)}) custom-call(bf16[64,4096]{1,0:T(8,128)(2,1)S(1)} %stage.1.q_ref, f32[4,512,128]{2,1,0:T(8,128)S(1)} %get-tuple-element.9.refs_2_.refs_0_, f32[4,512,256]{2,1,0:T(8,128)S(1)} %get-tuple-element.10.refs_1_, ...), custom_call_target="tpu_custom_call", output_to_operand_aliasing={{0}: (1, {}), {1}: (2, {})} | custom-call | tf_op jit(solution)/shard_map/fold10s/pallas_call | solution.py:226
  31.7 0.0 collective-permute-done.15.refs_0_.refs_3_
  31.7 0.1 collective-permute-start.17
  31.8 0.0 collective-permute-done.16.refs_4_
  31.8 1.5 %collective-permute-done.17.refs_5_ = bf16[128,1024]{1,0:T(8,128)(2,1)S(1)} collective-permute-done((bf16[128,1024]{1,0:T(8,128)(2,1)S(1)}, bf16[128,1024]{1,0:T(8,128)(2,1)S(1)}, u32[]{:S(2)}, u32[]{:S(2)}) %collective-permute-start.17) | collective-permute-done | bytes 262176 | tf_op jit(solution)/shard_map/ppermute | solution.py:245
  33.3 2.6 %fold4sl.1 = bf16[64,4096]{1,0:T(8,128)(2,1)} custom-call(bf16[64,4096]{1,0:T(8,128)(2,1)S(1)} %stage.1.q_ref, f32[4,512,128]{2,1,0:T(8,128)S(1)} %get-tuple-element.11.refs_1_.refs_0_, f32[4,512,256]{2,1,0:T(8,128)S(1)} %get-tuple-element.12.refs_1_, bf16[128,1024]{1,0:T(8,128)(2,1)S(1)} %join.16.refs_2_, ...), custom_call_target="tpu_custom_call" | custom-call | tf_op jit(solution)/shard_map/fold4sl/pallas_call | solution.py:226
  (11 shorter events, 0.2 us)
Async XLA Ops:
  0.0 0.8 %copy-start.1 = (bf16[64,512]{1,0:T(8,128)(2,1)S(1)}, bf16[64,512]{1,0:T(8,128)(2,1)}, u32[]{:S(2)}) copy-start(bf16[64,512]{1,0:T(8,128)(2,1)} %keys_ref.1) | copy-start | bytes 196612
  0.8 0.8 %copy-start.2 = (bf16[64,512]{1,0:T(8,128)(2,1)S(1)}, bf16[64,512]{1,0:T(8,128)(2,1)}, u32[]{:S(2)}) copy-start(bf16[64,512]{1,0:T(8,128)(2,1)} %values_ref.1) | copy-start | bytes 196612
  1.7 4.2 %collective-permute-start = (bf16[64,1024]{1,0:T(8,128)(2,1)S(1)}, bf16[64,1024]{1,0:T(8,128)(2,1)S(1)}, u32[]{:S(2)}, u32[]{:S(2)}) collective-permute-start(bf16[64,1024]{1,0:T(8,128)(2,1)S(1)} %pack.1.own_ref.refs_0_), channel_id=1, source_target_pairs={{0,4},{1,3},{2,6},{3,1},{4,0},{5,7},{6,2},{7,5},{8,12},{9,11},{10,... | collective-permute-start | bytes 393224 | tf_op jit(solution)/shard_map/ppermute | solution.py:245
  3.0 6.0 %collective-permute-start.8 = (bf16[64,1024]{1,0:T(8,128)(2,1)S(1)}, bf16[64,1024]{1,0:T(8,128)(2,1)S(1)}, u32[]{:S(2)}, u32[]{:S(2)}) collective-permute-start(bf16[64,1024]{1,0:T(8,128)(2,1)S(1)} %pack.1.own_ref.refs_0_), channel_id=1, source_target_pairs={{0,24},{1,25},{2,26},{3,27},{4,28},{5,29},{6,30},{7,31},{8,16},{9,... | collective-permute-start | bytes 393224 | tf_op jit(solution)/shard_map/ppermute | solution.py:245
  5.9 9.0 %collective-permute-start.1 = (bf16[128,1024]{1,0:T(8,128)(2,1)S(1)}, bf16[128,1024]{1,0:T(8,128)(2,1)S(1)}, u32[]{:S(2)}, u32[]{:S(2)}) collective-permute-start(bf16[128,1024]{1,0:T(8,128)(2,1)S(1)} %join.9.refs_0_), channel_id=1, source_target_pairs={{0,2},{1,5},{2,0},{3,7},{4,6},{5,1},{6,4},{7,3},{8,10},{9,13},{10,... | collective-permute-start | bytes 786440 | tf_op jit(solution)/shard_map/ppermute | solution.py:245
  7.2 12.2 %collective-permute-start.4 = (bf16[128,1024]{1,0:T(8,128)(2,1)S(1)}, bf16[128,1024]{1,0:T(8,128)(2,1)S(1)}, u32[]{:S(2)}, u32[]{:S(2)}) collective-permute-start(bf16[128,1024]{1,0:T(8,128)(2,1)S(1)} %join.9.refs_0_), channel_id=1, source_target_pairs={{0,8},{1,9},{2,10},{3,11},{4,12},{5,13},{6,14},{7,15},{8,0},{9,1},... | collective-permute-start | bytes 786440 | tf_op jit(solution)/shard_map/ppermute | solution.py:245
  9.0 6.8 %collective-permute-start.9 = (bf16[64,1024]{1,0:T(8,128)(2,1)S(1)}, bf16[64,1024]{1,0:T(8,128)(2,1)S(1)}, u32[]{:S(2)}, u32[]{:S(2)}) collective-permute-start(bf16[64,1024]{1,0:T(8,128)(2,1)S(1)} %join.13.refs_0_), channel_id=1, source_target_pairs={{0,4},{1,3},{2,6},{3,1},{4,0},{5,7},{6,2},{7,5},{8,12},{9,11},{10,... | collective-permute-start | bytes 393224 | tf_op jit(solution)/shard_map/ppermute | solution.py:245
  9.1 8.2 %collective-permute-start.13 = (bf16[64,1024]{1,0:T(8,128)(2,1)S(1)}, bf16[64,1024]{1,0:T(8,128)(2,1)S(1)}, u32[]{:S(2)}, u32[]{:S(2)}) collective-permute-start(bf16[64,1024]{1,0:T(8,128)(2,1)S(1)} %join.13.refs_0_), channel_id=1, source_target_pairs={{0,8},{1,9},{2,10},{3,11},{4,12},{5,13},{6,14},{7,15},{8,0},{9,1},... | collective-permute-start | bytes 393224 | tf_op jit(solution)/shard_map/ppermute | solution.py:245
  10.0 1.0 %copy-start = (bf16[64,4096]{1,0:T(8,128)(2,1)S(1)}, bf16[64,4096]{1,0:T(8,128)(2,1)}, u32[]{:S(2)}) copy-start(bf16[64,4096]{1,0:T(8,128)(2,1)} %queries_ref.1) | copy-start | bytes 1572868
  11.1 9.9 %collective-permute-start.2 = (bf16[128,1024]{1,0:T(8,128)(2,1)S(1)}, bf16[128,1024]{1,0:T(8,128)(2,1)S(1)}, u32[]{:S(2)}, u32[]{:S(2)}) collective-permute-start(bf16[128,1024]{1,0:T(8,128)(2,1)S(1)} %join.9.refs_0_), channel_id=1, source_target_pairs={{0,1},{1,0},{2,3},{3,2},{4,5},{5,4},{6,7},{7,6},{8,9},{9,8},{10,11... | collective-permute-start | bytes 786440 | tf_op jit(solution)/shard_map/ppermute | solution.py:245
  15.9 8.5 %collective-permute-start.10 = (bf16[128,1024]{1,0:T(8,128)(2,1)S(1)}, bf16[128,1024]{1,0:T(8,128)(2,1)S(1)}, u32[]{:S(2)}, u32[]{:S(2)}) collective-permute-start(bf16[128,1024]{1,0:T(8,128)(2,1)S(1)} %join.14.refs_8_), channel_id=1, source_target_pairs={{0,2},{1,5},{2,0},{3,7},{4,6},{5,1},{6,4},{7,3},{8,10},{9,13},{10,... | collective-permute-start | bytes 786440 | tf_op jit(solution)/shard_map/ppermute | solution.py:245
  16.2 8.4 %collective-permute-start.5 = (bf16[128,1024]{1,0:T(8,128)(2,1)S(1)}, bf16[128,1024]{1,0:T(8,128)(2,1)S(1)}, u32[]{:S(2)}, u32[]{:S(2)}) collective-permute-start(bf16[128,1024]{1,0:T(8,128)(2,1)S(1)} %collective-permute-done.1.refs_1_), channel_id=1, source_target_pairs={{0,8},{1,9},{2,10},{3,11},{4,12},{5,13},{6,14},{7,15},{8,0},{9,1},... | collective-permute-start | bytes 786440 | tf_op jit(solution)/shard_map/ppermute | solution.py:245
  17.3 7.7 %collective-permute-start.11 = (bf16[128,1024]{1,0:T(8,128)(2,1)S(1)}, bf16[128,1024]{1,0:T(8,128)(2,1)S(1)}, u32[]{:S(2)}, u32[]{:S(2)}) collective-permute-start(bf16[128,1024]{1,0:T(8,128)(2,1)S(1)} %join.14.refs_8_), channel_id=1, source_target_pairs={{0,1},{1,0},{2,3},{3,2},{4,5},{5,4},{6,7},{7,6},{8,9},{9,8},{10,11... | collective-permute-start | bytes 786440 | tf_op jit(solution)/shard_map/ppermute | solution.py:245
  19.4 4.7 %collective-permute-start.14 = (bf16[64,1024]{1,0:T(8,128)(2,1)S(1)}, bf16[64,1024]{1,0:T(8,128)(2,1)S(1)}, u32[]{:S(2)}, u32[]{:S(2)}) collective-permute-start(bf16[64,1024]{1,0:T(8,128)(2,1)S(1)} %join.15.refs_0_), channel_id=1, source_target_pairs={{0,4},{1,3},{2,6},{3,1},{4,0},{5,7},{6,2},{7,5},{8,12},{9,11},{10,... | collective-permute-start | bytes 393224 | tf_op jit(solution)/shard_map/ppermute | solution.py:245
  21.0 5.9 %collective-permute-start.6 = (bf16[128,1024]{1,0:T(8,128)(2,1)S(1)}, bf16[128,1024]{1,0:T(8,128)(2,1)S(1)}, u32[]{:S(2)}, u32[]{:S(2)}) collective-permute-start(bf16[128,1024]{1,0:T(8,128)(2,1)S(1)} %join.10.refs_4_), channel_id=1, source_target_pairs={{0,1},{1,0},{2,3},{3,2},{4,5},{5,4},{6,7},{7,6},{8,9},{9,8},{10,11... | collective-permute-start | bytes 786440 | tf_op jit(solution)/shard_map/ppermute | solution.py:245
  24.1 2.2 %collective-permute-start.3 = (bf16[128,1024]{1,0:T(8,128)(2,1)S(1)}, bf16[128,1024]{1,0:T(8,128)(2,1)S(1)}, u32[]{:S(2)}, u32[]{:S(2)}) collective-permute-start(bf16[128,1024]{1,0:T(8,128)(2,1)S(1)} %collective-permute-done.1.refs_1_), channel_id=1, source_target_pairs={{0,1},{1,0},{2,3},{3,2},{4,5},{5,4},{6,7},{7,6},{8,9},{9,8},{10,11... | collective-permute-start | bytes 786440 | tf_op jit(solution)/shard_map/ppermute | solution.py:245
  24.4 2.5 %collective-permute-start.12 = (bf16[128,1024]{1,0:T(8,128)(2,1)S(1)}, bf16[128,1024]{1,0:T(8,128)(2,1)S(1)}, u32[]{:S(2)}, u32[]{:S(2)}) collective-permute-start(bf16[128,1024]{1,0:T(8,128)(2,1)S(1)} %collective-permute-done.10.refs_9_), channel_id=1, source_target_pairs={{0,1},{1,0},{2,3},{3,2},{4,5},{5,4},{6,7},{7,6},{8,9},{9,8},{10,11... | collective-permute-start | bytes 786440 | tf_op jit(solution)/shard_map/ppermute | solution.py:245
  24.6 2.3 %collective-permute-start.7 = (bf16[128,1024]{1,0:T(8,128)(2,1)S(1)}, bf16[128,1024]{1,0:T(8,128)(2,1)S(1)}, u32[]{:S(2)}, u32[]{:S(2)}) collective-permute-start(bf16[128,1024]{1,0:T(8,128)(2,1)S(1)} %collective-permute-done.5.refs_5_), channel_id=1, source_target_pairs={{0,1},{1,0},{2,3},{3,2},{4,5},{5,4},{6,7},{7,6},{8,9},{9,8},{10,11... | collective-permute-start | bytes 786440 | tf_op jit(solution)/shard_map/ppermute | solution.py:245
  25.0 6.7 %collective-permute-start.15 = (bf16[128,1024]{1,0:T(8,128)(2,1)S(1)}, bf16[128,1024]{1,0:T(8,128)(2,1)S(1)}, u32[]{:S(2)}, u32[]{:S(2)}) collective-permute-start(bf16[128,1024]{1,0:T(8,128)(2,1)S(1)} %join.16.refs_2_), channel_id=1, source_target_pairs={{0,2},{1,5},{2,0},{3,7},{4,6},{5,1},{6,4},{7,3},{8,10},{9,13},{10,... | collective-permute-start | bytes 786440 | tf_op jit(solution)/shard_map/ppermute | solution.py:245
  26.3 5.5 %collective-permute-start.16 = (bf16[128,1024]{1,0:T(8,128)(2,1)S(1)}, bf16[128,1024]{1,0:T(8,128)(2,1)S(1)}, u32[]{:S(2)}, u32[]{:S(2)}) collective-permute-start(bf16[128,1024]{1,0:T(8,128)(2,1)S(1)} %join.16.refs_2_), channel_id=1, source_target_pairs={{0,1},{1,0},{2,3},{3,2},{4,5},{5,4},{6,7},{7,6},{8,9},{9,8},{10,11... | collective-permute-start | bytes 786440 | tf_op jit(solution)/shard_map/ppermute | solution.py:245
  31.7 1.6 %collective-permute-start.17 = (bf16[128,1024]{1,0:T(8,128)(2,1)S(1)}, bf16[128,1024]{1,0:T(8,128)(2,1)S(1)}, u32[]{:S(2)}, u32[]{:S(2)}) collective-permute-start(bf16[128,1024]{1,0:T(8,128)(2,1)S(1)} %join.17), channel_id=1, source_target_pairs={{0,1},{1,0},{2,3},{3,2},{4,5},{5,4},{6,7},{7,6},{8,9},{9,8},{10,11... | collective-permute-start | bytes 786440 | tf_op jit(solution)/shard_map/ppermute | solution.py:245
